TPU v7x, 1024 devices: a whole 8x8x8 slice. The times are simulated.
1024 devices in a mesh: expert: 64 (over x, y), tensor: 16 (over z, core).
Axes of the slice: x: 8, y: 8, z: 8, core: 2. Of those that a mesh axis runs over, the one named last changes fastest.
Arguments:
- tokens: bfloat16 [1024, 2048], P('expert', 'tensor'), may hold values from -6 to 6
- expert_ids: int32 [1024, 8], P('expert'), may hold values from 0 to 127, all different within a row; in each aligned block of 16 rows (0 to 15, 16 to 31, ...) at most 3 rows name the same one
- gate_scores: float32 [1024, 8], P('expert'), may hold values from 0.05 to 1
- w_in: bfloat16 [128, 2, 768, 2048], P('expert', None, 'tensor'), may hold values from -0.125 to 0.125
- w_down: bfloat16 [128, 768, 2048], P('expert', 'tensor'), may hold values from -0.3125 to 0.3125
Outputs:
- mixed: bfloat16 [1024, 2048], P('expert', 'tensor')
Inputs may be any that keep to these rules, and one draw needn't show every extreme that they name: `expert_ids`: each row names 8 different experts; in every aligned block of 16 rows no expert is named by more than 3 rows, a bound that some block reaches.
All inputs are finite; a program needn't handle non-finite values.
Results may differ from a plain program's by a relative error of at most 0.024.
Values may be sent and summed in bfloat16 or wider, within the bound.
No kernel may reach another device: no remote copies, remote signals or barrier semaphores. Data moves between devices by JAX's collectives and lax.ppermute only.
A program may use at most 32 MiB of HBM per device.

v0:
```python
import jax
import jax.numpy as jnp
from jax import lax
from jax.sharding import PartitionSpec as P


def route_tables(expert_ids, gate_scores, experts, capacity):
    tok_count, top_count = expert_ids.shape
    flattened = expert_ids.reshape(tok_count * top_count)
    onehot = (flattened[:, None] == jnp.arange(experts, dtype=jnp.int32)[None, :]).astype(jnp.int32)
    before = jnp.cumsum(onehot, axis=0) - onehot
    slot_index = jnp.sum(before * onehot, axis=1)
    column = flattened * capacity + slot_index
    placing = (column[:, None] == jnp.arange(experts * capacity, dtype=jnp.int32)[None, :]).astype(
        jnp.float32
    )
    placing = placing.reshape(tok_count, top_count, experts * capacity)
    weights = gate_scores / jnp.sum(gate_scores, axis=1, keepdims=True)
    dispatch = jnp.sum(placing, axis=1)
    combine = jnp.sum(placing * weights[:, :, None], axis=1)
    return (dispatch, combine)


def shards(tokens, expert_ids, gate_scores, w_in, w_down):
    n_expert = lax.axis_size("expert")
    exp_dev = w_in.shape[0]
    experts = n_expert * exp_dev
    tok_count, top_count = expert_ids.shape
    capacity = min(tok_count, 3 * tok_count * top_count // experts)
    feat_slice = tokens.shape[1]
    full_width = w_in.shape[3]
    dispatch, combine = route_tables(expert_ids, gate_scores, experts, capacity)
    routing = dispatch.astype(jnp.bfloat16)
    buffer = jnp.einsum(
        "tj,td->jd",
        routing,
        lax.all_gather(tokens, "tensor", axis=1, tiled=True),
        preferred_element_type=jnp.float32,
    ).astype(jnp.bfloat16)
    buffer = buffer.reshape(n_expert, exp_dev * capacity, full_width)
    arrived = lax.all_to_all(buffer, "expert", split_axis=0, concat_axis=0, tiled=True)
    arrived = arrived.reshape(n_expert, exp_dev, capacity, full_width)
    preact = jnp.einsum("secd,egfd->secgf", arrived, w_in, preferred_element_type=jnp.float32)
    hidden = (jax.nn.silu(preact[:, :, :, 0, :]) * preact[:, :, :, 1, :]).astype(jnp.bfloat16)
    partial_value = jnp.einsum("secf,efd->dsec", hidden, w_down, preferred_element_type=jnp.float32)
    scattered = lax.psum_scatter(
        partial_value.astype(jnp.bfloat16).astype(jnp.float32).astype(jnp.bfloat16),
        "tensor",
        scatter_dimension=0,
        tiled=True,
    )
    returned = lax.all_to_all(scattered, "expert", split_axis=1, concat_axis=1, tiled=True)
    flattened = returned.reshape(feat_slice, experts * capacity)
    mixed = jnp.einsum(
        "tj,dj->td", combine, flattened.astype(jnp.float32), precision=lax.Precision.HIGHEST
    )
    return mixed.astype(jnp.bfloat16)


def solution(mesh):
    in_specs = (
        P("expert", "tensor"),
        P("expert", None),
        P("expert", None),
        P("expert", None, "tensor", None),
        P("expert", "tensor", None),
    )
    out_specs = P("expert", "tensor")
    return jax.shard_map(shards, mesh=mesh, in_specs=in_specs, out_specs=out_specs, check_vma=False)
```

profile of v0, /device:TPU:16, one launch (start us, length us, event | category | flops | bytes accessed | tf_op | source)
XLA Modules:
  0.0 221.8 jit_solution(1239098674731353078)
XLA Ops:
  6.5 0.0 copy-start
  6.5 0.0 reduce-scatter.4.cloned.1.call-start
  6.5 0.8 reduce_sum.40
  7.3 0.7 broadcast_divide_fusion
  8.0 0.1 copy.32
  8.1 0.8 copy.30
  8.8 0.1 eq.29
  8.9 0.1 fusion.7
  9.0 0.2 reduce_window_sum.11
  9.2 0.2 select_reduce_fusion.1
  9.4 0.1 reduce_sum.39
  9.5 29.9 %all_gather.3 = bf16[16,2048]{1,0:T(8,128)(2,1)S(1)} all-gather(bf16[16,128]{1,0:T(8,128)(2,1)} %param.5), channel_id=1, replica_groups=mesh['expert'=64,'tensor'=16] {'tensor'}, dimensions={1}, use_global_device_ids=true | all-gather | bytes 69632 | tf_op jit(solution)/shard_map/all_gather | solution.py:37
  39.4 0.2 convert_reduce_fusion
  39.6 1.7 convolution_convert_fusion
  41.4 2.5 %reshape.30 = bf16[64,6,2048]{2,1,0:T(8,128)(2,1)S(1)} reshape(bf16[384,2048]{1,0:T(8,128)(2,1)} %convolution_convert_fusion) | data formatting | bytes 3145728 | tf_op jit(solution)/shard_map/reshape | solution.py:40
  43.9 65.7 %all_to_all.10 = bf16[64,6,2048]{2,1,0:T(8,128)(2,1)S(1)} all-to-all(bf16[64,6,2048]{2,1,0:T(8,128)(2,1)S(1)} %reshape.30), channel_id=1, replica_groups=mesh['expert'=64,'tensor'=16] {'expert'}, dimensions={0} | all-to-all | bytes 3145728 | tf_op jit(solution)/shard_map/all_to_all | solution.py:41
  109.6 0.9 copy.33
  110.4 0.0 copy-start.1
  110.4 0.0 copy-done
  110.5 0.8 convolution_bitcast_fusion
  111.3 0.2 copy-done.1
  111.4 0.6 fusion
  112.1 4.9 %copy.40 = bf16[2048,64,2,3]{1,3,2,0:T(4,128)(2,1)} copy(bf16[2048,64,2,3]{0,1,3,2:T(8,128)(2,1)S(1)} %fusion) | data formatting | bytes 3145728
  116.9 8.3 %reshape.36 = bf16[2048,384]{1,0:T(8,128)(2,1)} reshape(bf16[2048,2,3,64]{3,2,1,0:T(4,128)(2,1)} %bitcast.43) | data formatting | bytes 3145728
  125.2 0.0 reduce-scatter.4.cloned.1.call-update
  125.2 63.7 %reduce-scatter.4.cloned.1.call-done = bf16[128,384]{1,0:T(8,128)(2,1)} async-done(((bf16[2048,384]{1,0:T(8,128)(2,1)}), bf16[128,384]{1,0:T(8,128)(2,1)}) %reduce-scatter.4.cloned.1.call-update) | async-done | bytes 98320
  188.9 1.1 reshape.37
  190.0 0.2 copy.35
  190.2 23.8 %all_to_all.11 = bf16[128,64,2,3]{0,2,3,1:T(2,128)(2,1)S(1)} all-to-all(bf16[128,64,2,3]{0,2,3,1:T(2,128)(2,1)S(1)} %copy.35), channel_id=1, replica_groups=mesh['expert'=64,'tensor'=16] {'expert'}, dimensions={1} | all-to-all | bytes 196608 | tf_op jit(solution)/shard_map/all_to_all | solution.py:52
  214.1 0.1 reshape.32
  214.2 0.8 convolution_convert_fusion.2
  (2 shorter events, 0.1 us)
Async XLA Ops:
  6.5 103.9 %copy-start = (bf16[2,2,48,2048]{3,2,1,0:T(8,128)(2,1)S(1)}, bf16[2,2,48,2048]{3,2,1,0:T(8,128)(2,1)}, u32[]{:S(2)}) copy-start(bf16[2,2,48,2048]{3,2,1,0:T(8,128)(2,1)} %param.8) | copy-start | bytes 2359300
  6.5 182.4 %reduce-scatter.4.cloned.1.call-start = ((), (), s32[]{:S(2)}) async-start(), calls=%async_computation.3 | async-start | bytes 1671168
  110.4 1.0 copy-start.1
Sparse Core Ops, SparseCore 0:
  125.4 63.5 reduce-scatter.3
where the time goes:
time: 223 us; the launch traced here: 222 us
  blocking collectives  119 us (53%)
  waiting for transfers between devices  63.7 us (29%)
  local copies, waits for them, and re-layouts  19.1 us (9%)
  between operations  13.5 us (6%)
  matrix products  3.95 us (2%)
    all_to_all x1, blocking collectives, shards(): lax.all_to_all(buffer, 'expert', split_axis=0, concat_axis=0, tiled=True)  65.7 us
    unnamed x2, waiting for transfers between devices  63.7 us
    all_gather x1, blocking collectives, shards(): lax.all_gather(tokens, 'tensor', axis=1, tiled=True)  29.9 us
    all_to_all x1, blocking collectives, shards(): lax.all_to_all(scattered, 'expert', split_axis=1, concat_axis=1, tiled=True)  23.8 us
    unnamed x8, local copies, waits for them, and re-layouts  15.2 us
  transfers between devices with their start and end apart: 1, of which 1 were waited for; matrix products, arithmetic and copies ran while one was open for 0% of the time, Pallas kernels for 0%

commit v1 on v0

v1 whole, which is shorter than its diff:
```python
import functools

import jax
import jax.numpy as jnp
from jax import lax
from jax.experimental import pallas as pl
from jax.experimental.pallas import tpu as pltpu
from jax.sharding import PartitionSpec as P

LANES = 128
CAPACITY = 3
SPLIT = 2
VMEM = pl.BlockSpec(memory_space=pltpu.VMEM)
PARAMS = pltpu.CompilerParams(vmem_limit_bytes=48 * 1024 * 1024)


def iota(shape, dim):
    return lax.broadcasted_iota(jnp.int32, shape, dim)


def pair_column(values):
    top, toks = values.shape
    shape = (toks, top, toks)
    picked = jnp.where(iota(shape, 0) == iota(shape, 2), values[None], 0.0)
    return jnp.sum(picked, axis=2, keepdims=True)


def slot_columns(ids):
    top, toks = ids.shape
    pairs = top * toks
    down = pair_column(ids.astype(jnp.float32)).reshape(pairs, 1)
    ip, iq = iota((pairs, pairs), 0), iota((pairs, pairs), 1)
    across = jnp.sum(jnp.where(ip == iq, down, 0.0), axis=0, keepdims=True)
    same = down == across
    slot_down = jnp.sum(jnp.where(same & (iq < ip), 1.0, 0.0), axis=1, keepdims=True)
    slot_across = jnp.sum(jnp.where(same & (ip < iq), 1.0, 0.0), axis=0, keepdims=True)
    return (
        (CAPACITY * down + slot_down).astype(jnp.int32),
        (CAPACITY * across + slot_across).astype(jnp.int32),
    )


def pack_kernel(w_in_ref, w_down_ref, *out_refs):
    parts = len(out_refs)
    me = lax.axis_index("tensor")
    mine = lax.rem(me, parts)
    slices = out_refs[0].shape[1] // LANES
    hid = w_down_ref.shape[1]
    for r, out in enumerate(out_refs):
        other = jnp.bitwise_xor(mine, r)
        for j in range(slices):
            src = pl.ds(pl.multiple_of((parts * j + other) * LANES, LANES), LANES)
            dst = pl.ds(j * LANES, LANES)
            for e in range(2):
                for g in range(2):
                    out[pl.ds((2 * e + g) * hid, hid), dst] = w_in_ref[e, g, :, src]
                out[pl.ds((4 + e) * hid, hid), dst] = w_down_ref[e, :, src]


def dispatch_kernel(ids_ref, tok_ref, out_ref, scratch):
    slices, toks, _ = tok_ref.shape
    rows = out_ref.shape[0] // slices
    _, across = slot_columns(ids_ref[...])
    pairs = across.shape[1]
    placing = jnp.where(iota((rows, pairs), 0) == across, 1.0, 0.0).astype(jnp.bfloat16)
    top = pairs // toks
    token_of = jnp.where(iota((pairs, toks), 0) // top == iota((pairs, toks), 1), 1.0, 0.0)
    table = jnp.dot(
        placing, token_of.astype(jnp.bfloat16), preferred_element_type=jnp.float32
    ).astype(jnp.bfloat16)
    for j in range(slices):
        scratch[pl.ds(j, rows, stride=slices), :] = jnp.dot(
            table, tok_ref[j], preferred_element_type=jnp.float32
        )
    out_ref[...] = scratch[...].astype(jnp.bfloat16)


def unpack_rows(ref, scratch, slices):
    rows = ref.shape[0] // slices
    scratch[...] = ref[...].astype(jnp.float32)
    return jnp.concatenate(
        [
            scratch[pl.ds(j, rows, stride=slices), :].astype(jnp.bfloat16)
            for j in range(slices)
        ],
        axis=1,
    )


def first_of_pair(shape, dim):
    return lax.rem(iota(shape, dim), 2 * CAPACITY) < CAPACITY


def up_kernel(parts, *refs):
    x_ref, w_refs, out_ref, send_ref, scratch = refs[0], refs[1 : 1 + parts], *refs[1 + parts :]
    slices = w_refs[0].shape[1] // LANES
    x = unpack_rows(x_ref, scratch, slices)
    rows = x.shape[0]
    hid = w_refs[0].shape[0] // 6
    first = first_of_pair((2 * hid, rows), 1)
    for r in range(parts):
        both = lax.dot_general(
            w_refs[r][pl.ds(0, 4 * hid), :],
            x,
            (((1,), (1,)), ((), ())),
            preferred_element_type=jnp.float32,
        )
        part = jnp.where(first, both[: 2 * hid], both[2 * hid :])
        out_ref[r] = part
        send_ref[r] = part.astype(jnp.bfloat16)


def down_kernel(parts, *refs):
    own_ref, got_ref, w_refs, out_ref, scratch = (
        refs[0],
        refs[1],
        refs[2 : 2 + parts],
        *refs[2 + parts :],
    )
    slices = w_refs[0].shape[1] // LANES
    hid = w_refs[0].shape[0] // 6
    rows = own_ref.shape[2]
    first = first_of_pair((hid, rows), 1)
    values, weights = [], []
    for r in range(parts):
        pre = own_ref[r] + got_ref[r ^ 1].astype(jnp.float32)
        gate, up = pre[:hid], pre[hid:]
        hidden = gate / (1.0 + jnp.exp(-gate)) * up
        values += [jnp.where(first, hidden, 0.0), jnp.where(first, 0.0, hidden)]
        weights.append(w_refs[r][pl.ds(4 * hid, 2 * hid), :])
    values = jnp.concatenate(values, axis=0).T.astype(jnp.bfloat16)
    weights = jnp.concatenate(weights, axis=0)
    out = jnp.dot(values, weights, preferred_element_type=jnp.float32)
    for j in range(slices):
        scratch[pl.ds(j, rows, stride=slices), :] = out[:, j * LANES : (j + 1) * LANES]
    out_ref[...] = scratch[...].astype(jnp.bfloat16)


def combine_kernel(ids_ref, gates_ref, x_ref, out_ref, scratch):
    slices, toks, _ = out_ref.shape
    top = ids_ref.shape[0]
    down, _ = slot_columns(ids_ref[...])
    values = unpack_rows(x_ref, scratch, slices)
    rows = values.shape[0]
    picking = jnp.where(down == iota((top * toks, rows), 1), 1.0, 0.0).astype(jnp.bfloat16)
    picked = jnp.dot(picking, values, preferred_element_type=jnp.float32)
    gates = gates_ref[...]
    weights = pair_column(gates / jnp.sum(gates, axis=0, keepdims=True))
    mixed = jnp.sum(picked.reshape(toks, top, slices * LANES) * weights, axis=1)
    for j in range(slices):
        out_ref[j] = mixed[:, j * LANES : (j + 1) * LANES]


def call(kernel, shapes, args, scratch=()):
    return pl.pallas_call(
        kernel,
        out_shape=shapes,
        in_specs=[VMEM] * len(args),
        out_specs=jax.tree.map(lambda _: VMEM, shapes),
        scratch_shapes=list(scratch),
        compiler_params=PARAMS,
    )(*args)


def shards(tokens, expert_ids, gate_scores, w_in, w_down):
    n_expert, n_tensor = lax.axis_size("expert"), lax.axis_size("tensor")
    parts = SPLIT
    slices = n_tensor // parts
    toks = tokens.shape[0]
    exp_dev, _, hid, _ = w_in.shape
    slots = exp_dev * CAPACITY
    rows = n_expert * slots
    groups = [[parts * j + q for j in range(slices)] for q in range(parts)]
    ids, gates = expert_ids.T, gate_scores.T

    def bf16(*shape):
        return jax.ShapeDtypeStruct(shape, jnp.bfloat16)

    def f32(*shape):
        return jax.ShapeDtypeStruct(shape, jnp.float32)

    def exchange(value, r):
        return lax.ppermute(value, "tensor", [(i, i ^ r) for i in range(n_tensor)])

    packed = call(pack_kernel, [bf16(6 * hid, slices * LANES)] * parts, (w_in, w_down))
    weights = [packed[0]] + [exchange(packed[r], r) for r in range(1, parts)]

    gathered = lax.all_gather(tokens, "tensor", axis=0, axis_index_groups=groups)
    wide = pltpu.VMEM((rows * slices, LANES), jnp.float32)
    sent = call(dispatch_kernel, bf16(rows * slices, LANES), (ids, gathered), [wide])
    arrived = lax.all_to_all(
        sent.reshape(n_expert, slots * slices, LANES), "expert", 0, 0, tiled=True
    ).reshape(rows * slices, LANES)
    own, send = call(
        functools.partial(up_kernel, parts),
        [f32(parts, 2 * hid, rows), bf16(parts, 2 * hid, rows)],
        (arrived, *weights),
        [wide],
    )
    got = exchange(send, 1)
    out = call(
        functools.partial(down_kernel, parts),
        bf16(rows * slices, LANES),
        (own, got, *weights),
        [wide],
    )
    returned = lax.all_to_all(
        out.reshape(n_expert, slots * slices, LANES), "expert", 0, 0, tiled=True
    ).reshape(rows * slices, LANES)
    partial = call(combine_kernel, f32(slices, toks, LANES), (ids, gates, returned), [wide])
    pieces = lax.all_to_all(partial, "tensor", 0, 0, tiled=True, axis_index_groups=groups)
    return jnp.sum(pieces, axis=0).astype(jnp.bfloat16)


def solution(mesh):
    in_specs = (
        P("expert", "tensor"),
        P("expert", None),
        P("expert", None),
        P("expert", None, "tensor", None),
        P("expert", "tensor", None),
    )
    out_specs = P("expert", "tensor")
    return jax.shard_map(shards, mesh=mesh, in_specs=in_specs, out_specs=out_specs, check_vma=False)
```

time: 223 us -> 120 us (0.54)
  the two profiles are of different devices: /device:TPU:16 before, /device:TPU:4 now
where the time goes in v1:
time: 120 us
  blocking collectives  79.9 us (67%)
  waiting for transfers between devices  17.8 us (15%)
  starting transfers between devices  17.5 us (15%)
  Pallas kernels  3.93 us (3%)
    all_gather x1, blocking collectives, shards(): lax.all_gather(tokens, 'tensor', axis=0, axis_index_groups=groups)  37 us
    all_to_all x1, blocking collectives, shards(): lax.all_to_all(out.reshape(n_expert, slots * slices, LANES), 'expert', 0,...  30.6 us
    all_to_all x1, waiting for transfers between devices, shards(): lax.all_to_all(sent.reshape(n_expert, slots * slices, LANES), 'expert', 0...  14.5 us
    all_to_all x1, starting transfers between devices, shards(): lax.all_to_all(sent.reshape(n_expert, slots * slices, LANES), 'expert', 0...  13.7 us
    all_to_all x1, blocking collectives, shards(): lax.all_to_all(partial, 'tensor', 0, 0, tiled=True, axis_index_groups=gro...  12.4 us
    pallas_call x5, Pallas kernels, call(): pl.pallas_call(kernel, out_shape=shapes, in_specs=[VMEM] * len(args), out...  3.93 us
    ppermute x2, starting transfers between devices, exchange(): return lax.ppermute(value, 'tensor', [(i, i ^ r) for i in range(n_tensor)])  3.84 us
    ppermute x2, waiting for transfers between devices, exchange(): return lax.ppermute(value, 'tensor', [(i, i ^ r) for i in range(n_tensor)])  3.31 us
  transfers between devices with their start and end apart: 3, of which 3 were waited for; matrix products, arithmetic and copies ran while one was open for 0% of the time, Pallas kernels for 0%

profile of v1, /device:TPU:4, one launch (start us, length us, event | category | flops | bytes accessed | tf_op | source)
XLA Modules:
  0.0 119.9 jit_solution(1529905941018629164)
XLA Ops:
  0.0 0.0 copy-start.2
  0.0 37.0 %all-gather = bf16[128,128]{1,0:T(8,128)(2,1)S(1)} all-gather(bf16[16,128]{1,0:T(8,128)(2,1)} %param.5), channel_id=2, replica_groups={{0,2,4,6,8,10,12,14},{1,3,5,7,9,11,13,15},{16,18,20,22,24,26,28,30},{17..., dimensions={0}, use_global_device_ids=true | all-gather | bytes 36864 | tf_op jit(solution)/shard_map/all_gather | solution.py:188
  37.0 0.0 copy-done.2
  37.0 1.7 %shard_map.55 = bf16[3072,128]{1,0:T(8,128)(2,1)} custom-call(s32[8,16]{1,0:T(8,128)S(1)} %bitcast.11, bf16[8,16,128]{2,1,0:T(8,128)(2,1)S(1)} %bitcast.10), custom_call_target="tpu_custom_call" | custom-call | tf_op jit(solution)/shard_map/pallas_call | solution.py:155
  38.6 0.0 copy-start
  38.6 0.0 copy-start.1
  38.6 13.7 %all-to-all-start = ((bf16[64,48,128]{2,1,0:T(8,128)(2,1)}), bf16[64,48,128]{2,1,0:T(8,128)(2,1)S(1)}, u32[]{:S(2)}, u32[]{:S(2)}) async-start(bf16[64,48,128]{2,1,0:T(8,128)(2,1)} %bitcast.3), calls=%async_computation | async-start | bytes 1572864 | tf_op jit(solution)/shard_map/all_to_all | solution.py:191
  52.3 0.0 copy-done
  52.3 0.0 copy-done.1
  52.3 0.3 shard_map.56
  52.7 1.9 %collective-permute-start = (bf16[288,1024]{1,0:T(8,128)(2,1)S(1)}, bf16[288,1024]{1,0:T(8,128)(2,1)S(1)}, u32[]{:S(2)}, u32[]{:S(2)}) collective-permute-start(bf16[288,1024]{1,0:T(8,128)(2,1)S(1)} %get-tuple-element.10), channel_id=1, source_target_pairs={{0,1},{1,0},{2,3},{3,2},{4,5},{5,4},{6,7},{7,6},{8,9},{9,8},{10,11... | collective-permute-start | bytes 1769480 | tf_op jit(solution)/shard_map/ppermute | solution.py:183
  54.6 2.0 %collective-permute-done.refs_2_.refs_3_ = bf16[288,1024]{1,0:T(8,128)(2,1)S(1)} collective-permute-done((bf16[288,1024]{1,0:T(8,128)(2,1)S(1)}, bf16[288,1024]{1,0:T(8,128)(2,1)S(1)}, u32[]{:S(2)}, u32[]{:S(2)}) %collective-permute-start) | collective-permute-done | bytes 589856 | tf_op jit(solution)/shard_map/ppermute | solution.py:183
  56.6 14.5 %all-to-all-done = bf16[64,48,128]{2,1,0:T(8,128)(2,1)S(1)} async-done(((bf16[64,48,128]{2,1,0:T(8,128)(2,1)}), bf16[64,48,128]{2,1,0:T(8,128)(2,1)S(1)}, u32[]{:S(2)}, u32[]{:S(2)}) %all-to-all-start) | async-done | bytes 786464 | tf_op jit(solution)/shard_map/all_to_all | solution.py:191
  71.1 0.8 shard_map.57
  71.9 1.9 %collective-permute-start.1 = (bf16[2,96,384]{2,1,0:T(8,128)(2,1)S(1)}, bf16[2,96,384]{2,1,0:T(8,128)(2,1)S(1)}, u32[]{:S(2)}, u32[]{:S(2)}) collective-permute-start(bf16[2,96,384]{2,1,0:T(8,128)(2,1)S(1)} %get-tuple-element.12), channel_id=1, source_target_pairs={{0,1},{1,0},{2,3},{3,2},{4,5},{5,4},{6,7},{7,6},{8,9},{9,8},{10,11... | collective-permute-start | bytes 442376 | tf_op jit(solution)/shard_map/ppermute | solution.py:183
  73.8 1.3 %collective-permute-done.1.refs_1_ = bf16[2,96,384]{2,1,0:T(8,128)(2,1)S(1)} collective-permute-done((bf16[2,96,384]{2,1,0:T(8,128)(2,1)S(1)}, bf16[2,96,384]{2,1,0:T(8,128)(2,1)S(1)}, u32[]{:S(2)}, u32[]{:S(2)}) %collective-permute-start.1) | collective-permute-done | bytes 147488 | tf_op jit(solution)/shard_map/ppermute | solution.py:183
  75.1 0.6 shard_map.58
  75.7 0.0 copy-start.3
  75.7 30.6 %all_to_all.15 = bf16[64,48,128]{2,1,0:T(8,128)(2,1)S(1)} all-to-all(bf16[64,48,128]{2,1,0:T(8,128)(2,1)S(1)} %bitcast.9), channel_id=1, replica_groups=mesh['expert'=64,'tensor'=16] {'expert'}, dimensions={0} | all-to-all | bytes 1572864 | tf_op jit(solution)/shard_map/all_to_all | solution.py:207
  106.3 0.0 copy-done.3
  106.3 0.6 shard_map.59
  106.9 12.4 %all_to_all.16 = f32[8,16,128]{2,1,0:T(8,128)S(1)} all-to-all(f32[8,16,128]{2,1,0:T(8,128)S(1)} %shard_map.59), channel_id=1, replica_groups={{0,2,4,6,8,10,12,14},{1,3,5,7,9,11,13,15},{16,18,20,22,24,26,28,30},{17..., dimensions={0} | all-to-all | bytes 131072 | tf_op jit(solution)/shard_map/all_to_all | solution.py:211
  119.3 0.6 reduce_sum.9
Async XLA Ops:
  0.0 37.0 %copy-start.2 = (s32[16,8]{0,1:T(8,128)S(1)}, s32[16,8]{0,1:T(8,128)}, u32[]{:S(2)}) copy-start(s32[16,8]{0,1:T(8,128)} %param.6) | copy-start | bytes 1540
  38.6 13.7 %copy-start = (bf16[2,2,48,2048]{3,2,1,0:T(8,128)(2,1)S(1)}, bf16[2,2,48,2048]{3,2,1,0:T(8,128)(2,1)}, u32[]{:S(2)}) copy-start(bf16[2,2,48,2048]{3,2,1,0:T(8,128)(2,1)} %w_in_ref.1) | copy-start | bytes 2359300
  38.6 13.7 %copy-start.1 = (bf16[2,48,2048]{2,1,0:T(8,128)(2,1)S(1)}, bf16[2,48,2048]{2,1,0:T(8,128)(2,1)}, u32[]{:S(2)}) copy-start(bf16[2,48,2048]{2,1,0:T(8,128)(2,1)} %w_down_ref.1) | copy-start | bytes 1179652
  38.6 32.4 %all-to-all-start = ((bf16[64,48,128]{2,1,0:T(8,128)(2,1)}), bf16[64,48,128]{2,1,0:T(8,128)(2,1)S(1)}, u32[]{:S(2)}, u32[]{:S(2)}) async-start(bf16[64,48,128]{2,1,0:T(8,128)(2,1)} %bitcast.3), calls=%async_computation | async-start | bytes 1572864 | tf_op jit(solution)/shard_map/all_to_all | solution.py:191
  52.7 3.9 %collective-permute-start = (bf16[288,1024]{1,0:T(8,128)(2,1)S(1)}, bf16[288,1024]{1,0:T(8,128)(2,1)S(1)}, u32[]{:S(2)}, u32[]{:S(2)}) collective-permute-start(bf16[288,1024]{1,0:T(8,128)(2,1)S(1)} %get-tuple-element.10), channel_id=1, source_target_pairs={{0,1},{1,0},{2,3},{3,2},{4,5},{5,4},{6,7},{7,6},{8,9},{9,8},{10,11... | collective-permute-start | bytes 1769480 | tf_op jit(solution)/shard_map/ppermute | solution.py:183
  71.9 3.3 %collective-permute-start.1 = (bf16[2,96,384]{2,1,0:T(8,128)(2,1)S(1)}, bf16[2,96,384]{2,1,0:T(8,128)(2,1)S(1)}, u32[]{:S(2)}, u32[]{:S(2)}) collective-permute-start(bf16[2,96,384]{2,1,0:T(8,128)(2,1)S(1)} %get-tuple-element.12), channel_id=1, source_target_pairs={{0,1},{1,0},{2,3},{3,2},{4,5},{5,4},{6,7},{7,6},{8,9},{9,8},{10,11... | collective-permute-start | bytes 442376 | tf_op jit(solution)/shard_map/ppermute | solution.py:183
  75.7 30.6 %copy-start.3 = (f32[16,8]{0,1:T(8,128)S(1)}, f32[16,8]{0,1:T(8,128)}, u32[]{:S(2)}) copy-start(f32[16,8]{0,1:T(8,128)} %param.7) | copy-start | bytes 1540

commit v2 on v1

v2 whole, which is shorter than its diff:
```python
import functools

import jax
import jax.numpy as jnp
from jax import lax
from jax.experimental import pallas as pl
from jax.experimental.pallas import tpu as pltpu
from jax.sharding import PartitionSpec as P

LANES = 128
CAPACITY = 3
QUAD = 4
VMEM = pl.BlockSpec(memory_space=pltpu.VMEM)
PARAMS = pltpu.CompilerParams(vmem_limit_bytes=48 * 1024 * 1024)


def iota(shape, dim):
    return lax.broadcasted_iota(jnp.int32, shape, dim)


def pair_column(values):
    top, toks = values.shape
    shape = (toks, top, toks)
    picked = jnp.where(iota(shape, 0) == iota(shape, 2), values[None], 0.0)
    return jnp.sum(picked, axis=2, keepdims=True)


def slot_columns(ids):
    top, toks = ids.shape
    pairs = top * toks
    down = pair_column(ids.astype(jnp.float32)).reshape(pairs, 1)
    ip, iq = iota((pairs, pairs), 0), iota((pairs, pairs), 1)
    across = jnp.sum(jnp.where(ip == iq, down, 0.0), axis=0, keepdims=True)
    same = down == across
    slot_down = jnp.sum(jnp.where(same & (iq < ip), 1.0, 0.0), axis=1, keepdims=True)
    slot_across = jnp.sum(jnp.where(same & (ip < iq), 1.0, 0.0), axis=0, keepdims=True)
    return (
        (CAPACITY * down + slot_down).astype(jnp.int32),
        (CAPACITY * across + slot_across).astype(jnp.int32),
    )


def pack_kernel(w_in_ref, w_down_ref, keep_ref, core_ref, chip_ref):
    me = lax.axis_index("tensor")
    quad, place = lax.div(me, QUAD), lax.rem(me, QUAD)
    slices = keep_ref.shape[1] // LANES
    hid = w_down_ref.shape[1]
    for r, out in enumerate((keep_ref, core_ref, chip_ref.at[0], chip_ref.at[1])):
        for j in range(slices):
            owner = QUAD * jnp.bitwise_xor(quad, j) + jnp.bitwise_xor(place, r)
            src = pl.ds(pl.multiple_of(owner * LANES, LANES), LANES)
            dst = pl.ds(j * LANES, LANES)
            for e in range(2):
                for g in range(2):
                    out[pl.ds((2 * e + g) * hid, hid), dst] = w_in_ref[e, g, :, src]
                out[pl.ds((4 + e) * hid, hid), dst] = w_down_ref[e, :, src]


def dispatch_kernel(ids_ref, *refs):
    tok_refs, (out_ref, scratch) = refs[:-2], refs[-2:]
    slices = len(tok_refs)
    toks = tok_refs[0].shape[0]
    rows = out_ref.shape[0] // slices
    _, across = slot_columns(ids_ref[...])
    pairs = across.shape[1]
    placing = jnp.where(iota((rows, pairs), 0) == across, 1.0, 0.0).astype(jnp.bfloat16)
    top = pairs // toks
    token_of = jnp.where(iota((pairs, toks), 0) // top == iota((pairs, toks), 1), 1.0, 0.0)
    table = jnp.dot(
        placing, token_of.astype(jnp.bfloat16), preferred_element_type=jnp.float32
    ).astype(jnp.bfloat16)
    for j in range(slices):
        scratch[pl.ds(j, rows, stride=slices), :] = jnp.dot(
            table, tok_refs[j][...], preferred_element_type=jnp.float32
        )
    out_ref[...] = scratch[...].astype(jnp.bfloat16)


def unpack_rows(ref, scratch, slices):
    rows = ref.shape[0] // slices
    scratch[...] = ref[...].astype(jnp.float32)
    return jnp.concatenate(
        [
            scratch[pl.ds(j, rows, stride=slices), :].astype(jnp.bfloat16)
            for j in range(slices)
        ],
        axis=1,
    )


def first_of_pair(shape, dim):
    return lax.rem(iota(shape, dim), 2 * CAPACITY) < CAPACITY


def up_kernel(x_ref, w0_ref, w1_ref, w23_ref, w3_ref, own_ref, send_ref, scratch):
    slices = w0_ref.shape[1] // LANES
    x = unpack_rows(x_ref, scratch, slices)
    rows = x.shape[0]
    hid = w0_ref.shape[0] // 6
    first = first_of_pair((2 * hid, rows), 1)
    for r, w_ref in enumerate((w0_ref, w1_ref, w23_ref.at[0], w3_ref)):
        both = lax.dot_general(
            w_ref[pl.ds(0, 4 * hid), :],
            x,
            (((1,), (1,)), ((), ())),
            preferred_element_type=jnp.float32,
        )
        part = jnp.where(first, both[: 2 * hid], both[2 * hid :])
        if r % 2:
            send_ref[r // 2] = part.astype(jnp.bfloat16)
        else:
            own_ref[r // 2] = part


def add_kernel(own_ref, got_ref, sum_ref, send_ref):
    total = own_ref[...] + got_ref[...].astype(jnp.float32)
    sum_ref[...] = total
    send_ref[...] = total.astype(jnp.bfloat16)


def act_kernel(own_ref, got_ref, out_ref):
    hid = out_ref.shape[1]
    for r in range(2):
        pre = own_ref[r] + got_ref[1 - r].astype(jnp.float32)
        gate, up = pre[:hid], pre[hid:]
        out_ref[r] = (gate / (1.0 + jnp.exp(-gate)) * up).astype(jnp.bfloat16)


def down_kernel(own_ref, got_ref, w0_ref, w1_ref, w23_ref, w3_ref, out_ref, scratch):
    slices = w0_ref.shape[1] // LANES
    hid = w0_ref.shape[0] // 6
    rows = own_ref.shape[2]
    first = first_of_pair((hid, rows), 1)
    values, weights = [], []
    for r, w_ref in enumerate((w0_ref, w1_ref, w23_ref.at[0], w3_ref)):
        hidden = (got_ref if r % 2 else own_ref)[r // 2].astype(jnp.float32)
        values += [jnp.where(first, hidden, 0.0), jnp.where(first, 0.0, hidden)]
        weights.append(w_ref[pl.ds(4 * hid, 2 * hid), :])
    values = jnp.concatenate(values, axis=0).T.astype(jnp.bfloat16)
    weights = jnp.concatenate(weights, axis=0)
    out = jnp.dot(values, weights, preferred_element_type=jnp.float32)
    for j in range(slices):
        scratch[pl.ds(j, rows, stride=slices), :] = out[:, j * LANES : (j + 1) * LANES]
    out_ref[...] = scratch[...].astype(jnp.bfloat16)


def combine_kernel(ids_ref, gates_ref, x_ref, *refs):
    out_refs, scratch = refs[:-1], refs[-1]
    slices = len(out_refs)
    top, toks = ids_ref.shape
    down, _ = slot_columns(ids_ref[...])
    values = unpack_rows(x_ref, scratch, slices)
    rows = values.shape[0]
    picking = jnp.where(down == iota((top * toks, rows), 1), 1.0, 0.0).astype(jnp.bfloat16)
    picked = jnp.dot(picking, values, preferred_element_type=jnp.float32)
    gates = gates_ref[...]
    weights = pair_column(gates / jnp.sum(gates, axis=0, keepdims=True))
    mixed = jnp.sum(picked.reshape(toks, top, slices * LANES) * weights, axis=1)
    for j, out_ref in enumerate(out_refs):
        out_ref[...] = mixed[:, j * LANES : (j + 1) * LANES]


def call(kernel, shapes, args, scratch=()):
    return pl.pallas_call(
        kernel,
        out_shape=shapes,
        in_specs=[VMEM] * len(args),
        out_specs=jax.tree.map(lambda _: VMEM, shapes),
        scratch_shapes=list(scratch),
        compiler_params=PARAMS,
    )(*args)


def shards(tokens, expert_ids, gate_scores, w_in, w_down):
    n_expert, n_tensor = lax.axis_size("expert"), lax.axis_size("tensor")
    slices = n_tensor // QUAD
    toks = tokens.shape[0]
    exp_dev, _, hid, _ = w_in.shape
    slots = exp_dev * CAPACITY
    rows = n_expert * slots
    ids, gates = expert_ids.T, gate_scores.T

    def bf16(*shape):
        return jax.ShapeDtypeStruct(shape, jnp.bfloat16)

    def f32(*shape):
        return jax.ShapeDtypeStruct(shape, jnp.float32)

    def exchange(value, r):
        return lax.ppermute(value, "tensor", [(i, i ^ r) for i in range(n_tensor)])

    def across_experts(value):
        value = value.reshape(n_expert, slots * slices, LANES)
        value = lax.all_to_all(value, "expert", 0, 0, tiled=True)
        return value.reshape(rows * slices, LANES)

    gathered = [tokens] + [exchange(tokens, QUAD * r) for r in range(1, slices)]
    part = bf16(6 * hid, slices * LANES)
    keep, core, chip = call(
        pack_kernel, [part, part, bf16(2, 6 * hid, slices * LANES)], (w_in, w_down)
    )
    chip = exchange(chip, 2)
    weights = (keep, exchange(core, 1), chip, exchange(chip[1], 1))

    wide = pltpu.VMEM((rows * slices, LANES), jnp.float32)
    sent = call(dispatch_kernel, bf16(rows * slices, LANES), (ids, *gathered), [wide])
    arrived = across_experts(sent)
    pair = (2, 2 * hid, rows)
    own, send = call(up_kernel, [f32(*pair), bf16(*pair)], (arrived, *weights), [wide])
    own, send = call(add_kernel, [f32(*pair), bf16(*pair)], (own, exchange(send, 1)))
    hidden = call(act_kernel, bf16(2, hid, rows), (own, exchange(send, 2)))
    out = call(
        down_kernel, bf16(rows * slices, LANES), (hidden, exchange(hidden, 1), *weights), [wide]
    )
    returned = across_experts(out)
    mixed = call(combine_kernel, [f32(toks, LANES)] * slices, (ids, gates, returned), [wide])
    total = mixed[0]
    for r in range(1, slices):
        total = total + exchange(mixed[r], QUAD * r)
    return total.astype(jnp.bfloat16)


def solution(mesh):
    in_specs = (
        P("expert", "tensor"),
        P("expert", None),
        P("expert", None),
        P("expert", None, "tensor", None),
        P("expert", "tensor", None),
    )
    out_specs = P("expert", "tensor")
    return jax.shard_map(shards, mesh=mesh, in_specs=in_specs, out_specs=out_specs, check_vma=False)
```

time: 120 us -> 118 us (0.983)
  blocking collectives: 79.9 us -> 21.9 us
  starting transfers between devices: 17.5 us -> 62.7 us
  waiting for transfers between devices: 17.8 us -> 26.4 us
  local copies, waits for them, and re-layouts: 0.02 us -> 2.16 us
    ppermute x2 -> x12, starting transfers between devices: 3.84 us -> 49.2 us  [exchange(): return lax.ppermute(value, 'tensor', [(i, i ^ r) for i in range(n_tensor)])]
    all_gather x1 -> x0, blocking collectives: 37 us -> none  [shards(): lax.all_gather(tokens, 'tensor', axis=0, axis_index_groups=groups)]
    all_to_all x2 -> x1, blocking collectives: 43 us -> 21.9 us  [across_experts(): value = lax.all_to_all(value, 'expert', 0, 0, tiled=True)]
    ppermute x2 -> x12, waiting for transfers between devices: 3.31 us -> 15.7 us  [exchange(): return lax.ppermute(value, 'tensor', [(i, i ^ r) for i in range(n_tensor)])]
    all_to_all x1, waiting for transfers between devices: 14.5 us -> 10.7 us  [across_experts(): value = lax.all_to_all(value, 'expert', 0, 0, tiled=True)]
    unnamed x8 -> x10, local copies, waits for them, and re-layouts: 0.02 us -> 2.14 us
    pallas_call x5 -> x7, Pallas kernels: 3.93 us -> 3.32 us  [call(): pl.pallas_call(kernel, out_shape=shapes, in_specs=[VMEM] * len(args), out...]
  transfers between devices with their start and end apart: 3 -> 13, of which waited for: 3 -> 8; matrix products, arithmetic and copies ran while one was open for 0% -> 0% of each run, Pallas kernels for 0% -> 1%
where the time goes in v2:
time: 118 us; the launch traced here: 117 us
  starting transfers between devices  62.7 us (53%)
  waiting for transfers between devices  26.4 us (22%)
  blocking collectives  21.9 us (19%)
  Pallas kernels  3.32 us (3%)
  local copies, waits for them, and re-layouts  2.16 us (2%)
    ppermute x12, starting transfers between devices, exchange(): return lax.ppermute(value, 'tensor', [(i, i ^ r) for i in range(n_tensor)])  49.2 us
    all_to_all x1, blocking collectives, across_experts(): value = lax.all_to_all(value, 'expert', 0, 0, tiled=True)  21.9 us
    ppermute x12, waiting for transfers between devices, exchange(): return lax.ppermute(value, 'tensor', [(i, i ^ r) for i in range(n_tensor)])  15.7 us
    all_to_all x1, starting transfers between devices, across_experts(): value = lax.all_to_all(value, 'expert', 0, 0, tiled=True)  13.5 us
    all_to_all x1, waiting for transfers between devices, across_experts(): value = lax.all_to_all(value, 'expert', 0, 0, tiled=True)  10.7 us
    pallas_call x7, Pallas kernels, call(): pl.pallas_call(kernel, out_shape=shapes, in_specs=[VMEM] * len(args), out...  3.32 us
  transfers between devices with their start and end apart: 13, of which 8 were waited for; matrix products, arithmetic and copies ran while one was open for 0% of the time, Pallas kernels for 1%

profile of v2, /device:TPU:4, one launch (start us, length us, event | category | flops | bytes accessed | tf_op | source)
XLA Modules:
  0.0 117.3 jit_solution(6823573477513213282)
XLA Ops:
  0.0 0.0 copy-start
  0.0 1.1 copy-done
  1.1 0.0 copy-start.1
  1.1 1.0 copy-done.1
  2.1 0.0 copy-start.3
  2.1 0.0 copy-start.2
  2.1 0.3 shard_map.56
  2.5 5.2 %collective-permute-start.4 = (bf16[2,288,512]{2,1,0:T(8,128)(2,1)S(1)}, bf16[2,288,512]{2,1,0:T(8,128)(2,1)S(1)}, u32[]{:S(2)}, u32[]{:S(2)}) collective-permute-start(bf16[2,288,512]{2,1,0:T(8,128)(2,1)S(1)} %get-tuple-element.18), channel_id=1, source_target_pairs={{0,2},{1,3},{2,0},{3,1},{4,6},{5,7},{6,4},{7,5},{8,10},{9,11},{10,... | collective-permute-start | bytes 1769480 | tf_op jit(solution)/shard_map/ppermute | solution.py:190
  7.6 0.0 copy-done.3
  7.7 13.7 %collective-permute-start.1 = (bf16[16,128]{1,0:T(8,128)(2,1)S(1)}, bf16[16,128]{1,0:T(8,128)(2,1)S(1)}, u32[]{:S(2)}, u32[]{:S(2)}) collective-permute-start(bf16[16,128]{1,0:T(8,128)(2,1)S(1)} %copy-done.3), channel_id=1, source_target_pairs={{0,8},{1,9},{2,10},{3,11},{4,12},{5,13},{6,14},{7,15},{8,0},{9,1},... | collective-permute-start | bytes 12296 | tf_op jit(solution)/shard_map/ppermute | solution.py:190
  21.3 6.1 %collective-permute-start = (bf16[16,128]{1,0:T(8,128)(2,1)S(1)}, bf16[16,128]{1,0:T(8,128)(2,1)S(1)}, u32[]{:S(2)}, u32[]{:S(2)}) collective-permute-start(bf16[16,128]{1,0:T(8,128)(2,1)S(1)} %copy-done.3), channel_id=1, source_target_pairs={{0,4},{1,5},{2,6},{3,7},{4,0},{5,1},{6,2},{7,3},{8,12},{9,13},{10,... | collective-permute-start | bytes 12296 | tf_op jit(solution)/shard_map/ppermute | solution.py:190
  27.4 1.9 %collective-permute-start.2 = (bf16[16,128]{1,0:T(8,128)(2,1)S(1)}, bf16[16,128]{1,0:T(8,128)(2,1)S(1)}, u32[]{:S(2)}, u32[]{:S(2)}) collective-permute-start(bf16[16,128]{1,0:T(8,128)(2,1)S(1)} %copy-done.3), channel_id=1, source_target_pairs={{0,12},{1,13},{2,14},{3,15},{4,8},{5,9},{6,10},{7,11},{8,4},{9,5},... | collective-permute-start | bytes 12296 | tf_op jit(solution)/shard_map/ppermute | solution.py:190
  29.4 3.4 %collective-permute-done.1.refs_2_ = bf16[16,128]{1,0:T(8,128)(2,1)S(1)} collective-permute-done((bf16[16,128]{1,0:T(8,128)(2,1)S(1)}, bf16[16,128]{1,0:T(8,128)(2,1)S(1)}, u32[]{:S(2)}, u32[]{:S(2)}) %collective-permute-start.1) | collective-permute-done | bytes 4128 | tf_op jit(solution)/shard_map/ppermute | solution.py:190
  32.8 0.0 collective-permute-done.refs_1_
  32.8 2.3 %collective-permute-done.2.refs_3_ = bf16[16,128]{1,0:T(8,128)(2,1)S(1)} collective-permute-done((bf16[16,128]{1,0:T(8,128)(2,1)S(1)}, bf16[16,128]{1,0:T(8,128)(2,1)S(1)}, u32[]{:S(2)}, u32[]{:S(2)}) %collective-permute-start.2) | collective-permute-done | bytes 4128 | tf_op jit(solution)/shard_map/ppermute | solution.py:190
  35.0 0.0 copy-done.2
  35.1 1.3 %shard_map.55 = bf16[1536,128]{1,0:T(8,128)(2,1)} custom-call(s32[8,16]{1,0:T(8,128)S(1)} %bitcast.11, bf16[16,128]{1,0:T(8,128)(2,1)S(1)} %copy-done.3, bf16[16,128]{1,0:T(8,128)(2,1)S(1)} %collective-permute-done.refs_1_, bf16[16,128]{1,0:T(8,128)(2,1)S(1)} %collective-permute-done.1.refs_2_, bf16[16,128]{1,0:T(8,128)(2,1)S(1)} %collective-permute-done.2.refs_3_), custom_call_target="tpu_custom_call" | custom-call | tf_op jit(solution)/shard_map/pallas_call | solution.py:164
  36.4 13.5 %all-to-all-start = ((bf16[64,24,128]{2,1,0:T(8,128)(2,1)}), bf16[64,24,128]{2,1,0:T(8,128)(2,1)S(1)}, u32[]{:S(2)}, u32[]{:S(2)}) async-start(bf16[64,24,128]{2,1,0:T(8,128)(2,1)} %bitcast.2), calls=%async_computation | async-start | bytes 786432 | tf_op jit(solution)/shard_map/all_to_all | solution.py:194
  49.9 1.9 %collective-permute-start.3 = (bf16[288,512]{1,0:T(8,128)(2,1)S(1)}, bf16[288,512]{1,0:T(8,128)(2,1)S(1)}, u32[]{:S(2)}, u32[]{:S(2)}) collective-permute-start(bf16[288,512]{1,0:T(8,128)(2,1)S(1)} %get-tuple-element.17), channel_id=1, source_target_pairs={{0,1},{1,0},{2,3},{3,2},{4,5},{5,4},{6,7},{7,6},{8,9},{9,8},{10,11... | collective-permute-start | bytes 884744 | tf_op jit(solution)/shard_map/ppermute | solution.py:190
  51.8 0.0 collective-permute-done.4.w23_ref
  51.9 2.4 %collective-permute-start.5 = (bf16[288,512]{1,0:T(8,128)(2,1)S(1)}, bf16[288,512]{1,0:T(8,128)(2,1)S(1)}, u32[]{:S(2)}, u32[]{:S(2)}) collective-permute-start(bf16[288,512]{1,0:T(8,128)(2,1)S(1)} %slice_bitcast_fusion), channel_id=1, source_target_pairs={{0,1},{1,0},{2,3},{3,2},{4,5},{5,4},{6,7},{7,6},{8,9},{9,8},{10,11... | collective-permute-start | bytes 884744 | tf_op jit(solution)/shard_map/ppermute | solution.py:190
  54.3 0.0 collective-permute-done.3.w1_ref
  54.3 10.7 %all-to-all-done = bf16[64,24,128]{2,1,0:T(8,128)(2,1)S(1)} async-done(((bf16[64,24,128]{2,1,0:T(8,128)(2,1)}), bf16[64,24,128]{2,1,0:T(8,128)(2,1)S(1)}, u32[]{:S(2)}, u32[]{:S(2)}) %all-to-all-start) | async-done | bytes 393248 | tf_op jit(solution)/shard_map/all_to_all | solution.py:194
  65.0 0.0 collective-permute-done.5.w3_ref
  65.0 0.7 shard_map.57
  65.7 1.9 %collective-permute-start.6 = (bf16[2,96,384]{2,1,0:T(8,128)(2,1)S(1)}, bf16[2,96,384]{2,1,0:T(8,128)(2,1)S(1)}, u32[]{:S(2)}, u32[]{:S(2)}) collective-permute-start(bf16[2,96,384]{2,1,0:T(8,128)(2,1)S(1)} %get-tuple-element.20), channel_id=1, source_target_pairs={{0,1},{1,0},{2,3},{3,2},{4,5},{5,4},{6,7},{7,6},{8,9},{9,8},{10,11... | collective-permute-start | bytes 442376 | tf_op jit(solution)/shard_map/ppermute | solution.py:190
  67.6 1.3 %collective-permute-done.6.got_ref = bf16[2,96,384]{2,1,0:T(8,128)(2,1)S(1)} collective-permute-done((bf16[2,96,384]{2,1,0:T(8,128)(2,1)S(1)}, bf16[2,96,384]{2,1,0:T(8,128)(2,1)S(1)}, u32[]{:S(2)}, u32[]{:S(2)}) %collective-permute-start.6) | collective-permute-done | bytes 147488 | tf_op jit(solution)/shard_map/ppermute | solution.py:190
  69.0 1.9 %collective-permute-start.7 = (bf16[2,96,384]{2,1,0:T(8,128)(2,1)S(1)}, bf16[2,96,384]{2,1,0:T(8,128)(2,1)S(1)}, u32[]{:S(2)}, u32[]{:S(2)}) collective-permute-start(bf16[2,96,384]{2,1,0:T(8,128)(2,1)S(1)} %get-tuple-element.22), channel_id=1, source_target_pairs={{0,2},{1,3},{2,0},{3,1},{4,6},{5,7},{6,4},{7,5},{8,10},{9,11},{10,... | collective-permute-start | bytes 442376 | tf_op jit(solution)/shard_map/ppermute | solution.py:190
  70.9 5.9 %collective-permute-done.7.got_ref = bf16[2,96,384]{2,1,0:T(8,128)(2,1)S(1)} collective-permute-done((bf16[2,96,384]{2,1,0:T(8,128)(2,1)S(1)}, bf16[2,96,384]{2,1,0:T(8,128)(2,1)S(1)}, u32[]{:S(2)}, u32[]{:S(2)}) %collective-permute-start.7) | collective-permute-done | bytes 147488 | tf_op jit(solution)/shard_map/ppermute | solution.py:190
  76.8 0.1 shard_map.59.own_ref
  76.9 1.9 %collective-permute-start.8 = (bf16[2,48,384]{2,1,0:T(8,128)(2,1)S(1)}, bf16[2,48,384]{2,1,0:T(8,128)(2,1)S(1)}, u32[]{:S(2)}, u32[]{:S(2)}) collective-permute-start(bf16[2,48,384]{2,1,0:T(8,128)(2,1)S(1)} %shard_map.59.own_ref), channel_id=1, source_target_pairs={{0,1},{1,0},{2,3},{3,2},{4,5},{5,4},{6,7},{7,6},{8,9},{9,8},{10,11... | collective-permute-start | bytes 221192 | tf_op jit(solution)/shard_map/ppermute | solution.py:190
  78.8 1.2 %collective-permute-done.8.got_ref = bf16[2,48,384]{2,1,0:T(8,128)(2,1)S(1)} collective-permute-done((bf16[2,48,384]{2,1,0:T(8,128)(2,1)S(1)}, bf16[2,48,384]{2,1,0:T(8,128)(2,1)S(1)}, u32[]{:S(2)}, u32[]{:S(2)}) %collective-permute-start.8) | collective-permute-done | bytes 73760 | tf_op jit(solution)/shard_map/ppermute | solution.py:190
  80.0 0.5 shard_map.60
  80.5 0.0 copy-start.4
  80.5 21.9 %all_to_all.10 = bf16[64,24,128]{2,1,0:T(8,128)(2,1)S(1)} all-to-all(bf16[64,24,128]{2,1,0:T(8,128)(2,1)S(1)} %bitcast.10), channel_id=1, replica_groups=mesh['expert'=64,'tensor'=16] {'expert'}, dimensions={0} | all-to-all | bytes 786432 | tf_op jit(solution)/shard_map/all_to_all | solution.py:194
  102.4 0.0 copy-done.4
  102.4 0.4 shard_map.61
  102.9 4.2 %collective-permute-start.9 = (f32[16,128]{1,0:T(8,128)S(1)}, f32[16,128]{1,0:T(8,128)S(1)}, u32[]{:S(2)}, u32[]{:S(2)}) collective-permute-start(f32[16,128]{1,0:T(8,128)S(1)} %get-tuple-element.24), channel_id=1, source_target_pairs={{0,4},{1,5},{2,6},{3,7},{4,0},{5,1},{6,2},{7,3},{8,12},{9,13},{10,... | collective-permute-start | bytes 24584 | tf_op jit(solution)/shard_map/ppermute | solution.py:190
  107.1 2.0 %collective-permute-start.10 = (f32[16,128]{1,0:T(8,128)S(1)}, f32[16,128]{1,0:T(8,128)S(1)}, u32[]{:S(2)}, u32[]{:S(2)}) collective-permute-start(f32[16,128]{1,0:T(8,128)S(1)} %get-tuple-element.25), channel_id=1, source_target_pairs={{0,8},{1,9},{2,10},{3,11},{4,12},{5,13},{6,14},{7,15},{8,0},{9,1},... | collective-permute-start | bytes 24584 | tf_op jit(solution)/shard_map/ppermute | solution.py:190
  109.1 6.0 %collective-permute-start.11 = (f32[16,128]{1,0:T(8,128)S(1)}, f32[16,128]{1,0:T(8,128)S(1)}, u32[]{:S(2)}, u32[]{:S(2)}) collective-permute-start(f32[16,128]{1,0:T(8,128)S(1)} %get-tuple-element.26), channel_id=1, source_target_pairs={{0,12},{1,13},{2,14},{3,15},{4,8},{5,9},{6,10},{7,11},{8,4},{9,5},... | collective-permute-start | bytes 24584 | tf_op jit(solution)/shard_map/ppermute | solution.py:190
  115.1 0.0 collective-permute-done.9
  115.1 1.4 %collective-permute-done.10 = f32[16,128]{1,0:T(8,128)S(1)} collective-permute-done((f32[16,128]{1,0:T(8,128)S(1)}, f32[16,128]{1,0:T(8,128)S(1)}, u32[]{:S(2)}, u32[]{:S(2)}) %collective-permute-start.10) | collective-permute-done | bytes 8224 | tf_op jit(solution)/shard_map/ppermute | solution.py:190
  116.5 0.2 collective-permute-done.11
  116.7 0.6 add_convert_fusion
  (2 shorter events, 0.1 us)
Async XLA Ops:
  0.0 1.1 copy-start
  1.1 1.0 copy-start.1
  2.1 5.5 %copy-start.3 = (bf16[16,128]{1,0:T(8,128)(2,1)S(1)}, bf16[16,128]{1,0:T(8,128)(2,1)}, u32[]{:S(2)}) copy-start(bf16[16,128]{1,0:T(8,128)(2,1)} %refs_0_.1) | copy-start | bytes 12292
  2.1 32.9 %copy-start.2 = (s32[16,8]{0,1:T(8,128)S(1)}, s32[16,8]{0,1:T(8,128)}, u32[]{:S(2)}) copy-start(s32[16,8]{0,1:T(8,128)} %param.6) | copy-start | bytes 1540
  2.5 49.4 %collective-permute-start.4 = (bf16[2,288,512]{2,1,0:T(8,128)(2,1)S(1)}, bf16[2,288,512]{2,1,0:T(8,128)(2,1)S(1)}, u32[]{:S(2)}, u32[]{:S(2)}) collective-permute-start(bf16[2,288,512]{2,1,0:T(8,128)(2,1)S(1)} %get-tuple-element.18), channel_id=1, source_target_pairs={{0,2},{1,3},{2,0},{3,1},{4,6},{5,7},{6,4},{7,5},{8,10},{9,11},{10,... | collective-permute-start | bytes 1769480 | tf_op jit(solution)/shard_map/ppermute | solution.py:190
  7.7 25.1 %collective-permute-start.1 = (bf16[16,128]{1,0:T(8,128)(2,1)S(1)}, bf16[16,128]{1,0:T(8,128)(2,1)S(1)}, u32[]{:S(2)}, u32[]{:S(2)}) collective-permute-start(bf16[16,128]{1,0:T(8,128)(2,1)S(1)} %copy-done.3), channel_id=1, source_target_pairs={{0,8},{1,9},{2,10},{3,11},{4,12},{5,13},{6,14},{7,15},{8,0},{9,1},... | collective-permute-start | bytes 12296 | tf_op jit(solution)/shard_map/ppermute | solution.py:190
  21.3 11.5 %collective-permute-start = (bf16[16,128]{1,0:T(8,128)(2,1)S(1)}, bf16[16,128]{1,0:T(8,128)(2,1)S(1)}, u32[]{:S(2)}, u32[]{:S(2)}) collective-permute-start(bf16[16,128]{1,0:T(8,128)(2,1)S(1)} %copy-done.3), channel_id=1, source_target_pairs={{0,4},{1,5},{2,6},{3,7},{4,0},{5,1},{6,2},{7,3},{8,12},{9,13},{10,... | collective-permute-start | bytes 12296 | tf_op jit(solution)/shard_map/ppermute | solution.py:190
  27.4 7.6 %collective-permute-start.2 = (bf16[16,128]{1,0:T(8,128)(2,1)S(1)}, bf16[16,128]{1,0:T(8,128)(2,1)S(1)}, u32[]{:S(2)}, u32[]{:S(2)}) collective-permute-start(bf16[16,128]{1,0:T(8,128)(2,1)S(1)} %copy-done.3), channel_id=1, source_target_pairs={{0,12},{1,13},{2,14},{3,15},{4,8},{5,9},{6,10},{7,11},{8,4},{9,5},... | collective-permute-start | bytes 12296 | tf_op jit(solution)/shard_map/ppermute | solution.py:190
  36.4 28.6 %all-to-all-start = ((bf16[64,24,128]{2,1,0:T(8,128)(2,1)}), bf16[64,24,128]{2,1,0:T(8,128)(2,1)S(1)}, u32[]{:S(2)}, u32[]{:S(2)}) async-start(bf16[64,24,128]{2,1,0:T(8,128)(2,1)} %bitcast.2), calls=%async_computation | async-start | bytes 786432 | tf_op jit(solution)/shard_map/all_to_all | solution.py:194
  49.9 4.4 %collective-permute-start.3 = (bf16[288,512]{1,0:T(8,128)(2,1)S(1)}, bf16[288,512]{1,0:T(8,128)(2,1)S(1)}, u32[]{:S(2)}, u32[]{:S(2)}) collective-permute-start(bf16[288,512]{1,0:T(8,128)(2,1)S(1)} %get-tuple-element.17), channel_id=1, source_target_pairs={{0,1},{1,0},{2,3},{3,2},{4,5},{5,4},{6,7},{7,6},{8,9},{9,8},{10,11... | collective-permute-start | bytes 884744 | tf_op jit(solution)/shard_map/ppermute | solution.py:190
  51.9 13.1 %collective-permute-start.5 = (bf16[288,512]{1,0:T(8,128)(2,1)S(1)}, bf16[288,512]{1,0:T(8,128)(2,1)S(1)}, u32[]{:S(2)}, u32[]{:S(2)}) collective-permute-start(bf16[288,512]{1,0:T(8,128)(2,1)S(1)} %slice_bitcast_fusion), channel_id=1, source_target_pairs={{0,1},{1,0},{2,3},{3,2},{4,5},{5,4},{6,7},{7,6},{8,9},{9,8},{10,11... | collective-permute-start | bytes 884744 | tf_op jit(solution)/shard_map/ppermute | solution.py:190
  65.7 3.3 %collective-permute-start.6 = (bf16[2,96,384]{2,1,0:T(8,128)(2,1)S(1)}, bf16[2,96,384]{2,1,0:T(8,128)(2,1)S(1)}, u32[]{:S(2)}, u32[]{:S(2)}) collective-permute-start(bf16[2,96,384]{2,1,0:T(8,128)(2,1)S(1)} %get-tuple-element.20), channel_id=1, source_target_pairs={{0,1},{1,0},{2,3},{3,2},{4,5},{5,4},{6,7},{7,6},{8,9},{9,8},{10,11... | collective-permute-start | bytes 442376 | tf_op jit(solution)/shard_map/ppermute | solution.py:190
  69.0 7.8 %collective-permute-start.7 = (bf16[2,96,384]{2,1,0:T(8,128)(2,1)S(1)}, bf16[2,96,384]{2,1,0:T(8,128)(2,1)S(1)}, u32[]{:S(2)}, u32[]{:S(2)}) collective-permute-start(bf16[2,96,384]{2,1,0:T(8,128)(2,1)S(1)} %get-tuple-element.22), channel_id=1, source_target_pairs={{0,2},{1,3},{2,0},{3,1},{4,6},{5,7},{6,4},{7,5},{8,10},{9,11},{10,... | collective-permute-start | bytes 442376 | tf_op jit(solution)/shard_map/ppermute | solution.py:190
  76.9 3.2 %collective-permute-start.8 = (bf16[2,48,384]{2,1,0:T(8,128)(2,1)S(1)}, bf16[2,48,384]{2,1,0:T(8,128)(2,1)S(1)}, u32[]{:S(2)}, u32[]{:S(2)}) collective-permute-start(bf16[2,48,384]{2,1,0:T(8,128)(2,1)S(1)} %shard_map.59.own_ref), channel_id=1, source_target_pairs={{0,1},{1,0},{2,3},{3,2},{4,5},{5,4},{6,7},{7,6},{8,9},{9,8},{10,11... | collective-permute-start | bytes 221192 | tf_op jit(solution)/shard_map/ppermute | solution.py:190
  80.5 21.9 %copy-start.4 = (f32[16,8]{0,1:T(8,128)S(1)}, f32[16,8]{0,1:T(8,128)}, u32[]{:S(2)}) copy-start(f32[16,8]{0,1:T(8,128)} %param.7) | copy-start | bytes 1540
  102.9 12.2 %collective-permute-start.9 = (f32[16,128]{1,0:T(8,128)S(1)}, f32[16,128]{1,0:T(8,128)S(1)}, u32[]{:S(2)}, u32[]{:S(2)}) collective-permute-start(f32[16,128]{1,0:T(8,128)S(1)} %get-tuple-element.24), channel_id=1, source_target_pairs={{0,4},{1,5},{2,6},{3,7},{4,0},{5,1},{6,2},{7,3},{8,12},{9,13},{10,... | collective-permute-start | bytes 24584 | tf_op jit(solution)/shard_map/ppermute | solution.py:190
  107.1 9.5 %collective-permute-start.10 = (f32[16,128]{1,0:T(8,128)S(1)}, f32[16,128]{1,0:T(8,128)S(1)}, u32[]{:S(2)}, u32[]{:S(2)}) collective-permute-start(f32[16,128]{1,0:T(8,128)S(1)} %get-tuple-element.25), channel_id=1, source_target_pairs={{0,8},{1,9},{2,10},{3,11},{4,12},{5,13},{6,14},{7,15},{8,0},{9,1},... | collective-permute-start | bytes 24584 | tf_op jit(solution)/shard_map/ppermute | solution.py:190
  109.1 7.7 %collective-permute-start.11 = (f32[16,128]{1,0:T(8,128)S(1)}, f32[16,128]{1,0:T(8,128)S(1)}, u32[]{:S(2)}, u32[]{:S(2)}) collective-permute-start(f32[16,128]{1,0:T(8,128)S(1)} %get-tuple-element.26), channel_id=1, source_target_pairs={{0,12},{1,13},{2,14},{3,15},{4,8},{5,9},{6,10},{7,11},{8,4},{9,5},... | collective-permute-start | bytes 24584 | tf_op jit(solution)/shard_map/ppermute | solution.py:190

commit v3 on v2

v3 whole, which is shorter than its diff:
```python
import jax
import jax.numpy as jnp
from jax import lax
from jax.experimental import pallas as pl
from jax.experimental.pallas import tpu as pltpu
from jax.sharding import PartitionSpec as P

LANES = 128
CAPACITY = 3
QUAD = 4
LOCAL = 2
SLOTS = LOCAL * CAPACITY
TILE = 8
VMEM = pl.BlockSpec(memory_space=pltpu.VMEM)
PARAMS = pltpu.CompilerParams(vmem_limit_bytes=48 * 1024 * 1024)


def iota(shape, dim):
    return lax.broadcasted_iota(jnp.int32, shape, dim)


def pair_column(values):
    top, toks = values.shape
    shape = (toks, top, toks)
    picked = jnp.where(iota(shape, 0) == iota(shape, 2), values[None], 0.0)
    return jnp.sum(picked, axis=2, keepdims=True)


def slot_rows(ids, owners):
    top, toks = ids.shape
    pairs = top * toks
    down = pair_column(ids.astype(jnp.float32)).reshape(pairs, 1)
    ip, iq = iota((pairs, pairs), 0), iota((pairs, pairs), 1)
    across = jnp.sum(jnp.where(ip == iq, down, 0.0), axis=0, keepdims=True)
    same = down == across
    slot_down = jnp.sum(jnp.where(same & (iq < ip), 1.0, 0.0), axis=1, keepdims=True)
    slot_across = jnp.sum(jnp.where(same & (ip < iq), 1.0, 0.0), axis=0, keepdims=True)

    def row(number, slot):
        number, slot = number.astype(jnp.int32), slot.astype(jnp.int32)
        return (number % LOCAL * CAPACITY + slot) * owners + number // LOCAL

    return row(down, slot_down), row(across, slot_across)


def rows_of(slot, group, groups, owners):
    return pl.ds(group * TILE + slot, owners, stride=groups * TILE)


def pack_kernel(w_in_ref, w_down_ref, keep_ref, core_ref, chip_ref):
    place = lax.rem(lax.axis_index("tensor"), QUAD)
    slices = keep_ref.shape[1] // LANES
    hid = w_down_ref.shape[1]
    for r, out in enumerate((keep_ref, core_ref, chip_ref.at[0], chip_ref.at[1])):
        for j in range(slices):
            owner = QUAD * j + jnp.bitwise_xor(place, r)
            src = pl.ds(pl.multiple_of(owner * LANES, LANES), LANES)
            dst = pl.ds(j * LANES, LANES)
            for e in range(LOCAL):
                for g in range(2):
                    out[pl.ds((2 * e + g) * hid, hid), dst] = w_in_ref[e, g, :, src]
                out[pl.ds((2 * LOCAL + e) * hid, hid), dst] = w_down_ref[e, :, src]


def dispatch_kernel(ids_ref, tok_ref, out_ref, scratch):
    groups = 4
    owners = out_ref.shape[0] // (groups * TILE)
    rows = owners * SLOTS
    toks = tok_ref.shape[0]
    _, across = slot_rows(ids_ref[...], owners)
    pairs = across.shape[1]
    top = pairs // toks
    placing = jnp.where(iota((rows, pairs), 0) == across, 1.0, 0.0).astype(jnp.bfloat16)
    token_of = jnp.where(iota((pairs, toks), 0) // top == iota((pairs, toks), 1), 1.0, 0.0)
    table = jnp.dot(
        placing, token_of.astype(jnp.bfloat16), preferred_element_type=jnp.float32
    ).astype(jnp.bfloat16)
    values = jnp.dot(table, tok_ref[...], preferred_element_type=jnp.float32)
    blank = jnp.zeros((owners, LANES), jnp.float32)
    for r in range(TILE):
        part = values[r * owners : (r + 1) * owners] if r < SLOTS else blank
        for m in range(groups):
            scratch[rows_of(r, m, groups, owners), :] = part
    out_ref[...] = scratch[...].astype(jnp.bfloat16)


def up_kernel(x_ref, w0_ref, w1_ref, w23_ref, w3_ref, own_ref, send_ref, scratch):
    groups = w0_ref.shape[1] // LANES
    owners = x_ref.shape[0] // (groups * TILE)
    scratch[...] = x_ref[...].astype(jnp.float32)
    x = jnp.concatenate(
        [
            jnp.concatenate(
                [scratch[rows_of(r, m, groups, owners), :] for r in range(SLOTS)], axis=0
            ).astype(jnp.bfloat16)
            for m in range(groups)
        ],
        axis=1,
    )
    rows = x.shape[0]
    hid = w0_ref.shape[0] // (3 * LOCAL)
    first = iota((2 * hid, rows), 1) < rows // LOCAL
    for r, w_ref in enumerate((w0_ref, w1_ref, w23_ref.at[0], w3_ref)):
        both = lax.dot_general(
            w_ref[pl.ds(0, 4 * hid), :],
            x,
            (((1,), (1,)), ((), ())),
            preferred_element_type=jnp.float32,
        )
        part = jnp.where(first, both[: 2 * hid], both[2 * hid :])
        if r % 2:
            send_ref[r // 2] = part.astype(jnp.bfloat16)
        else:
            own_ref[r // 2] = part


def add_kernel(own_ref, got_ref, sum_ref, send_ref):
    total = own_ref[...] + got_ref[...].astype(jnp.float32)
    sum_ref[...] = total
    send_ref[...] = total.astype(jnp.bfloat16)


def act_kernel(own_ref, got_ref, out_ref):
    hid = out_ref.shape[1]
    for r in range(2):
        pre = own_ref[r] + got_ref[1 - r].astype(jnp.float32)
        gate, up = pre[:hid], pre[hid:]
        out_ref[r] = (gate / (1.0 + jnp.exp(-gate)) * up).astype(jnp.bfloat16)


def down_kernel(own_ref, got_ref, w0_ref, w1_ref, w23_ref, w3_ref, out_ref, scratch):
    groups = w0_ref.shape[1] // LANES
    hid = w0_ref.shape[0] // (3 * LOCAL)
    rows = own_ref.shape[2]
    owners = rows // SLOTS
    first = iota((hid, rows), 1) < rows // LOCAL
    values, weights = [], []
    for r, w_ref in enumerate((w0_ref, w1_ref, w23_ref.at[0], w3_ref)):
        hidden = (got_ref if r % 2 else own_ref)[r // 2].astype(jnp.float32)
        values += [jnp.where(first, hidden, 0.0), jnp.where(first, 0.0, hidden)]
        weights.append(w_ref[pl.ds(4 * hid, 2 * hid), :])
    values = jnp.concatenate(values, axis=0).T.astype(jnp.bfloat16)
    weights = jnp.concatenate(weights, axis=0)
    out = jnp.dot(values, weights, preferred_element_type=jnp.float32)
    blank = jnp.zeros((owners, LANES), jnp.float32)
    for m in range(groups):
        for r in range(TILE):
            part = blank
            if r < SLOTS:
                part = out[r * owners : (r + 1) * owners, m * LANES : (m + 1) * LANES]
            scratch[rows_of(r, m, groups, owners), :] = part
    out_ref[...] = scratch[...].astype(jnp.bfloat16)


def combine_kernel(ids_ref, gates_ref, x_ref, out_ref, scratch):
    groups = 4
    owners = x_ref.shape[0] // (groups * TILE)
    top, toks = ids_ref.shape
    down, _ = slot_rows(ids_ref[...], owners)
    scratch[...] = x_ref[...].astype(jnp.float32)
    values = jnp.concatenate(
        [
            sum(scratch[rows_of(r, m, groups, owners), :] for m in range(groups))
            for r in range(SLOTS)
        ],
        axis=0,
    ).astype(jnp.bfloat16)
    rows = values.shape[0]
    picking = jnp.where(down == iota((top * toks, rows), 1), 1.0, 0.0).astype(jnp.bfloat16)
    picked = jnp.dot(picking, values, preferred_element_type=jnp.float32)
    gates = gates_ref[...]
    weights = pair_column(gates / jnp.sum(gates, axis=0, keepdims=True))
    mixed = jnp.sum(picked.reshape(toks, top, LANES) * weights, axis=1)
    out_ref[...] = mixed.astype(jnp.bfloat16)


def call(kernel, shapes, args, scratch=()):
    return pl.pallas_call(
        kernel,
        out_shape=shapes,
        in_specs=[VMEM] * len(args),
        out_specs=jax.tree.map(lambda _: VMEM, shapes),
        scratch_shapes=list(scratch),
        compiler_params=PARAMS,
    )(*args)


def shards(tokens, expert_ids, gate_scores, w_in, w_down):
    n_expert, n_tensor = lax.axis_size("expert"), lax.axis_size("tensor")
    groups = n_tensor // QUAD
    toks = tokens.shape[0]
    _, _, hid, _ = w_in.shape
    rows = n_expert * SLOTS
    ids, gates = expert_ids.T, gate_scores.T
    peers = [
        [e * n_tensor + QUAD * m + q for e in range(n_expert) for m in range(groups)]
        for q in range(QUAD)
    ]
    held = n_expert * groups * TILE

    def bf16(*shape):
        return jax.ShapeDtypeStruct(shape, jnp.bfloat16)

    def f32(*shape):
        return jax.ShapeDtypeStruct(shape, jnp.float32)

    def exchange(value, r):
        return lax.ppermute(value, "tensor", [(i, i ^ r) for i in range(n_tensor)])

    def deal(value):
        value = value.reshape(n_expert * groups, TILE, LANES)
        value = lax.all_to_all(
            value, ("expert", "tensor"), 0, 0, tiled=True, axis_index_groups=peers
        )
        return value.reshape(held, LANES)

    part = bf16(3 * LOCAL * hid, groups * LANES)
    keep, core, chip = call(
        pack_kernel, [part, part, bf16(2, *part.shape)], (w_in, w_down)
    )
    chip = exchange(chip, 2)
    weights = (keep, exchange(core, 1), chip, exchange(chip[1], 1))

    wide = pltpu.VMEM((held, LANES), jnp.float32)
    arrived = deal(call(dispatch_kernel, bf16(held, LANES), (ids, tokens), [wide]))
    pair = (2, 2 * hid, rows)
    own, send = call(up_kernel, [f32(*pair), bf16(*pair)], (arrived, *weights), [wide])
    own, send = call(add_kernel, [f32(*pair), bf16(*pair)], (own, exchange(send, 1)))
    hidden = call(act_kernel, bf16(2, hid, rows), (own, exchange(send, 2)))
    out = call(
        down_kernel, bf16(held, LANES), (hidden, exchange(hidden, 1), *weights), [wide]
    )
    return call(combine_kernel, bf16(toks, LANES), (ids, gates, deal(out)), [wide])


def solution(mesh):
    in_specs = (
        P("expert", "tensor"),
        P("expert", None),
        P("expert", None),
        P("expert", None, "tensor", None),
        P("expert", "tensor", None),
    )
    out_specs = P("expert", "tensor")
    return jax.shard_map(shards, mesh=mesh, in_specs=in_specs, out_specs=out_specs, check_vma=False)
```

time: 118 us -> 110 us (0.932)
  starting transfers between devices: 62.7 us -> 44.7 us
  blocking collectives: 21.9 us -> 31.2 us
  Pallas kernels: 3.32 us -> 5.74 us
    ppermute x12 -> x6, starting transfers between devices: 49.2 us -> 15.5 us  [exchange(): return lax.ppermute(value, 'tensor', [(i, i ^ r) for i in range(n_tensor)])]
    all_to_all x1, starting transfers between devices: 13.5 us -> 29.2 us  [deal(): lax.all_to_all(value, ('expert', 'tensor'), 0, 0, tiled=True, axis_index_...]
    all_to_all x1, blocking collectives: 21.9 us -> 31.2 us  [deal(): lax.all_to_all(value, ('expert', 'tensor'), 0, 0, tiled=True, axis_index_...]
    ppermute x12 -> x6, waiting for transfers between devices: 15.7 us -> 9.35 us  [exchange(): return lax.ppermute(value, 'tensor', [(i, i ^ r) for i in range(n_tensor)])]
    all_to_all x1, waiting for transfers between devices: 10.7 us -> 16.6 us  [deal(): lax.all_to_all(value, ('expert', 'tensor'), 0, 0, tiled=True, axis_index_...]
    pallas_call x7, Pallas kernels: 3.32 us -> 5.74 us  [call(): pl.pallas_call(kernel, out_shape=shapes, in_specs=[VMEM] * len(args), out...]
  transfers between devices with their start and end apart: 13 -> 7, of which waited for: 8 -> 5; matrix products, arithmetic and copies ran while one was open for 0% -> 0% of each run, Pallas kernels for 1% -> 2%
where the time goes in v3:
time: 110 us
  starting transfers between devices  44.7 us (41%)
  blocking collectives  31.2 us (28%)
  waiting for transfers between devices  25.9 us (24%)
  Pallas kernels  5.74 us (5%)
  local copies, waits for them, and re-layouts  2.16 us (2%)
    all_to_all x1, blocking collectives, deal(): lax.all_to_all(value, ('expert', 'tensor'), 0, 0, tiled=True, axis_index_...  31.2 us
    all_to_all x1, starting transfers between devices, deal(): lax.all_to_all(value, ('expert', 'tensor'), 0, 0, tiled=True, axis_index_...  29.2 us
    all_to_all x1, waiting for transfers between devices, deal(): lax.all_to_all(value, ('expert', 'tensor'), 0, 0, tiled=True, axis_index_...  16.6 us
    ppermute x6, starting transfers between devices, exchange(): return lax.ppermute(value, 'tensor', [(i, i ^ r) for i in range(n_tensor)])  15.5 us
    ppermute x6, waiting for transfers between devices, exchange(): return lax.ppermute(value, 'tensor', [(i, i ^ r) for i in range(n_tensor)])  9.35 us
    pallas_call x7, Pallas kernels, call(): pl.pallas_call(kernel, out_shape=shapes, in_specs=[VMEM] * len(args), out...  5.74 us
  transfers between devices with their start and end apart: 7, of which 5 were waited for; matrix products, arithmetic and copies ran while one was open for 0% of the time, Pallas kernels for 2%

profile of v3, /device:TPU:4, one launch (start us, length us, event | category | flops | bytes accessed | tf_op | source)
XLA Modules:
  0.0 109.9 jit_solution(2634494202057700570)
XLA Ops:
  0.0 0.0 copy-start
  0.0 1.1 %copy-done = bf16[2,2,48,2048]{3,2,1,0:T(8,128)(2,1)S(1)} copy-done((bf16[2,2,48,2048]{3,2,1,0:T(8,128)(2,1)S(1)}, bf16[2,2,48,2048]{3,2,1,0:T(8,128)(2,1)}, u32[]{:S(2)}) %copy-start) | copy-done | bytes 786456
  1.1 0.0 copy-start.1
  1.1 1.0 copy-done.1
  2.1 0.0 copy-start.2
  2.1 0.0 copy-start.3
  2.1 0.3 shard_map.56
  2.5 5.2 %collective-permute-start.1 = (bf16[2,288,512]{2,1,0:T(8,128)(2,1)S(1)}, bf16[2,288,512]{2,1,0:T(8,128)(2,1)S(1)}, u32[]{:S(2)}, u32[]{:S(2)}) collective-permute-start(bf16[2,288,512]{2,1,0:T(8,128)(2,1)S(1)} %get-tuple-element.14), channel_id=1, source_target_pairs={{0,2},{1,3},{2,0},{3,1},{4,6},{5,7},{6,4},{7,5},{8,10},{9,11},{10,... | collective-permute-start | bytes 1769480 | tf_op jit(solution)/shard_map/ppermute | solution.py:208
  7.6 0.0 copy-done.2
  7.7 0.0 copy-done.3
  7.7 1.9 %shard_map.55 = bf16[2048,128]{1,0:T(8,128)(2,1)} custom-call(s32[8,16]{1,0:T(8,128)S(1)} %bitcast.11, bf16[16,128]{1,0:T(8,128)(2,1)S(1)} %copy-done.3), custom_call_target="tpu_custom_call" | custom-call | tf_op jit(solution)/shard_map/pallas_call | solution.py:178
  9.5 29.2 %all-to-all-start = ((bf16[256,8,128]{2,1,0:T(8,128)(2,1)}), bf16[256,8,128]{2,1,0:T(8,128)(2,1)S(1)}, u32[]{:S(2)}, u32[]{:S(2)}) async-start(bf16[256,8,128]{2,1,0:T(8,128)(2,1)} %bitcast.2), calls=%async_computation | async-start | bytes 1048576 | tf_op jit(solution)/shard_map/all_to_all | solution.py:212
  38.7 1.9 %collective-permute-start = (bf16[288,512]{1,0:T(8,128)(2,1)S(1)}, bf16[288,512]{1,0:T(8,128)(2,1)S(1)}, u32[]{:S(2)}, u32[]{:S(2)}) collective-permute-start(bf16[288,512]{1,0:T(8,128)(2,1)S(1)} %get-tuple-element.13), channel_id=1, source_target_pairs={{0,1},{1,0},{2,3},{3,2},{4,5},{5,4},{6,7},{7,6},{8,9},{9,8},{10,11... | collective-permute-start | bytes 884744 | tf_op jit(solution)/shard_map/ppermute | solution.py:208
  40.6 0.0 collective-permute-done.1.w23_ref
  40.7 2.4 %collective-permute-start.2 = (bf16[288,512]{1,0:T(8,128)(2,1)S(1)}, bf16[288,512]{1,0:T(8,128)(2,1)S(1)}, u32[]{:S(2)}, u32[]{:S(2)}) collective-permute-start(bf16[288,512]{1,0:T(8,128)(2,1)S(1)} %slice_bitcast_fusion), channel_id=1, source_target_pairs={{0,1},{1,0},{2,3},{3,2},{4,5},{5,4},{6,7},{7,6},{8,9},{9,8},{10,11... | collective-permute-start | bytes 884744 | tf_op jit(solution)/shard_map/ppermute | solution.py:208
  43.1 0.0 collective-permute-done.w1_ref
  43.1 1.2 %collective-permute-done.2.w3_ref = bf16[288,512]{1,0:T(8,128)(2,1)S(1)} collective-permute-done((bf16[288,512]{1,0:T(8,128)(2,1)S(1)}, bf16[288,512]{1,0:T(8,128)(2,1)S(1)}, u32[]{:S(2)}, u32[]{:S(2)}) %collective-permute-start.2) | collective-permute-done | bytes 294944 | tf_op jit(solution)/shard_map/ppermute | solution.py:208
  44.3 16.6 %all-to-all-done = bf16[256,8,128]{2,1,0:T(8,128)(2,1)S(1)} async-done(((bf16[256,8,128]{2,1,0:T(8,128)(2,1)}), bf16[256,8,128]{2,1,0:T(8,128)(2,1)S(1)}, u32[]{:S(2)}, u32[]{:S(2)}) %all-to-all-start) | async-done | bytes 524320 | tf_op jit(solution)/shard_map/all_to_all | solution.py:212
  60.9 1.0 shard_map.57
  61.9 1.9 %collective-permute-start.3 = (bf16[2,96,384]{2,1,0:T(8,128)(2,1)S(1)}, bf16[2,96,384]{2,1,0:T(8,128)(2,1)S(1)}, u32[]{:S(2)}, u32[]{:S(2)}) collective-permute-start(bf16[2,96,384]{2,1,0:T(8,128)(2,1)S(1)} %get-tuple-element.16), channel_id=1, source_target_pairs={{0,1},{1,0},{2,3},{3,2},{4,5},{5,4},{6,7},{7,6},{8,9},{9,8},{10,11... | collective-permute-start | bytes 442376 | tf_op jit(solution)/shard_map/ppermute | solution.py:208
  63.9 1.3 %collective-permute-done.3.got_ref = bf16[2,96,384]{2,1,0:T(8,128)(2,1)S(1)} collective-permute-done((bf16[2,96,384]{2,1,0:T(8,128)(2,1)S(1)}, bf16[2,96,384]{2,1,0:T(8,128)(2,1)S(1)}, u32[]{:S(2)}, u32[]{:S(2)}) %collective-permute-start.3) | collective-permute-done | bytes 147488 | tf_op jit(solution)/shard_map/ppermute | solution.py:208
  65.2 2.2 %collective-permute-start.4 = (bf16[2,96,384]{2,1,0:T(8,128)(2,1)S(1)}, bf16[2,96,384]{2,1,0:T(8,128)(2,1)S(1)}, u32[]{:S(2)}, u32[]{:S(2)}) collective-permute-start(bf16[2,96,384]{2,1,0:T(8,128)(2,1)S(1)} %get-tuple-element.18), channel_id=1, source_target_pairs={{0,2},{1,3},{2,0},{3,1},{4,6},{5,7},{6,4},{7,5},{8,10},{9,11},{10,... | collective-permute-start | bytes 442376 | tf_op jit(solution)/shard_map/ppermute | solution.py:208
  67.4 5.6 %collective-permute-done.4.got_ref = bf16[2,96,384]{2,1,0:T(8,128)(2,1)S(1)} collective-permute-done((bf16[2,96,384]{2,1,0:T(8,128)(2,1)S(1)}, bf16[2,96,384]{2,1,0:T(8,128)(2,1)S(1)}, u32[]{:S(2)}, u32[]{:S(2)}) %collective-permute-start.4) | collective-permute-done | bytes 147488 | tf_op jit(solution)/shard_map/ppermute | solution.py:208
  73.0 0.1 shard_map.59.own_ref
  73.1 1.9 %collective-permute-start.5 = (bf16[2,48,384]{2,1,0:T(8,128)(2,1)S(1)}, bf16[2,48,384]{2,1,0:T(8,128)(2,1)S(1)}, u32[]{:S(2)}, u32[]{:S(2)}) collective-permute-start(bf16[2,48,384]{2,1,0:T(8,128)(2,1)S(1)} %shard_map.59.own_ref), channel_id=1, source_target_pairs={{0,1},{1,0},{2,3},{3,2},{4,5},{5,4},{6,7},{7,6},{8,9},{9,8},{10,11... | collective-permute-start | bytes 221192 | tf_op jit(solution)/shard_map/ppermute | solution.py:208
  75.0 1.2 %collective-permute-done.5.got_ref = bf16[2,48,384]{2,1,0:T(8,128)(2,1)S(1)} collective-permute-done((bf16[2,48,384]{2,1,0:T(8,128)(2,1)S(1)}, bf16[2,48,384]{2,1,0:T(8,128)(2,1)S(1)}, u32[]{:S(2)}, u32[]{:S(2)}) %collective-permute-start.5) | collective-permute-done | bytes 73760 | tf_op jit(solution)/shard_map/ppermute | solution.py:208
  76.3 1.1 shard_map.60
  77.4 0.0 copy-start.4
  77.4 31.2 %all_to_all.10 = bf16[256,8,128]{2,1,0:T(8,128)(2,1)S(1)} all-to-all(bf16[256,8,128]{2,1,0:T(8,128)(2,1)S(1)} %bitcast.10), channel_id=1, replica_groups={{0,4,8,12,16,20,24,28,32,36,40,44,48,52,56,60,64,68,72,76,80,84,88,92,9..., dimensions={0} | all-to-all | bytes 1048576 | tf_op jit(solution)/shard_map/all_to_all | solution.py:212
  108.6 0.0 copy-done.4
  108.6 1.3 %shard_map.61 = bf16[16,128]{1,0:T(8,128)(2,1)} custom-call(s32[8,16]{1,0:T(8,128)S(1)} %bitcast.12, f32[8,16]{1,0:T(8,128)S(1)} %bitcast.13, bf16[2048,128]{1,0:T(8,128)(2,1)S(1)} %bitcast.8), custom_call_target="tpu_custom_call" | custom-call | tf_op jit(solution)/shard_map/pallas_call | solution.py:178
  (2 shorter events, 0.1 us)
Async XLA Ops:
  0.0 1.1 %copy-start = (bf16[2,2,48,2048]{3,2,1,0:T(8,128)(2,1)S(1)}, bf16[2,2,48,2048]{3,2,1,0:T(8,128)(2,1)}, u32[]{:S(2)}) copy-start(bf16[2,2,48,2048]{3,2,1,0:T(8,128)(2,1)} %w_in_ref.1) | copy-start | bytes 2359300
  1.1 1.0 copy-start.1
  2.1 5.5 %copy-start.2 = (s32[16,8]{0,1:T(8,128)S(1)}, s32[16,8]{0,1:T(8,128)}, u32[]{:S(2)}) copy-start(s32[16,8]{0,1:T(8,128)} %param.6) | copy-start | bytes 1540
  2.1 5.5 %copy-start.3 = (bf16[16,128]{1,0:T(8,128)(2,1)S(1)}, bf16[16,128]{1,0:T(8,128)(2,1)}, u32[]{:S(2)}) copy-start(bf16[16,128]{1,0:T(8,128)(2,1)} %tok_ref.1) | copy-start | bytes 12292
  2.5 38.2 %collective-permute-start.1 = (bf16[2,288,512]{2,1,0:T(8,128)(2,1)S(1)}, bf16[2,288,512]{2,1,0:T(8,128)(2,1)S(1)}, u32[]{:S(2)}, u32[]{:S(2)}) collective-permute-start(bf16[2,288,512]{2,1,0:T(8,128)(2,1)S(1)} %get-tuple-element.14), channel_id=1, source_target_pairs={{0,2},{1,3},{2,0},{3,1},{4,6},{5,7},{6,4},{7,5},{8,10},{9,11},{10,... | collective-permute-start | bytes 1769480 | tf_op jit(solution)/shard_map/ppermute | solution.py:208
  9.5 51.3 %all-to-all-start = ((bf16[256,8,128]{2,1,0:T(8,128)(2,1)}), bf16[256,8,128]{2,1,0:T(8,128)(2,1)S(1)}, u32[]{:S(2)}, u32[]{:S(2)}) async-start(bf16[256,8,128]{2,1,0:T(8,128)(2,1)} %bitcast.2), calls=%async_computation | async-start | bytes 1048576 | tf_op jit(solution)/shard_map/all_to_all | solution.py:212
  38.7 4.4 %collective-permute-start = (bf16[288,512]{1,0:T(8,128)(2,1)S(1)}, bf16[288,512]{1,0:T(8,128)(2,1)S(1)}, u32[]{:S(2)}, u32[]{:S(2)}) collective-permute-start(bf16[288,512]{1,0:T(8,128)(2,1)S(1)} %get-tuple-element.13), channel_id=1, source_target_pairs={{0,1},{1,0},{2,3},{3,2},{4,5},{5,4},{6,7},{7,6},{8,9},{9,8},{10,11... | collective-permute-start | bytes 884744 | tf_op jit(solution)/shard_map/ppermute | solution.py:208
  40.7 3.6 %collective-permute-start.2 = (bf16[288,512]{1,0:T(8,128)(2,1)S(1)}, bf16[288,512]{1,0:T(8,128)(2,1)S(1)}, u32[]{:S(2)}, u32[]{:S(2)}) collective-permute-start(bf16[288,512]{1,0:T(8,128)(2,1)S(1)} %slice_bitcast_fusion), channel_id=1, source_target_pairs={{0,1},{1,0},{2,3},{3,2},{4,5},{5,4},{6,7},{7,6},{8,9},{9,8},{10,11... | collective-permute-start | bytes 884744 | tf_op jit(solution)/shard_map/ppermute | solution.py:208
  61.9 3.3 %collective-permute-start.3 = (bf16[2,96,384]{2,1,0:T(8,128)(2,1)S(1)}, bf16[2,96,384]{2,1,0:T(8,128)(2,1)S(1)}, u32[]{:S(2)}, u32[]{:S(2)}) collective-permute-start(bf16[2,96,384]{2,1,0:T(8,128)(2,1)S(1)} %get-tuple-element.16), channel_id=1, source_target_pairs={{0,1},{1,0},{2,3},{3,2},{4,5},{5,4},{6,7},{7,6},{8,9},{9,8},{10,11... | collective-permute-start | bytes 442376 | tf_op jit(solution)/shard_map/ppermute | solution.py:208
  65.2 7.8 %collective-permute-start.4 = (bf16[2,96,384]{2,1,0:T(8,128)(2,1)S(1)}, bf16[2,96,384]{2,1,0:T(8,128)(2,1)S(1)}, u32[]{:S(2)}, u32[]{:S(2)}) collective-permute-start(bf16[2,96,384]{2,1,0:T(8,128)(2,1)S(1)} %get-tuple-element.18), channel_id=1, source_target_pairs={{0,2},{1,3},{2,0},{3,1},{4,6},{5,7},{6,4},{7,5},{8,10},{9,11},{10,... | collective-permute-start | bytes 442376 | tf_op jit(solution)/shard_map/ppermute | solution.py:208
  73.1 3.2 %collective-permute-start.5 = (bf16[2,48,384]{2,1,0:T(8,128)(2,1)S(1)}, bf16[2,48,384]{2,1,0:T(8,128)(2,1)S(1)}, u32[]{:S(2)}, u32[]{:S(2)}) collective-permute-start(bf16[2,48,384]{2,1,0:T(8,128)(2,1)S(1)} %shard_map.59.own_ref), channel_id=1, source_target_pairs={{0,1},{1,0},{2,3},{3,2},{4,5},{5,4},{6,7},{7,6},{8,9},{9,8},{10,11... | collective-permute-start | bytes 221192 | tf_op jit(solution)/shard_map/ppermute | solution.py:208
  77.4 31.2 %copy-start.4 = (f32[16,8]{0,1:T(8,128)S(1)}, f32[16,8]{0,1:T(8,128)}, u32[]{:S(2)}) copy-start(f32[16,8]{0,1:T(8,128)} %param.7) | copy-start | bytes 1540

commit v4 on v3

v4 whole, which is shorter than its diff:
```python
import jax
import jax.numpy as jnp
from jax import lax
from jax.experimental import pallas as pl
from jax.experimental.pallas import tpu as pltpu
from jax.sharding import PartitionSpec as P

LANES = 128
CAPACITY = 3
QUAD = 4
LOCAL = 2
SLOTS = LOCAL * CAPACITY
TILE = 8
VMEM = pl.BlockSpec(memory_space=pltpu.VMEM)
PARAMS = pltpu.CompilerParams(vmem_limit_bytes=48 * 1024 * 1024)


def iota(shape, dim):
    return lax.broadcasted_iota(jnp.int32, shape, dim)


def pair_column(values):
    top, toks = values.shape
    shape = (toks, top, toks)
    picked = jnp.where(iota(shape, 0) == iota(shape, 2), values[None], 0.0)
    return jnp.sum(picked, axis=2, keepdims=True)


def slot_rows(ids):
    top, toks = ids.shape
    pairs = top * toks
    down = pair_column(ids.astype(jnp.float32)).reshape(pairs, 1)
    ip, iq = iota((pairs, pairs), 0), iota((pairs, pairs), 1)
    across = jnp.sum(jnp.where(ip == iq, down, 0.0), axis=0, keepdims=True)
    same = down == across
    slot_down = jnp.sum(jnp.where(same & (iq < ip), 1.0, 0.0), axis=1, keepdims=True)
    slot_across = jnp.sum(jnp.where(same & (ip < iq), 1.0, 0.0), axis=0, keepdims=True)

    def row(number, slot):
        number, slot = number.astype(jnp.int32), slot.astype(jnp.int32)
        return number // LOCAL * TILE + number % LOCAL * CAPACITY + slot

    return row(down, slot_down), row(across, slot_across)


def dense_row(shape, dim, owners):
    row = iota(shape, dim)
    slot = row % TILE
    return jnp.where(slot < SLOTS, slot * owners + row // TILE, -1)


def onehot(found):
    return jnp.where(found, 1.0, 0.0).astype(jnp.bfloat16)


def pack_kernel(w_in_ref, w_down_ref, *out_refs):
    place = lax.rem(lax.axis_index("tensor"), QUAD)
    slices = out_refs[0].shape[1] // LANES
    hid = w_down_ref.shape[1]
    for r, out in enumerate(out_refs):
        for j in range(slices):
            owner = QUAD * j + jnp.bitwise_xor(place, r)
            src = pl.ds(pl.multiple_of(owner * LANES, LANES), LANES)
            dst = pl.ds(j * LANES, LANES)
            for e in range(LOCAL):
                for g in range(2):
                    out[pl.ds((2 * e + g) * hid, hid), dst] = w_in_ref[e, g, :, src]
                out[pl.ds((2 * LOCAL + e) * hid, hid), dst] = w_down_ref[e, :, src]


def dispatch_kernel(ids_ref, tok_ref, out_ref):
    owners, groups = out_ref.shape[:2]
    toks = tok_ref.shape[0]
    _, across = slot_rows(ids_ref[...])
    pairs = across.shape[1]
    token_of = onehot(iota((pairs, toks), 0) // (pairs // toks) == iota((pairs, toks), 1))
    values = jnp.dot(token_of, tok_ref[...], preferred_element_type=jnp.float32)
    placing = onehot(iota((owners * TILE, pairs), 0) == across)
    values = jnp.dot(placing, values.astype(jnp.bfloat16), preferred_element_type=jnp.float32)
    values = values.reshape(owners, TILE, LANES).astype(jnp.bfloat16)
    for m in range(groups):
        out_ref[:, m] = values


def up_kernel(x_ref, w0_ref, w1_ref, w2_ref, w3_ref, own_ref, send_ref):
    owners, groups = x_ref.shape[:2]
    held = owners * TILE
    rows = own_ref.shape[2]
    x = jnp.concatenate(
        [
            x_ref[:, m].astype(jnp.float32).reshape(held, LANES).astype(jnp.bfloat16)
            for m in range(groups)
        ],
        axis=1,
    )
    picking = onehot(iota((rows, held), 0) == dense_row((1, held), 1, owners))
    x = jnp.dot(picking, x, preferred_element_type=jnp.float32).astype(jnp.bfloat16)
    hid = w0_ref.shape[0] // (3 * LOCAL)
    first = iota((2 * hid, rows), 1) < rows // LOCAL
    for r, w_ref in enumerate((w0_ref, w1_ref, w2_ref, w3_ref)):
        both = lax.dot_general(
            w_ref[pl.ds(0, 4 * hid), :],
            x,
            (((1,), (1,)), ((), ())),
            preferred_element_type=jnp.float32,
        )
        part = jnp.where(first, both[: 2 * hid], both[2 * hid :])
        if r % 2:
            send_ref[r // 2] = part.astype(jnp.bfloat16)
        else:
            own_ref[r // 2] = part


def add_kernel(own_ref, got_ref, sum_ref, send_ref):
    total = own_ref[...] + got_ref[...].astype(jnp.float32)
    sum_ref[...] = total
    send_ref[...] = total.astype(jnp.bfloat16)


def act_kernel(own_ref, got_ref, out_ref):
    hid = out_ref.shape[1]
    for r in range(2):
        pre = own_ref[r] + got_ref[1 - r].astype(jnp.float32)
        gate, up = pre[:hid], pre[hid:]
        out_ref[r] = (gate / (1.0 + jnp.exp(-gate)) * up).astype(jnp.bfloat16)


def down_kernel(own_ref, got_ref, w0_ref, w1_ref, w2_ref, w3_ref, out_ref):
    owners, groups = out_ref.shape[:2]
    hid, rows = own_ref.shape[1:]
    first = iota((hid, rows), 1) < rows // LOCAL
    values, weights = [], []
    for r, w_ref in enumerate((w0_ref, w1_ref, w2_ref, w3_ref)):
        hidden = (got_ref if r % 2 else own_ref)[r // 2].astype(jnp.float32)
        values += [jnp.where(first, hidden, 0.0), jnp.where(first, 0.0, hidden)]
        weights.append(w_ref[pl.ds(4 * hid, 2 * hid), :])
    values = jnp.concatenate(values, axis=0).astype(jnp.bfloat16)
    weights = jnp.concatenate(weights, axis=0)
    held = owners * TILE
    placing = onehot(iota((held, rows), 1) == dense_row((held, 1), 0, owners))
    values = lax.dot_general(
        placing, values, (((1,), (1,)), ((), ())), preferred_element_type=jnp.float32
    ).astype(jnp.bfloat16)
    out = jnp.dot(values, weights, preferred_element_type=jnp.float32)
    for m in range(groups):
        part = out[:, m * LANES : (m + 1) * LANES]
        out_ref[:, m] = part.reshape(owners, TILE, LANES).astype(jnp.bfloat16)


def combine_kernel(ids_ref, gates_ref, x_ref, out_ref):
    owners, groups = x_ref.shape[:2]
    top, toks = ids_ref.shape
    held = owners * TILE
    down, _ = slot_rows(ids_ref[...])
    values = x_ref[:, 0].astype(jnp.float32)
    for m in range(1, groups):
        values = values + x_ref[:, m].astype(jnp.float32)
    values = values.reshape(held, LANES).astype(jnp.bfloat16)
    picking = onehot(down == iota((top * toks, held), 1))
    picked = jnp.dot(picking, values, preferred_element_type=jnp.float32)
    gates = gates_ref[...]
    weights = pair_column(gates / jnp.sum(gates, axis=0, keepdims=True))
    mixed = jnp.sum(picked.reshape(toks, top, LANES) * weights, axis=1)
    out_ref[...] = mixed.astype(jnp.bfloat16)


def call(kernel, shapes, args):
    return pl.pallas_call(
        kernel,
        out_shape=shapes,
        in_specs=[VMEM] * len(args),
        out_specs=jax.tree.map(lambda _: VMEM, shapes),
        compiler_params=PARAMS,
    )(*args)


def shards(tokens, expert_ids, gate_scores, w_in, w_down):
    n_expert, n_tensor = lax.axis_size("expert"), lax.axis_size("tensor")
    groups = n_tensor // QUAD
    toks = tokens.shape[0]
    _, _, hid, _ = w_in.shape
    rows = n_expert * SLOTS
    ids, gates = expert_ids.T, gate_scores.T
    peers = [
        [e * n_tensor + QUAD * m + q for e in range(n_expert) for m in range(groups)]
        for q in range(QUAD)
    ]
    held = (n_expert, groups, TILE, LANES)

    def bf16(*shape):
        return jax.ShapeDtypeStruct(shape, jnp.bfloat16)

    def f32(*shape):
        return jax.ShapeDtypeStruct(shape, jnp.float32)

    def exchange(value, r):
        return lax.ppermute(value, "tensor", [(i, i ^ r) for i in range(n_tensor)])

    def deal(value):
        value = value.reshape(n_expert * groups, TILE, LANES)
        value = lax.all_to_all(
            value, ("expert", "tensor"), 0, 0, tiled=True, axis_index_groups=peers
        )
        return value.reshape(held)

    packed = call(
        pack_kernel, [bf16(3 * LOCAL * hid, groups * LANES)] * QUAD, (w_in, w_down)
    )
    moved = {r: exchange(packed[r], r) for r in (2, 3, 1)}
    weights = [packed[0]] + [moved[r] for r in range(1, QUAD)]

    arrived = deal(call(dispatch_kernel, bf16(*held), (ids, tokens)))
    pair = (2, 2 * hid, rows)
    own, send = call(up_kernel, [f32(*pair), bf16(*pair)], (arrived, *weights))
    own, send = call(add_kernel, [f32(*pair), bf16(*pair)], (own, exchange(send, 1)))
    hidden = call(act_kernel, bf16(2, hid, rows), (own, exchange(send, 2)))
    out = call(down_kernel, bf16(*held), (hidden, exchange(hidden, 1), *weights))
    return call(combine_kernel, bf16(toks, LANES), (ids, gates, deal(out)))


def solution(mesh):
    in_specs = (
        P("expert", "tensor"),
        P("expert", None),
        P("expert", None),
        P("expert", None, "tensor", None),
        P("expert", "tensor", None),
    )
    out_specs = P("expert", "tensor")
    return jax.shard_map(shards, mesh=mesh, in_specs=in_specs, out_specs=out_specs, check_vma=False)
```

time: 110 us -> 117 us (1.064)
  blocking collectives: 31.2 us -> 39.1 us
  Pallas kernels: 5.74 us -> 4.26 us
    ppermute x6, waiting for transfers between devices: 9.35 us -> 26.6 us  [exchange(): return lax.ppermute(value, 'tensor', [(i, i ^ r) for i in range(n_tensor)])]
    all_to_all x1, waiting for transfers between devices: 16.6 us -> 0.01 us  [deal(): lax.all_to_all(value, ('expert', 'tensor'), 0, 0, tiled=True, axis_index_...]
    all_to_all x1, blocking collectives: 31.2 us -> 39.1 us  [deal(): lax.all_to_all(value, ('expert', 'tensor'), 0, 0, tiled=True, axis_index_...]
    pallas_call x7, Pallas kernels: 5.74 us -> 4.26 us  [call(): pl.pallas_call(kernel, out_shape=shapes, in_specs=[VMEM] * len(args), out...]
  transfers between devices with their start and end apart: 7 -> 7, of which waited for: 5 -> 5; matrix products, arithmetic and copies ran while one was open for 0% -> 0% of each run, Pallas kernels for 2% -> 0%
where the time goes in v4:
time: 117 us
  starting transfers between devices  45.4 us (39%)
  blocking collectives  39.1 us (33%)
  waiting for transfers between devices  26.6 us (23%)
  Pallas kernels  4.26 us (4%)
  local copies, waits for them, and re-layouts  1.39 us (1%)
    all_to_all x1, blocking collectives, deal(): lax.all_to_all(value, ('expert', 'tensor'), 0, 0, tiled=True, axis_index_...  39.1 us
    all_to_all x1, starting transfers between devices, deal(): lax.all_to_all(value, ('expert', 'tensor'), 0, 0, tiled=True, axis_index_...  30.2 us
    ppermute x6, waiting for transfers between devices, exchange(): return lax.ppermute(value, 'tensor', [(i, i ^ r) for i in range(n_tensor)])  26.6 us
    ppermute x6, starting transfers between devices, exchange(): return lax.ppermute(value, 'tensor', [(i, i ^ r) for i in range(n_tensor)])  15.2 us
    pallas_call x7, Pallas kernels, call(): pl.pallas_call(kernel, out_shape=shapes, in_specs=[VMEM] * len(args), out...  4.26 us
  transfers between devices with their start and end apart: 7, of which 5 were waited for; matrix products, arithmetic and copies ran while one was open for 0% of the time, Pallas kernels for 0%

profile of v4, /device:TPU:4, one launch (start us, length us, event | category | flops | bytes accessed | tf_op | source)
XLA Modules:
  0.0 116.9 jit_solution(13283799758462816258)
XLA Ops:
  0.0 0.0 copy-start.2
  0.0 0.7 copy-done.2
  0.7 0.0 copy-start.4
  0.7 0.7 copy-done.4
  1.4 0.0 copy-start
  1.4 1.1 shard_map.55
  2.5 0.0 copy-start.1
  2.5 30.2 %all-to-all-start = ((bf16[256,8,128]{2,1,0:T(8,128)(2,1)}), bf16[256,8,128]{2,1,0:T(8,128)(2,1)S(1)}, u32[]{:S(2)}, u32[]{:S(2)}) async-start(bf16[256,8,128]{2,1,0:T(8,128)(2,1)} %bitcast.2), calls=%async_computation | async-start | bytes 1048576 | tf_op jit(solution)/shard_map/all_to_all | solution.py:201
  32.7 0.0 copy-done
  32.7 0.0 copy-done.1
  32.7 0.3 shard_map.56
  33.1 1.9 %collective-permute-start = (bf16[288,512]{1,0:T(8,128)(2,1)S(1)}, bf16[288,512]{1,0:T(8,128)(2,1)S(1)}, u32[]{:S(2)}, u32[]{:S(2)}) collective-permute-start(bf16[288,512]{1,0:T(8,128)(2,1)S(1)} %get-tuple-element.14), channel_id=1, source_target_pairs={{0,1},{1,0},{2,3},{3,2},{4,5},{5,4},{6,7},{7,6},{8,9},{9,8},{10,11... | collective-permute-start | bytes 884744 | tf_op jit(solution)/shard_map/ppermute | solution.py:197
  35.0 4.3 %collective-permute-start.1 = (bf16[288,512]{1,0:T(8,128)(2,1)S(1)}, bf16[288,512]{1,0:T(8,128)(2,1)S(1)}, u32[]{:S(2)}, u32[]{:S(2)}) collective-permute-start(bf16[288,512]{1,0:T(8,128)(2,1)S(1)} %get-tuple-element.15), channel_id=1, source_target_pairs={{0,2},{1,3},{2,0},{3,1},{4,6},{5,7},{6,4},{7,5},{8,10},{9,11},{10,... | collective-permute-start | bytes 884744 | tf_op jit(solution)/shard_map/ppermute | solution.py:197
  39.3 2.0 %collective-permute-start.2 = (bf16[288,512]{1,0:T(8,128)(2,1)S(1)}, bf16[288,512]{1,0:T(8,128)(2,1)S(1)}, u32[]{:S(2)}, u32[]{:S(2)}) collective-permute-start(bf16[288,512]{1,0:T(8,128)(2,1)S(1)} %get-tuple-element.16), channel_id=1, source_target_pairs={{0,3},{1,2},{2,1},{3,0},{4,7},{5,6},{6,5},{7,4},{8,11},{9,10},{10,... | collective-permute-start | bytes 884744 | tf_op jit(solution)/shard_map/ppermute | solution.py:197
  41.3 0.0 collective-permute-done.w1_ref
  41.3 13.1 %collective-permute-done.1.w2_ref = bf16[288,512]{1,0:T(8,128)(2,1)S(1)} collective-permute-done((bf16[288,512]{1,0:T(8,128)(2,1)S(1)}, bf16[288,512]{1,0:T(8,128)(2,1)S(1)}, u32[]{:S(2)}, u32[]{:S(2)}) %collective-permute-start.1) | collective-permute-done | bytes 294944 | tf_op jit(solution)/shard_map/ppermute | solution.py:197
  54.4 6.3 %collective-permute-done.2.w3_ref = bf16[288,512]{1,0:T(8,128)(2,1)S(1)} collective-permute-done((bf16[288,512]{1,0:T(8,128)(2,1)S(1)}, bf16[288,512]{1,0:T(8,128)(2,1)S(1)}, u32[]{:S(2)}, u32[]{:S(2)}) %collective-permute-start.2) | collective-permute-done | bytes 294944 | tf_op jit(solution)/shard_map/ppermute | solution.py:197
  60.7 0.0 all-to-all-done
  60.7 1.0 shard_map.57
  61.7 2.0 %collective-permute-start.3 = (bf16[2,96,384]{2,1,0:T(8,128)(2,1)S(1)}, bf16[2,96,384]{2,1,0:T(8,128)(2,1)S(1)}, u32[]{:S(2)}, u32[]{:S(2)}) collective-permute-start(bf16[2,96,384]{2,1,0:T(8,128)(2,1)S(1)} %get-tuple-element.18), channel_id=1, source_target_pairs={{0,1},{1,0},{2,3},{3,2},{4,5},{5,4},{6,7},{7,6},{8,9},{9,8},{10,11... | collective-permute-start | bytes 442376 | tf_op jit(solution)/shard_map/ppermute | solution.py:197
  63.7 1.2 %collective-permute-done.3.got_ref = bf16[2,96,384]{2,1,0:T(8,128)(2,1)S(1)} collective-permute-done((bf16[2,96,384]{2,1,0:T(8,128)(2,1)S(1)}, bf16[2,96,384]{2,1,0:T(8,128)(2,1)S(1)}, u32[]{:S(2)}, u32[]{:S(2)}) %collective-permute-start.3) | collective-permute-done | bytes 147488 | tf_op jit(solution)/shard_map/ppermute | solution.py:197
  65.0 3.0 %collective-permute-start.4 = (bf16[2,96,384]{2,1,0:T(8,128)(2,1)S(1)}, bf16[2,96,384]{2,1,0:T(8,128)(2,1)S(1)}, u32[]{:S(2)}, u32[]{:S(2)}) collective-permute-start(bf16[2,96,384]{2,1,0:T(8,128)(2,1)S(1)} %get-tuple-element.20), channel_id=1, source_target_pairs={{0,2},{1,3},{2,0},{3,1},{4,6},{5,7},{6,4},{7,5},{8,10},{9,11},{10,... | collective-permute-start | bytes 442376 | tf_op jit(solution)/shard_map/ppermute | solution.py:197
  68.0 4.8 %collective-permute-done.4.got_ref = bf16[2,96,384]{2,1,0:T(8,128)(2,1)S(1)} collective-permute-done((bf16[2,96,384]{2,1,0:T(8,128)(2,1)S(1)}, bf16[2,96,384]{2,1,0:T(8,128)(2,1)S(1)}, u32[]{:S(2)}, u32[]{:S(2)}) %collective-permute-start.4) | collective-permute-done | bytes 147488 | tf_op jit(solution)/shard_map/ppermute | solution.py:197
  72.8 0.1 shard_map.59.own_ref
  72.9 1.9 %collective-permute-start.5 = (bf16[2,48,384]{2,1,0:T(8,128)(2,1)S(1)}, bf16[2,48,384]{2,1,0:T(8,128)(2,1)S(1)}, u32[]{:S(2)}, u32[]{:S(2)}) collective-permute-start(bf16[2,48,384]{2,1,0:T(8,128)(2,1)S(1)} %shard_map.59.own_ref), channel_id=1, source_target_pairs={{0,1},{1,0},{2,3},{3,2},{4,5},{5,4},{6,7},{7,6},{8,9},{9,8},{10,11... | collective-permute-start | bytes 221192 | tf_op jit(solution)/shard_map/ppermute | solution.py:197
  74.8 1.2 %collective-permute-done.5.got_ref = bf16[2,48,384]{2,1,0:T(8,128)(2,1)S(1)} collective-permute-done((bf16[2,48,384]{2,1,0:T(8,128)(2,1)S(1)}, bf16[2,48,384]{2,1,0:T(8,128)(2,1)S(1)}, u32[]{:S(2)}, u32[]{:S(2)}) %collective-permute-start.5) | collective-permute-done | bytes 73760 | tf_op jit(solution)/shard_map/ppermute | solution.py:197
  76.0 0.7 shard_map.60
  76.8 0.0 copy-start.3
  76.8 0.0 copy-start.5
  76.8 39.1 %all_to_all.10 = bf16[256,8,128]{2,1,0:T(8,128)(2,1)S(1)} all-to-all(bf16[256,8,128]{2,1,0:T(8,128)(2,1)S(1)} %bitcast.6), channel_id=1, replica_groups={{0,4,8,12,16,20,24,28,32,36,40,44,48,52,56,60,64,68,72,76,80,84,88,92,9..., dimensions={0} | all-to-all | bytes 1048576 | tf_op jit(solution)/shard_map/all_to_all | solution.py:201
  115.9 0.0 copy-done.3
  115.9 0.0 copy-done.5
  115.9 1.0 shard_map.61
  (1 shorter events, 0.0 us)
Async XLA Ops:
  0.0 0.7 copy-start.2
  0.7 0.7 copy-start.4
  1.4 31.3 %copy-start = (bf16[2,2,48,2048]{3,2,1,0:T(8,128)(2,1)S(1)}, bf16[2,2,48,2048]{3,2,1,0:T(8,128)(2,1)}, u32[]{:S(2)}) copy-start(bf16[2,2,48,2048]{3,2,1,0:T(8,128)(2,1)} %w_in_ref.1) | copy-start | bytes 2359300
  2.5 30.2 %copy-start.1 = (bf16[2,48,2048]{2,1,0:T(8,128)(2,1)S(1)}, bf16[2,48,2048]{2,1,0:T(8,128)(2,1)}, u32[]{:S(2)}) copy-start(bf16[2,48,2048]{2,1,0:T(8,128)(2,1)} %w_down_ref.1) | copy-start | bytes 1179652
  2.5 58.2 %all-to-all-start = ((bf16[256,8,128]{2,1,0:T(8,128)(2,1)}), bf16[256,8,128]{2,1,0:T(8,128)(2,1)S(1)}, u32[]{:S(2)}, u32[]{:S(2)}) async-start(bf16[256,8,128]{2,1,0:T(8,128)(2,1)} %bitcast.2), calls=%async_computation | async-start | bytes 1048576 | tf_op jit(solution)/shard_map/all_to_all | solution.py:201
  33.1 8.3 %collective-permute-start = (bf16[288,512]{1,0:T(8,128)(2,1)S(1)}, bf16[288,512]{1,0:T(8,128)(2,1)S(1)}, u32[]{:S(2)}, u32[]{:S(2)}) collective-permute-start(bf16[288,512]{1,0:T(8,128)(2,1)S(1)} %get-tuple-element.14), channel_id=1, source_target_pairs={{0,1},{1,0},{2,3},{3,2},{4,5},{5,4},{6,7},{7,6},{8,9},{9,8},{10,11... | collective-permute-start | bytes 884744 | tf_op jit(solution)/shard_map/ppermute | solution.py:197
  35.0 19.4 %collective-permute-start.1 = (bf16[288,512]{1,0:T(8,128)(2,1)S(1)}, bf16[288,512]{1,0:T(8,128)(2,1)S(1)}, u32[]{:S(2)}, u32[]{:S(2)}) collective-permute-start(bf16[288,512]{1,0:T(8,128)(2,1)S(1)} %get-tuple-element.15), channel_id=1, source_target_pairs={{0,2},{1,3},{2,0},{3,1},{4,6},{5,7},{6,4},{7,5},{8,10},{9,11},{10,... | collective-permute-start | bytes 884744 | tf_op jit(solution)/shard_map/ppermute | solution.py:197
  39.3 21.4 %collective-permute-start.2 = (bf16[288,512]{1,0:T(8,128)(2,1)S(1)}, bf16[288,512]{1,0:T(8,128)(2,1)S(1)}, u32[]{:S(2)}, u32[]{:S(2)}) collective-permute-start(bf16[288,512]{1,0:T(8,128)(2,1)S(1)} %get-tuple-element.16), channel_id=1, source_target_pairs={{0,3},{1,2},{2,1},{3,0},{4,7},{5,6},{6,5},{7,4},{8,11},{9,10},{10,... | collective-permute-start | bytes 884744 | tf_op jit(solution)/shard_map/ppermute | solution.py:197
  61.7 3.3 %collective-permute-start.3 = (bf16[2,96,384]{2,1,0:T(8,128)(2,1)S(1)}, bf16[2,96,384]{2,1,0:T(8,128)(2,1)S(1)}, u32[]{:S(2)}, u32[]{:S(2)}) collective-permute-start(bf16[2,96,384]{2,1,0:T(8,128)(2,1)S(1)} %get-tuple-element.18), channel_id=1, source_target_pairs={{0,1},{1,0},{2,3},{3,2},{4,5},{5,4},{6,7},{7,6},{8,9},{9,8},{10,11... | collective-permute-start | bytes 442376 | tf_op jit(solution)/shard_map/ppermute | solution.py:197
  65.0 7.8 %collective-permute-start.4 = (bf16[2,96,384]{2,1,0:T(8,128)(2,1)S(1)}, bf16[2,96,384]{2,1,0:T(8,128)(2,1)S(1)}, u32[]{:S(2)}, u32[]{:S(2)}) collective-permute-start(bf16[2,96,384]{2,1,0:T(8,128)(2,1)S(1)} %get-tuple-element.20), channel_id=1, source_target_pairs={{0,2},{1,3},{2,0},{3,1},{4,6},{5,7},{6,4},{7,5},{8,10},{9,11},{10,... | collective-permute-start | bytes 442376 | tf_op jit(solution)/shard_map/ppermute | solution.py:197
  72.9 3.2 %collective-permute-start.5 = (bf16[2,48,384]{2,1,0:T(8,128)(2,1)S(1)}, bf16[2,48,384]{2,1,0:T(8,128)(2,1)S(1)}, u32[]{:S(2)}, u32[]{:S(2)}) collective-permute-start(bf16[2,48,384]{2,1,0:T(8,128)(2,1)S(1)} %shard_map.59.own_ref), channel_id=1, source_target_pairs={{0,1},{1,0},{2,3},{3,2},{4,5},{5,4},{6,7},{7,6},{8,9},{9,8},{10,11... | collective-permute-start | bytes 221192 | tf_op jit(solution)/shard_map/ppermute | solution.py:197
  76.8 39.1 %copy-start.3 = (s32[16,8]{0,1:T(8,128)S(1)}, s32[16,8]{0,1:T(8,128)}, u32[]{:S(2)}) copy-start(s32[16,8]{0,1:T(8,128)} %param.6) | copy-start | bytes 1540
  76.8 39.1 %copy-start.5 = (f32[16,8]{0,1:T(8,128)S(1)}, f32[16,8]{0,1:T(8,128)}, u32[]{:S(2)}) copy-start(f32[16,8]{0,1:T(8,128)} %param.7) | copy-start | bytes 1540

commit v5 on v4

--- a/solution.py
+++ b/solution.py
@@ -12,7 +12,7 @@
 SLOTS = LOCAL * CAPACITY
 TILE = 8
 VMEM = pl.BlockSpec(memory_space=pltpu.VMEM)
-PARAMS = pltpu.CompilerParams(vmem_limit_bytes=48 * 1024 * 1024)
+MIB = 1024 * 1024
 
 
 def iota(shape, dim):
@@ -53,23 +53,31 @@
     return jnp.where(found, 1.0, 0.0).astype(jnp.bfloat16)
 
 
-def pack_kernel(w_in_ref, w_down_ref, *out_refs):
-    place = lax.rem(lax.axis_index("tensor"), QUAD)
-    slices = out_refs[0].shape[1] // LANES
-    hid = w_down_ref.shape[1]
-    for r, out in enumerate(out_refs):
-        for j in range(slices):
-            owner = QUAD * j + jnp.bitwise_xor(place, r)
-            src = pl.ds(pl.multiple_of(owner * LANES, LANES), LANES)
-            dst = pl.ds(j * LANES, LANES)
-            for e in range(LOCAL):
-                for g in range(2):
-                    out[pl.ds((2 * e + g) * hid, hid), dst] = w_in_ref[e, g, :, src]
-                out[pl.ds((2 * LOCAL + e) * hid, hid), dst] = w_down_ref[e, :, src]
-
-
-def dispatch_kernel(ids_ref, tok_ref, out_ref):
-    owners, groups = out_ref.shape[:2]
+def start_kernel(
+    ids_hbm,
+    tok_hbm,
+    w_in_hbm,
+    w_down_hbm,
+    sent_ref,
+    keep_ref,
+    core_ref,
+    chip_ref,
+    ids_ref,
+    tok_ref,
+    w_in_ref,
+    w_down_ref,
+    sems,
+):
+    moves = [(ids_hbm, ids_ref), (tok_hbm, tok_ref)]
+    moves += [(w_in_hbm.at[e], w_in_ref.at[e]) for e in range(LOCAL)]
+    moves += [(w_down_hbm, w_down_ref)]
+    copies = [pltpu.make_async_copy(a, b, sems.at[i]) for i, (a, b) in enumerate(moves)]
+    for copy in copies:
+        copy.start()
+    for copy in copies[:2]:
+        copy.wait()
+
+    owners, groups = sent_ref.shape[:2]
     toks = tok_ref.shape[0]
     _, across = slot_rows(ids_ref[...])
     pairs = across.shape[1]
@@ -79,7 +87,21 @@
     values = jnp.dot(placing, values.astype(jnp.bfloat16), preferred_element_type=jnp.float32)
     values = values.reshape(owners, TILE, LANES).astype(jnp.bfloat16)
     for m in range(groups):
-        out_ref[:, m] = values
+        sent_ref[:, m] = values
+
+    for copy in copies[2:]:
+        copy.wait()
+    place = lax.rem(lax.axis_index("tensor"), QUAD)
+    hid = w_down_ref.shape[1]
+    for r, out in enumerate((keep_ref, core_ref, chip_ref.at[0], chip_ref.at[1])):
+        for j in range(groups):
+            owner = QUAD * j + jnp.bitwise_xor(place, r)
+            src = pl.ds(pl.multiple_of(owner * LANES, LANES), LANES)
+            dst = pl.ds(j * LANES, LANES)
+            for e in range(LOCAL):
+                for g in range(2):
+                    out[pl.ds((2 * e + g) * hid, hid), dst] = w_in_ref[e, g, :, src]
+                out[pl.ds((2 * LOCAL + e) * hid, hid), dst] = w_down_ref[e, :, src]
 
 
 def up_kernel(x_ref, w0_ref, w1_ref, w2_ref, w3_ref, own_ref, send_ref):
@@ -97,7 +119,7 @@
     x = jnp.dot(picking, x, preferred_element_type=jnp.float32).astype(jnp.bfloat16)
     hid = w0_ref.shape[0] // (3 * LOCAL)
     first = iota((2 * hid, rows), 1) < rows // LOCAL
-    for r, w_ref in enumerate((w0_ref, w1_ref, w2_ref, w3_ref)):
+    for r, w_ref in enumerate((w0_ref, w1_ref, w2_ref.at[0], w3_ref)):
         both = lax.dot_general(
             w_ref[pl.ds(0, 4 * hid), :],
             x,
@@ -130,7 +152,7 @@
     hid, rows = own_ref.shape[1:]
     first = iota((hid, rows), 1) < rows // LOCAL
     values, weights = [], []
-    for r, w_ref in enumerate((w0_ref, w1_ref, w2_ref, w3_ref)):
+    for r, w_ref in enumerate((w0_ref, w1_ref, w2_ref.at[0], w3_ref)):
         hidden = (got_ref if r % 2 else own_ref)[r // 2].astype(jnp.float32)
         values += [jnp.where(first, hidden, 0.0), jnp.where(first, 0.0, hidden)]
         weights.append(w_ref[pl.ds(4 * hid, 2 * hid), :])
@@ -147,30 +169,33 @@
         out_ref[:, m] = part.reshape(owners, TILE, LANES).astype(jnp.bfloat16)
 
 
-def combine_kernel(ids_ref, gates_ref, x_ref, out_ref):
+def pick_kernel(ids_ref, gates_ref, picking_ref, weights_ref):
+    down, _ = slot_rows(ids_ref[...])
+    picking_ref[...] = onehot(down == iota(picking_ref.shape, 1))
+    gates = gates_ref[...]
+    weights = pair_column(gates / jnp.sum(gates, axis=0, keepdims=True))
+    weights_ref[...] = jnp.broadcast_to(weights, weights_ref.shape)
+
+
+def combine_kernel(picking_ref, weights_ref, x_ref, out_ref):
     owners, groups = x_ref.shape[:2]
-    top, toks = ids_ref.shape
-    held = owners * TILE
-    down, _ = slot_rows(ids_ref[...])
     values = x_ref[:, 0].astype(jnp.float32)
     for m in range(1, groups):
         values = values + x_ref[:, m].astype(jnp.float32)
-    values = values.reshape(held, LANES).astype(jnp.bfloat16)
-    picking = onehot(down == iota((top * toks, held), 1))
-    picked = jnp.dot(picking, values, preferred_element_type=jnp.float32)
-    gates = gates_ref[...]
-    weights = pair_column(gates / jnp.sum(gates, axis=0, keepdims=True))
-    mixed = jnp.sum(picked.reshape(toks, top, LANES) * weights, axis=1)
+    values = values.reshape(owners * TILE, LANES).astype(jnp.bfloat16)
+    picked = jnp.dot(picking_ref[...], values, preferred_element_type=jnp.float32)
+    mixed = jnp.sum(picked.reshape(weights_ref.shape) * weights_ref[...], axis=1)
     out_ref[...] = mixed.astype(jnp.bfloat16)
 
 
-def call(kernel, shapes, args):
+def call(kernel, shapes, args, space=pltpu.VMEM, scratch=(), limit=48 * MIB):
     return pl.pallas_call(
         kernel,
         out_shape=shapes,
-        in_specs=[VMEM] * len(args),
+        in_specs=[pl.BlockSpec(memory_space=space)] * len(args),
         out_specs=jax.tree.map(lambda _: VMEM, shapes),
-        compiler_params=PARAMS,
+        scratch_shapes=list(scratch),
+        compiler_params=pltpu.CompilerParams(vmem_limit_bytes=limit),
     )(*args)
 
 
@@ -203,19 +228,31 @@
         )
         return value.reshape(held)
 
-    packed = call(
-        pack_kernel, [bf16(3 * LOCAL * hid, groups * LANES)] * QUAD, (w_in, w_down)
-    )
-    moved = {r: exchange(packed[r], r) for r in (2, 3, 1)}
-    weights = [packed[0]] + [moved[r] for r in range(1, QUAD)]
-
-    arrived = deal(call(dispatch_kernel, bf16(*held), (ids, tokens)))
+    args = (ids, tokens, w_in, w_down)
+    part = bf16(3 * LOCAL * hid, groups * LANES)
+    sent, keep, core, chip = call(
+        start_kernel,
+        [bf16(*held), part, part, bf16(2, *part.shape)],
+        args,
+        pl.ANY,
+        [pltpu.VMEM(a.shape, a.dtype) for a in args] + [pltpu.SemaphoreType.DMA((5,))],
+        60 * MIB,
+    )
+    chip = exchange(chip, 2)
+    weights = (keep, exchange(core, 1), chip, exchange(chip[1], 1))
+
     pair = (2, 2 * hid, rows)
-    own, send = call(up_kernel, [f32(*pair), bf16(*pair)], (arrived, *weights))
+    own, send = call(up_kernel, [f32(*pair), bf16(*pair)], (deal(sent), *weights))
     own, send = call(add_kernel, [f32(*pair), bf16(*pair)], (own, exchange(send, 1)))
     hidden = call(act_kernel, bf16(2, hid, rows), (own, exchange(send, 2)))
     out = call(down_kernel, bf16(*held), (hidden, exchange(hidden, 1), *weights))
-    return call(combine_kernel, bf16(toks, LANES), (ids, gates, deal(out)))
+
+    out, ids, gates = lax.optimization_barrier((out, ids, gates))
+    top = ids.shape[0]
+    picking, shares = call(
+        pick_kernel, [bf16(top * toks, n_expert * TILE), f32(toks, top, LANES)], (ids, gates)
+    )
+    return call(combine_kernel, bf16(toks, LANES), (picking, shares, deal(out)))
 
 
 def solution(mesh):

time: 117 us -> 109 us (0.932)
  blocking collectives: 39.1 us -> 0 us
  waiting for transfers between devices: 26.6 us -> 48.3 us
  starting transfers between devices: 45.4 us -> 53.8 us
  Pallas kernels: 4.26 us -> 6.47 us
  local copies, waits for them, and re-layouts: 1.39 us -> 0.04 us
    all_to_all x1 -> x0, blocking collectives: 39.1 us -> none  [deal(): lax.all_to_all(value, ('expert', 'tensor'), 0, 0, tiled=True, axis_index_...]
    all_to_all x1 -> x2, waiting for transfers between devices: 0.01 us -> 39 us  [deal(): lax.all_to_all(value, ('expert', 'tensor'), 0, 0, tiled=True, axis_index_...]
    ppermute x6, waiting for transfers between devices: 26.6 us -> 9.35 us  [exchange(): return lax.ppermute(value, 'tensor', [(i, i ^ r) for i in range(n_tensor)])]
    all_to_all x1 -> x2, starting transfers between devices: 30.2 us -> 38.1 us  [deal(): lax.all_to_all(value, ('expert', 'tensor'), 0, 0, tiled=True, axis_index_...]
    pallas_call x7, Pallas kernels: 4.26 us -> 6.47 us  [call(): pl.pallas_call(kernel, out_shape=shapes, in_specs=[pl.BlockSpec(memory_sp...]
    unnamed x12 -> x8, local copies, waits for them, and re-layouts: 1.39 us -> 0.02 us
  transfers between devices with their start and end apart: 7 -> 8, of which waited for: 5 -> 6; matrix products, arithmetic and copies ran while one was open for 0% -> 0% of each run, Pallas kernels for 0% -> 0%
where the time goes in v5:
time: 109 us
  starting transfers between devices  53.8 us (49%)
  waiting for transfers between devices  48.3 us (44%)
  Pallas kernels  6.47 us (6%)
    all_to_all x2, waiting for transfers between devices, deal(): lax.all_to_all(value, ('expert', 'tensor'), 0, 0, tiled=True, axis_index_...  39 us
    all_to_all x2, starting transfers between devices, deal(): lax.all_to_all(value, ('expert', 'tensor'), 0, 0, tiled=True, axis_index_...  38.1 us
    ppermute x6, starting transfers between devices, exchange(): return lax.ppermute(value, 'tensor', [(i, i ^ r) for i in range(n_tensor)])  15.7 us
    ppermute x6, waiting for transfers between devices, exchange(): return lax.ppermute(value, 'tensor', [(i, i ^ r) for i in range(n_tensor)])  9.35 us
    pallas_call x7, Pallas kernels, call(): pl.pallas_call(kernel, out_shape=shapes, in_specs=[pl.BlockSpec(memory_sp...  6.47 us
  transfers between devices with their start and end apart: 8, of which 6 were waited for; matrix products, arithmetic and copies ran while one was open for 0% of the time, Pallas kernels for 0%

profile of v5, /device:TPU:4, one launch (start us, length us, event | category | flops | bytes accessed | tf_op | source)
XLA Modules:
  0.0 108.8 jit_solution(3469421185323946425)
XLA Ops:
  0.0 2.8 %shard_map.55 = (bf16[64,4,8,128]{3,2,1,0:T(8,128)(2,1)}, bf16[288,512]{1,0:T(8,128)(2,1)}, bf16[288,512]{1,0:T(8,128)(2,1)}, bf16[2,288,512]{2,1,0:T(8,128)(2,1)}) custom-call(s32[8,16]{1,0:T(8,128)} %bitcast.10, bf16[16,128]{1,0:T(8,128)(2,1)} %tok_hbm.1, bf16[2,2,48,2048]{3,2,1,0:T(8,128)(2,1)} %w_in_hbm.1, bf16[2,48,2048]{2,1,0:T(8,128)(2,1)} %w_down_hbm.1), custom_call_target="tpu_custom_call" | custom-call | tf_op jit(solution)/shard_map/pallas_call | solution.py:192
  2.8 5.2 %collective-permute-start.1 = (bf16[2,288,512]{2,1,0:T(8,128)(2,1)}, bf16[2,288,512]{2,1,0:T(8,128)(2,1)S(1)}, u32[]{:S(2)}, u32[]{:S(2)}) collective-permute-start(bf16[2,288,512]{2,1,0:T(8,128)(2,1)} %get-tuple-element.21), channel_id=1, source_target_pairs={{0,2},{1,3},{2,0},{3,1},{4,6},{5,7},{6,4},{7,5},{8,10},{9,11},{10,... | collective-permute-start | bytes 1769480 | tf_op jit(solution)/shard_map/ppermute | solution.py:222
  8.0 0.0 copy-start.3
  8.0 29.3 %all-to-all-start = ((bf16[256,8,128]{2,1,0:T(8,128)(2,1)}), bf16[256,8,128]{2,1,0:T(8,128)(2,1)S(1)}, u32[]{:S(2)}, u32[]{:S(2)}) async-start(bf16[256,8,128]{2,1,0:T(8,128)(2,1)} %bitcast.13), calls=%async_computation | async-start | bytes 1048576 | tf_op jit(solution)/shard_map/all_to_all | solution.py:226
  37.3 0.0 copy-done.3
  37.3 0.0 copy-start
  37.3 2.1 %collective-permute-start = (bf16[288,512]{1,0:T(8,128)(2,1)S(1)}, bf16[288,512]{1,0:T(8,128)(2,1)S(1)}, u32[]{:S(2)}, u32[]{:S(2)}) collective-permute-start(bf16[288,512]{1,0:T(8,128)(2,1)S(1)} %copy-done.3), channel_id=1, source_target_pairs={{0,1},{1,0},{2,3},{3,2},{4,5},{5,4},{6,7},{7,6},{8,9},{9,8},{10,11... | collective-permute-start | bytes 884744 | tf_op jit(solution)/shard_map/ppermute | solution.py:222
  39.4 0.0 collective-permute-done.1.w2_ref
  39.4 2.4 %collective-permute-start.2 = (bf16[288,512]{1,0:T(8,128)(2,1)S(1)}, bf16[288,512]{1,0:T(8,128)(2,1)S(1)}, u32[]{:S(2)}, u32[]{:S(2)}) collective-permute-start(bf16[288,512]{1,0:T(8,128)(2,1)S(1)} %slice_bitcast_fusion), channel_id=1, source_target_pairs={{0,1},{1,0},{2,3},{3,2},{4,5},{5,4},{6,7},{7,6},{8,9},{9,8},{10,11... | collective-permute-start | bytes 884744 | tf_op jit(solution)/shard_map/ppermute | solution.py:222
  41.9 0.0 collective-permute-done.w1_ref
  41.9 1.2 %collective-permute-done.2.w3_ref = bf16[288,512]{1,0:T(8,128)(2,1)S(1)} collective-permute-done((bf16[288,512]{1,0:T(8,128)(2,1)S(1)}, bf16[288,512]{1,0:T(8,128)(2,1)S(1)}, u32[]{:S(2)}, u32[]{:S(2)}) %collective-permute-start.2) | collective-permute-done | bytes 294944 | tf_op jit(solution)/shard_map/ppermute | solution.py:222
  43.0 16.4 %all-to-all-done = bf16[256,8,128]{2,1,0:T(8,128)(2,1)S(1)} async-done(((bf16[256,8,128]{2,1,0:T(8,128)(2,1)}), bf16[256,8,128]{2,1,0:T(8,128)(2,1)S(1)}, u32[]{:S(2)}, u32[]{:S(2)}) %all-to-all-start) | async-done | bytes 524320 | tf_op jit(solution)/shard_map/all_to_all | solution.py:226
  59.5 0.0 copy-done
  59.5 1.0 shard_map.56
  60.5 1.9 %collective-permute-start.3 = (bf16[2,96,384]{2,1,0:T(8,128)(2,1)S(1)}, bf16[2,96,384]{2,1,0:T(8,128)(2,1)S(1)}, u32[]{:S(2)}, u32[]{:S(2)}) collective-permute-start(bf16[2,96,384]{2,1,0:T(8,128)(2,1)S(1)} %get-tuple-element.23), channel_id=1, source_target_pairs={{0,1},{1,0},{2,3},{3,2},{4,5},{5,4},{6,7},{7,6},{8,9},{9,8},{10,11... | collective-permute-start | bytes 442376 | tf_op jit(solution)/shard_map/ppermute | solution.py:222
  62.4 1.3 %collective-permute-done.3.got_ref = bf16[2,96,384]{2,1,0:T(8,128)(2,1)S(1)} collective-permute-done((bf16[2,96,384]{2,1,0:T(8,128)(2,1)S(1)}, bf16[2,96,384]{2,1,0:T(8,128)(2,1)S(1)}, u32[]{:S(2)}, u32[]{:S(2)}) %collective-permute-start.3) | collective-permute-done | bytes 147488 | tf_op jit(solution)/shard_map/ppermute | solution.py:222
  63.8 2.2 %collective-permute-start.4 = (bf16[2,96,384]{2,1,0:T(8,128)(2,1)S(1)}, bf16[2,96,384]{2,1,0:T(8,128)(2,1)S(1)}, u32[]{:S(2)}, u32[]{:S(2)}) collective-permute-start(bf16[2,96,384]{2,1,0:T(8,128)(2,1)S(1)} %get-tuple-element.25), channel_id=1, source_target_pairs={{0,2},{1,3},{2,0},{3,1},{4,6},{5,7},{6,4},{7,5},{8,10},{9,11},{10,... | collective-permute-start | bytes 442376 | tf_op jit(solution)/shard_map/ppermute | solution.py:222
  66.0 5.6 %collective-permute-done.4.got_ref = bf16[2,96,384]{2,1,0:T(8,128)(2,1)S(1)} collective-permute-done((bf16[2,96,384]{2,1,0:T(8,128)(2,1)S(1)}, bf16[2,96,384]{2,1,0:T(8,128)(2,1)S(1)}, u32[]{:S(2)}, u32[]{:S(2)}) %collective-permute-start.4) | collective-permute-done | bytes 147488 | tf_op jit(solution)/shard_map/ppermute | solution.py:222
  71.6 0.1 shard_map.58.own_ref
  71.6 1.9 %collective-permute-start.5 = (bf16[2,48,384]{2,1,0:T(8,128)(2,1)S(1)}, bf16[2,48,384]{2,1,0:T(8,128)(2,1)S(1)}, u32[]{:S(2)}, u32[]{:S(2)}) collective-permute-start(bf16[2,48,384]{2,1,0:T(8,128)(2,1)S(1)} %shard_map.58.own_ref), channel_id=1, source_target_pairs={{0,1},{1,0},{2,3},{3,2},{4,5},{5,4},{6,7},{7,6},{8,9},{9,8},{10,11... | collective-permute-start | bytes 221192 | tf_op jit(solution)/shard_map/ppermute | solution.py:222
  73.6 1.2 %collective-permute-done.5.got_ref = bf16[2,48,384]{2,1,0:T(8,128)(2,1)S(1)} collective-permute-done((bf16[2,48,384]{2,1,0:T(8,128)(2,1)S(1)}, bf16[2,48,384]{2,1,0:T(8,128)(2,1)S(1)}, u32[]{:S(2)}, u32[]{:S(2)}) %collective-permute-start.5) | collective-permute-done | bytes 73760 | tf_op jit(solution)/shard_map/ppermute | solution.py:222
  74.8 1.6 %shard_map.59 = bf16[64,4,8,128]{3,2,1,0:T(8,128)(2,1)} custom-call(bf16[2,48,384]{2,1,0:T(8,128)(2,1)S(1)} %shard_map.58.own_ref, bf16[2,48,384]{2,1,0:T(8,128)(2,1)S(1)} %collective-permute-done.5.got_ref, bf16[288,512]{1,0:T(8,128)(2,1)S(1)} %copy-done, bf16[288,512]{1,0:T(8,128)(2,1)S(1)} %collective-permute-done.w1_ref, ...), custom_call_target="tpu_custom_call" | custom-call | tf_op jit(solution)/shard_map/pallas_call | solution.py:192
  76.4 0.0 copy-start.1
  76.4 0.0 copy-start.2
  76.4 8.8 %all-to-all-start.1 = ((bf16[256,8,128]{2,1,0:T(8,128)(2,1)}), bf16[256,8,128]{2,1,0:T(8,128)(2,1)S(1)}, u32[]{:S(2)}, u32[]{:S(2)}) async-start(bf16[256,8,128]{2,1,0:T(8,128)(2,1)} %bitcast.5), calls=%async_computation.1 | async-start | bytes 1048576 | tf_op jit(solution)/shard_map/all_to_all | solution.py:226
  85.2 0.0 copy-done.1
  85.2 0.0 copy-done.2
  85.2 0.2 shard_map.60
  85.4 22.6 %all-to-all-done.1 = bf16[256,8,128]{2,1,0:T(8,128)(2,1)S(1)} async-done(((bf16[256,8,128]{2,1,0:T(8,128)(2,1)}), bf16[256,8,128]{2,1,0:T(8,128)(2,1)S(1)}, u32[]{:S(2)}, u32[]{:S(2)}) %all-to-all-start.1) | async-done | bytes 524320 | tf_op jit(solution)/shard_map/all_to_all | solution.py:226
  108.0 0.8 shard_map.61
  (2 shorter events, 0.1 us)
Async XLA Ops:
  2.8 36.6 %collective-permute-start.1 = (bf16[2,288,512]{2,1,0:T(8,128)(2,1)}, bf16[2,288,512]{2,1,0:T(8,128)(2,1)S(1)}, u32[]{:S(2)}, u32[]{:S(2)}) collective-permute-start(bf16[2,288,512]{2,1,0:T(8,128)(2,1)} %get-tuple-element.21), channel_id=1, source_target_pairs={{0,2},{1,3},{2,0},{3,1},{4,6},{5,7},{6,4},{7,5},{8,10},{9,11},{10,... | collective-permute-start | bytes 1769480 | tf_op jit(solution)/shard_map/ppermute | solution.py:222
  8.0 29.3 %copy-start.3 = (bf16[288,512]{1,0:T(8,128)(2,1)S(1)}, bf16[288,512]{1,0:T(8,128)(2,1)}, u32[]{:S(2)}) copy-start(bf16[288,512]{1,0:T(8,128)(2,1)} %get-tuple-element.20) | copy-start | bytes 884740
  8.0 51.5 %all-to-all-start = ((bf16[256,8,128]{2,1,0:T(8,128)(2,1)}), bf16[256,8,128]{2,1,0:T(8,128)(2,1)S(1)}, u32[]{:S(2)}, u32[]{:S(2)}) async-start(bf16[256,8,128]{2,1,0:T(8,128)(2,1)} %bitcast.13), calls=%async_computation | async-start | bytes 1048576 | tf_op jit(solution)/shard_map/all_to_all | solution.py:226
  37.3 22.1 %copy-start = (bf16[288,512]{1,0:T(8,128)(2,1)S(1)}, bf16[288,512]{1,0:T(8,128)(2,1)}, u32[]{:S(2)}) copy-start(bf16[288,512]{1,0:T(8,128)(2,1)} %get-tuple-element.19.w0_ref) | copy-start | bytes 884740
  37.3 4.5 %collective-permute-start = (bf16[288,512]{1,0:T(8,128)(2,1)S(1)}, bf16[288,512]{1,0:T(8,128)(2,1)S(1)}, u32[]{:S(2)}, u32[]{:S(2)}) collective-permute-start(bf16[288,512]{1,0:T(8,128)(2,1)S(1)} %copy-done.3), channel_id=1, source_target_pairs={{0,1},{1,0},{2,3},{3,2},{4,5},{5,4},{6,7},{7,6},{8,9},{9,8},{10,11... | collective-permute-start | bytes 884744 | tf_op jit(solution)/shard_map/ppermute | solution.py:222
  39.4 3.6 %collective-permute-start.2 = (bf16[288,512]{1,0:T(8,128)(2,1)S(1)}, bf16[288,512]{1,0:T(8,128)(2,1)S(1)}, u32[]{:S(2)}, u32[]{:S(2)}) collective-permute-start(bf16[288,512]{1,0:T(8,128)(2,1)S(1)} %slice_bitcast_fusion), channel_id=1, source_target_pairs={{0,1},{1,0},{2,3},{3,2},{4,5},{5,4},{6,7},{7,6},{8,9},{9,8},{10,11... | collective-permute-start | bytes 884744 | tf_op jit(solution)/shard_map/ppermute | solution.py:222
  60.5 3.3 %collective-permute-start.3 = (bf16[2,96,384]{2,1,0:T(8,128)(2,1)S(1)}, bf16[2,96,384]{2,1,0:T(8,128)(2,1)S(1)}, u32[]{:S(2)}, u32[]{:S(2)}) collective-permute-start(bf16[2,96,384]{2,1,0:T(8,128)(2,1)S(1)} %get-tuple-element.23), channel_id=1, source_target_pairs={{0,1},{1,0},{2,3},{3,2},{4,5},{5,4},{6,7},{7,6},{8,9},{9,8},{10,11... | collective-permute-start | bytes 442376 | tf_op jit(solution)/shard_map/ppermute | solution.py:222
  63.8 7.8 %collective-permute-start.4 = (bf16[2,96,384]{2,1,0:T(8,128)(2,1)S(1)}, bf16[2,96,384]{2,1,0:T(8,128)(2,1)S(1)}, u32[]{:S(2)}, u32[]{:S(2)}) collective-permute-start(bf16[2,96,384]{2,1,0:T(8,128)(2,1)S(1)} %get-tuple-element.25), channel_id=1, source_target_pairs={{0,2},{1,3},{2,0},{3,1},{4,6},{5,7},{6,4},{7,5},{8,10},{9,11},{10,... | collective-permute-start | bytes 442376 | tf_op jit(solution)/shard_map/ppermute | solution.py:222
  71.6 3.2 %collective-permute-start.5 = (bf16[2,48,384]{2,1,0:T(8,128)(2,1)S(1)}, bf16[2,48,384]{2,1,0:T(8,128)(2,1)S(1)}, u32[]{:S(2)}, u32[]{:S(2)}) collective-permute-start(bf16[2,48,384]{2,1,0:T(8,128)(2,1)S(1)} %shard_map.58.own_ref), channel_id=1, source_target_pairs={{0,1},{1,0},{2,3},{3,2},{4,5},{5,4},{6,7},{7,6},{8,9},{9,8},{10,11... | collective-permute-start | bytes 221192 | tf_op jit(solution)/shard_map/ppermute | solution.py:222
  76.4 8.8 %copy-start.1 = (s32[16,8]{0,1:T(8,128)S(1)}, s32[16,8]{0,1:T(8,128)}, u32[]{:S(2)}) copy-start(s32[16,8]{0,1:T(8,128)} %param.6) | copy-start | bytes 1540
  76.4 8.8 %copy-start.2 = (f32[16,8]{0,1:T(8,128)S(1)}, f32[16,8]{0,1:T(8,128)}, u32[]{:S(2)}) copy-start(f32[16,8]{0,1:T(8,128)} %param.7) | copy-start | bytes 1540
  76.4 31.6 %all-to-all-start.1 = ((bf16[256,8,128]{2,1,0:T(8,128)(2,1)}), bf16[256,8,128]{2,1,0:T(8,128)(2,1)S(1)}, u32[]{:S(2)}, u32[]{:S(2)}) async-start(bf16[256,8,128]{2,1,0:T(8,128)(2,1)} %bitcast.5), calls=%async_computation.1 | async-start | bytes 1048576 | tf_op jit(solution)/shard_map/all_to_all | solution.py:226

commit v6 on v5

--- a/solution.py
+++ b/solution.py
@@ -51,6 +51,12 @@
 
 def onehot(found):
     return jnp.where(found, 1.0, 0.0).astype(jnp.bfloat16)
+
+
+def padded(values):
+    owners = values.shape[0]
+    blank = jnp.zeros((owners, TILE - SLOTS, LANES), values.dtype)
+    return jnp.concatenate([values, blank], axis=1).reshape(owners * TILE, LANES)
 
 
 def start_kernel(
@@ -85,7 +91,7 @@
     values = jnp.dot(token_of, tok_ref[...], preferred_element_type=jnp.float32)
     placing = onehot(iota((owners * TILE, pairs), 0) == across)
     values = jnp.dot(placing, values.astype(jnp.bfloat16), preferred_element_type=jnp.float32)
-    values = values.reshape(owners, TILE, LANES).astype(jnp.bfloat16)
+    values = values.reshape(owners, TILE, LANES)[:, :SLOTS].astype(jnp.bfloat16)
     for m in range(groups):
         sent_ref[:, m] = values
 
@@ -110,7 +116,7 @@
     rows = own_ref.shape[2]
     x = jnp.concatenate(
         [
-            x_ref[:, m].astype(jnp.float32).reshape(held, LANES).astype(jnp.bfloat16)
+            padded(x_ref[:, m].astype(jnp.float32)).astype(jnp.bfloat16)
             for m in range(groups)
         ],
         axis=1,
@@ -166,25 +172,22 @@
     out = jnp.dot(values, weights, preferred_element_type=jnp.float32)
     for m in range(groups):
         part = out[:, m * LANES : (m + 1) * LANES]
-        out_ref[:, m] = part.reshape(owners, TILE, LANES).astype(jnp.bfloat16)
-
-
-def pick_kernel(ids_ref, gates_ref, picking_ref, weights_ref):
+        out_ref[:, m] = part.reshape(owners, TILE, LANES)[:, :SLOTS].astype(jnp.bfloat16)
+
+
+def combine_kernel(ids_ref, gates_ref, x_ref, out_ref):
+    owners, groups = x_ref.shape[:2]
+    top, toks = ids_ref.shape
     down, _ = slot_rows(ids_ref[...])
-    picking_ref[...] = onehot(down == iota(picking_ref.shape, 1))
-    gates = gates_ref[...]
-    weights = pair_column(gates / jnp.sum(gates, axis=0, keepdims=True))
-    weights_ref[...] = jnp.broadcast_to(weights, weights_ref.shape)
-
-
-def combine_kernel(picking_ref, weights_ref, x_ref, out_ref):
-    owners, groups = x_ref.shape[:2]
     values = x_ref[:, 0].astype(jnp.float32)
     for m in range(1, groups):
         values = values + x_ref[:, m].astype(jnp.float32)
-    values = values.reshape(owners * TILE, LANES).astype(jnp.bfloat16)
-    picked = jnp.dot(picking_ref[...], values, preferred_element_type=jnp.float32)
-    mixed = jnp.sum(picked.reshape(weights_ref.shape) * weights_ref[...], axis=1)
+    values = padded(values).astype(jnp.bfloat16)
+    picking = onehot(down == iota((top * toks, owners * TILE), 1))
+    picked = jnp.dot(picking, values, preferred_element_type=jnp.float32)
+    gates = gates_ref[...]
+    weights = pair_column(gates / jnp.sum(gates, axis=0, keepdims=True))
+    mixed = jnp.sum(picked.reshape(toks, top, LANES) * weights, axis=1)
     out_ref[...] = mixed.astype(jnp.bfloat16)
 
 
@@ -210,7 +213,7 @@
         [e * n_tensor + QUAD * m + q for e in range(n_expert) for m in range(groups)]
         for q in range(QUAD)
     ]
-    held = (n_expert, groups, TILE, LANES)
+    held = (n_expert, groups, SLOTS, LANES)
 
     def bf16(*shape):
         return jax.ShapeDtypeStruct(shape, jnp.bfloat16)
@@ -222,7 +225,7 @@
         return lax.ppermute(value, "tensor", [(i, i ^ r) for i in range(n_tensor)])
 
     def deal(value):
-        value = value.reshape(n_expert * groups, TILE, LANES)
+        value = value.reshape(n_expert * groups, SLOTS, LANES)
         value = lax.all_to_all(
             value, ("expert", "tensor"), 0, 0, tiled=True, axis_index_groups=peers
         )
@@ -246,13 +249,7 @@
     own, send = call(add_kernel, [f32(*pair), bf16(*pair)], (own, exchange(send, 1)))
     hidden = call(act_kernel, bf16(2, hid, rows), (own, exchange(send, 2)))
     out = call(down_kernel, bf16(*held), (hidden, exchange(hidden, 1), *weights))
-
-    out, ids, gates = lax.optimization_barrier((out, ids, gates))
-    top = ids.shape[0]
-    picking, shares = call(
-        pick_kernel, [bf16(top * toks, n_expert * TILE), f32(toks, top, LANES)], (ids, gates)
-    )
-    return call(combine_kernel, bf16(toks, LANES), (picking, shares, deal(out)))
+    return call(combine_kernel, bf16(toks, LANES), (ids, gates, deal(out)))
 
 
 def solution(mesh):

time: 109 us -> 108 us (level)
  blocking collectives: 0 us -> 31.2 us
  waiting for transfers between devices: 48.3 us -> 25.8 us
  starting transfers between devices: 53.8 us -> 45 us
    all_to_all x0 -> x1, blocking collectives: none -> 31.2 us  [deal(): lax.all_to_all(value, ('expert', 'tensor'), 0, 0, tiled=True, axis_index_...]
    all_to_all x2 -> x1, waiting for transfers between devices: 39 us -> 17.6 us  [deal(): lax.all_to_all(value, ('expert', 'tensor'), 0, 0, tiled=True, axis_index_...]
    all_to_all x2 -> x1, starting transfers between devices: 38.1 us -> 29.3 us  [deal(): lax.all_to_all(value, ('expert', 'tensor'), 0, 0, tiled=True, axis_index_...]
    ppermute x6, waiting for transfers between devices: 9.35 us -> 8.17 us  [exchange(): return lax.ppermute(value, 'tensor', [(i, i ^ r) for i in range(n_tensor)])]
    pallas_call x7 -> x6, Pallas kernels: 6.47 us -> 5.61 us  [call(): pl.pallas_call(kernel, out_shape=shapes, in_specs=[pl.BlockSpec(memory_sp...]
  transfers between devices with their start and end apart: 8 -> 7, of which waited for: 6 -> 4; matrix products, arithmetic and copies ran while one was open for 0% -> 0% of each run, Pallas kernels for 0% -> 0%
where the time goes in v6:
time: 108 us
  starting transfers between devices  45 us (42%)
  blocking collectives  31.2 us (29%)
  waiting for transfers between devices  25.8 us (24%)
  Pallas kernels  5.61 us (5%)
    all_to_all x1, blocking collectives, deal(): lax.all_to_all(value, ('expert', 'tensor'), 0, 0, tiled=True, axis_index_...  31.2 us
    all_to_all x1, starting transfers between devices, deal(): lax.all_to_all(value, ('expert', 'tensor'), 0, 0, tiled=True, axis_index_...  29.3 us
    all_to_all x1, waiting for transfers between devices, deal(): lax.all_to_all(value, ('expert', 'tensor'), 0, 0, tiled=True, axis_index_...  17.6 us
    ppermute x6, starting transfers between devices, exchange(): return lax.ppermute(value, 'tensor', [(i, i ^ r) for i in range(n_tensor)])  15.7 us
    ppermute x6, waiting for transfers between devices, exchange(): return lax.ppermute(value, 'tensor', [(i, i ^ r) for i in range(n_tensor)])  8.17 us
    pallas_call x6, Pallas kernels, call(): pl.pallas_call(kernel, out_shape=shapes, in_specs=[pl.BlockSpec(memory_sp...  5.61 us
  transfers between devices with their start and end apart: 7, of which 4 were waited for; matrix products, arithmetic and copies ran while one was open for 0% of the time, Pallas kernels for 0%

profile of v6, /device:TPU:4, one launch (start us, length us, event | category | flops | bytes accessed | tf_op | source)
XLA Modules:
  0.0 107.8 jit_solution(17079287322526906156)
XLA Ops:
  0.0 2.8 %shard_map.55 = (bf16[64,4,6,128]{3,2,1,0:T(8,128)(2,1)}, bf16[288,512]{1,0:T(8,128)(2,1)}, bf16[288,512]{1,0:T(8,128)(2,1)}, bf16[2,288,512]{2,1,0:T(8,128)(2,1)}) custom-call(s32[8,16]{1,0:T(8,128)} %bitcast.11, bf16[16,128]{1,0:T(8,128)(2,1)} %tok_hbm.1, bf16[2,2,48,2048]{3,2,1,0:T(8,128)(2,1)} %w_in_hbm.1, bf16[2,48,2048]{2,1,0:T(8,128)(2,1)} %w_down_hbm.1), custom_call_target="tpu_custom_call" | custom-call | tf_op jit(solution)/shard_map/pallas_call | solution.py:195
  2.8 5.2 %collective-permute-start.1 = (bf16[2,288,512]{2,1,0:T(8,128)(2,1)}, bf16[2,288,512]{2,1,0:T(8,128)(2,1)S(1)}, u32[]{:S(2)}, u32[]{:S(2)}) collective-permute-start(bf16[2,288,512]{2,1,0:T(8,128)(2,1)} %get-tuple-element.16), channel_id=1, source_target_pairs={{0,2},{1,3},{2,0},{3,1},{4,6},{5,7},{6,4},{7,5},{8,10},{9,11},{10,... | collective-permute-start | bytes 1769480 | tf_op jit(solution)/shard_map/ppermute | solution.py:225
  8.0 0.0 copy-start.3
  8.0 29.3 %all-to-all-start = ((bf16[256,6,128]{2,1,0:T(8,128)(2,1)}), bf16[256,6,128]{2,1,0:T(8,128)(2,1)S(1)}, u32[]{:S(2)}, u32[]{:S(2)}) async-start(bf16[256,6,128]{2,1,0:T(8,128)(2,1)} %bitcast.14), calls=%async_computation | async-start | bytes 1048576 | tf_op jit(solution)/shard_map/all_to_all | solution.py:229
  37.3 0.0 copy-done.3
  37.3 0.0 copy-start
  37.4 2.1 %collective-permute-start = (bf16[288,512]{1,0:T(8,128)(2,1)S(1)}, bf16[288,512]{1,0:T(8,128)(2,1)S(1)}, u32[]{:S(2)}, u32[]{:S(2)}) collective-permute-start(bf16[288,512]{1,0:T(8,128)(2,1)S(1)} %copy-done.3), channel_id=1, source_target_pairs={{0,1},{1,0},{2,3},{3,2},{4,5},{5,4},{6,7},{7,6},{8,9},{9,8},{10,11... | collective-permute-start | bytes 884744 | tf_op jit(solution)/shard_map/ppermute | solution.py:225
  39.4 0.0 collective-permute-done.1.w2_ref
  39.4 2.4 %collective-permute-start.2 = (bf16[288,512]{1,0:T(8,128)(2,1)S(1)}, bf16[288,512]{1,0:T(8,128)(2,1)S(1)}, u32[]{:S(2)}, u32[]{:S(2)}) collective-permute-start(bf16[288,512]{1,0:T(8,128)(2,1)S(1)} %slice_bitcast_fusion), channel_id=1, source_target_pairs={{0,1},{1,0},{2,3},{3,2},{4,5},{5,4},{6,7},{7,6},{8,9},{9,8},{10,11... | collective-permute-start | bytes 884744 | tf_op jit(solution)/shard_map/ppermute | solution.py:225
  41.9 0.0 collective-permute-done.w1_ref
  41.9 17.6 %all-to-all-done = bf16[256,6,128]{2,1,0:T(8,128)(2,1)S(1)} async-done(((bf16[256,6,128]{2,1,0:T(8,128)(2,1)}), bf16[256,6,128]{2,1,0:T(8,128)(2,1)S(1)}, u32[]{:S(2)}, u32[]{:S(2)}) %all-to-all-start) | async-done | bytes 393248 | tf_op jit(solution)/shard_map/all_to_all | solution.py:229
  59.5 0.0 collective-permute-done.2.w3_ref
  59.5 0.0 copy-done
  59.5 1.0 shard_map.56
  60.5 1.9 %collective-permute-start.3 = (bf16[2,96,384]{2,1,0:T(8,128)(2,1)S(1)}, bf16[2,96,384]{2,1,0:T(8,128)(2,1)S(1)}, u32[]{:S(2)}, u32[]{:S(2)}) collective-permute-start(bf16[2,96,384]{2,1,0:T(8,128)(2,1)S(1)} %get-tuple-element.18), channel_id=1, source_target_pairs={{0,1},{1,0},{2,3},{3,2},{4,5},{5,4},{6,7},{7,6},{8,9},{9,8},{10,11... | collective-permute-start | bytes 442376 | tf_op jit(solution)/shard_map/ppermute | solution.py:225
  62.4 1.3 %collective-permute-done.3.got_ref = bf16[2,96,384]{2,1,0:T(8,128)(2,1)S(1)} collective-permute-done((bf16[2,96,384]{2,1,0:T(8,128)(2,1)S(1)}, bf16[2,96,384]{2,1,0:T(8,128)(2,1)S(1)}, u32[]{:S(2)}, u32[]{:S(2)}) %collective-permute-start.3) | collective-permute-done | bytes 147488 | tf_op jit(solution)/shard_map/ppermute | solution.py:225
  63.8 2.2 %collective-permute-start.4 = (bf16[2,96,384]{2,1,0:T(8,128)(2,1)S(1)}, bf16[2,96,384]{2,1,0:T(8,128)(2,1)S(1)}, u32[]{:S(2)}, u32[]{:S(2)}) collective-permute-start(bf16[2,96,384]{2,1,0:T(8,128)(2,1)S(1)} %get-tuple-element.20), channel_id=1, source_target_pairs={{0,2},{1,3},{2,0},{3,1},{4,6},{5,7},{6,4},{7,5},{8,10},{9,11},{10,... | collective-permute-start | bytes 442376 | tf_op jit(solution)/shard_map/ppermute | solution.py:225
  66.0 5.6 %collective-permute-done.4.got_ref = bf16[2,96,384]{2,1,0:T(8,128)(2,1)S(1)} collective-permute-done((bf16[2,96,384]{2,1,0:T(8,128)(2,1)S(1)}, bf16[2,96,384]{2,1,0:T(8,128)(2,1)S(1)}, u32[]{:S(2)}, u32[]{:S(2)}) %collective-permute-start.4) | collective-permute-done | bytes 147488 | tf_op jit(solution)/shard_map/ppermute | solution.py:225
  71.6 0.1 shard_map.58.own_ref
  71.7 1.9 %collective-permute-start.5 = (bf16[2,48,384]{2,1,0:T(8,128)(2,1)S(1)}, bf16[2,48,384]{2,1,0:T(8,128)(2,1)S(1)}, u32[]{:S(2)}, u32[]{:S(2)}) collective-permute-start(bf16[2,48,384]{2,1,0:T(8,128)(2,1)S(1)} %shard_map.58.own_ref), channel_id=1, source_target_pairs={{0,1},{1,0},{2,3},{3,2},{4,5},{5,4},{6,7},{7,6},{8,9},{9,8},{10,11... | collective-permute-start | bytes 221192 | tf_op jit(solution)/shard_map/ppermute | solution.py:225
  73.6 1.2 %collective-permute-done.5.got_ref = bf16[2,48,384]{2,1,0:T(8,128)(2,1)S(1)} collective-permute-done((bf16[2,48,384]{2,1,0:T(8,128)(2,1)S(1)}, bf16[2,48,384]{2,1,0:T(8,128)(2,1)S(1)}, u32[]{:S(2)}, u32[]{:S(2)}) %collective-permute-start.5) | collective-permute-done | bytes 73760 | tf_op jit(solution)/shard_map/ppermute | solution.py:225
  74.8 0.8 shard_map.59
  75.6 0.0 copy-start.1
  75.6 0.0 copy-start.2
  75.6 31.2 %all_to_all.10 = bf16[256,6,128]{2,1,0:T(8,128)(2,1)S(1)} all-to-all(bf16[256,6,128]{2,1,0:T(8,128)(2,1)S(1)} %bitcast.10), channel_id=1, replica_groups={{0,4,8,12,16,20,24,28,32,36,40,44,48,52,56,60,64,68,72,76,80,84,88,92,9..., dimensions={0} | all-to-all | bytes 786432 | tf_op jit(solution)/shard_map/all_to_all | solution.py:229
  106.8 0.0 copy-done.1
  106.8 0.0 copy-done.2
  106.8 1.0 shard_map.60
  (2 shorter events, 0.1 us)
Async XLA Ops:
  2.8 36.6 %collective-permute-start.1 = (bf16[2,288,512]{2,1,0:T(8,128)(2,1)}, bf16[2,288,512]{2,1,0:T(8,128)(2,1)S(1)}, u32[]{:S(2)}, u32[]{:S(2)}) collective-permute-start(bf16[2,288,512]{2,1,0:T(8,128)(2,1)} %get-tuple-element.16), channel_id=1, source_target_pairs={{0,2},{1,3},{2,0},{3,1},{4,6},{5,7},{6,4},{7,5},{8,10},{9,11},{10,... | collective-permute-start | bytes 1769480 | tf_op jit(solution)/shard_map/ppermute | solution.py:225
  8.0 29.3 %copy-start.3 = (bf16[288,512]{1,0:T(8,128)(2,1)S(1)}, bf16[288,512]{1,0:T(8,128)(2,1)}, u32[]{:S(2)}) copy-start(bf16[288,512]{1,0:T(8,128)(2,1)} %get-tuple-element.15) | copy-start | bytes 884740
  8.0 51.5 %all-to-all-start = ((bf16[256,6,128]{2,1,0:T(8,128)(2,1)}), bf16[256,6,128]{2,1,0:T(8,128)(2,1)S(1)}, u32[]{:S(2)}, u32[]{:S(2)}) async-start(bf16[256,6,128]{2,1,0:T(8,128)(2,1)} %bitcast.14), calls=%async_computation | async-start | bytes 1048576 | tf_op jit(solution)/shard_map/all_to_all | solution.py:229
  37.3 22.1 %copy-start = (bf16[288,512]{1,0:T(8,128)(2,1)S(1)}, bf16[288,512]{1,0:T(8,128)(2,1)}, u32[]{:S(2)}) copy-start(bf16[288,512]{1,0:T(8,128)(2,1)} %get-tuple-element.14.w0_ref) | copy-start | bytes 884740
  37.4 4.5 %collective-permute-start = (bf16[288,512]{1,0:T(8,128)(2,1)S(1)}, bf16[288,512]{1,0:T(8,128)(2,1)S(1)}, u32[]{:S(2)}, u32[]{:S(2)}) collective-permute-start(bf16[288,512]{1,0:T(8,128)(2,1)S(1)} %copy-done.3), channel_id=1, source_target_pairs={{0,1},{1,0},{2,3},{3,2},{4,5},{5,4},{6,7},{7,6},{8,9},{9,8},{10,11... | collective-permute-start | bytes 884744 | tf_op jit(solution)/shard_map/ppermute | solution.py:225
  39.4 20.0 %collective-permute-start.2 = (bf16[288,512]{1,0:T(8,128)(2,1)S(1)}, bf16[288,512]{1,0:T(8,128)(2,1)S(1)}, u32[]{:S(2)}, u32[]{:S(2)}) collective-permute-start(bf16[288,512]{1,0:T(8,128)(2,1)S(1)} %slice_bitcast_fusion), channel_id=1, source_target_pairs={{0,1},{1,0},{2,3},{3,2},{4,5},{5,4},{6,7},{7,6},{8,9},{9,8},{10,11... | collective-permute-start | bytes 884744 | tf_op jit(solution)/shard_map/ppermute | solution.py:225
  60.5 3.3 %collective-permute-start.3 = (bf16[2,96,384]{2,1,0:T(8,128)(2,1)S(1)}, bf16[2,96,384]{2,1,0:T(8,128)(2,1)S(1)}, u32[]{:S(2)}, u32[]{:S(2)}) collective-permute-start(bf16[2,96,384]{2,1,0:T(8,128)(2,1)S(1)} %get-tuple-element.18), channel_id=1, source_target_pairs={{0,1},{1,0},{2,3},{3,2},{4,5},{5,4},{6,7},{7,6},{8,9},{9,8},{10,11... | collective-permute-start | bytes 442376 | tf_op jit(solution)/shard_map/ppermute | solution.py:225
  63.8 7.8 %collective-permute-start.4 = (bf16[2,96,384]{2,1,0:T(8,128)(2,1)S(1)}, bf16[2,96,384]{2,1,0:T(8,128)(2,1)S(1)}, u32[]{:S(2)}, u32[]{:S(2)}) collective-permute-start(bf16[2,96,384]{2,1,0:T(8,128)(2,1)S(1)} %get-tuple-element.20), channel_id=1, source_target_pairs={{0,2},{1,3},{2,0},{3,1},{4,6},{5,7},{6,4},{7,5},{8,10},{9,11},{10,... | collective-permute-start | bytes 442376 | tf_op jit(solution)/shard_map/ppermute | solution.py:225
  71.7 3.2 %collective-permute-start.5 = (bf16[2,48,384]{2,1,0:T(8,128)(2,1)S(1)}, bf16[2,48,384]{2,1,0:T(8,128)(2,1)S(1)}, u32[]{:S(2)}, u32[]{:S(2)}) collective-permute-start(bf16[2,48,384]{2,1,0:T(8,128)(2,1)S(1)} %shard_map.58.own_ref), channel_id=1, source_target_pairs={{0,1},{1,0},{2,3},{3,2},{4,5},{5,4},{6,7},{7,6},{8,9},{9,8},{10,11... | collective-permute-start | bytes 221192 | tf_op jit(solution)/shard_map/ppermute | solution.py:225
  75.6 31.2 %copy-start.1 = (s32[16,8]{0,1:T(8,128)S(1)}, s32[16,8]{0,1:T(8,128)}, u32[]{:S(2)}) copy-start(s32[16,8]{0,1:T(8,128)} %param.6) | copy-start | bytes 1540
  75.6 31.2 %copy-start.2 = (f32[16,8]{0,1:T(8,128)S(1)}, f32[16,8]{0,1:T(8,128)}, u32[]{:S(2)}) copy-start(f32[16,8]{0,1:T(8,128)} %param.7) | copy-start | bytes 1540

commit v7 on v4

v7 whole, which is shorter than its diff:
```python
import jax
import jax.numpy as jnp
from jax import lax
from jax.experimental import pallas as pl
from jax.experimental.pallas import tpu as pltpu
from jax.sharding import PartitionSpec as P

LANES = 128
CAPACITY = 3
QUAD = 4
LOCAL = 2
SLOTS = LOCAL * CAPACITY
TILE = 8
VMEM = pl.BlockSpec(memory_space=pltpu.VMEM)
ANY = pl.BlockSpec(memory_space=pl.ANY)
MIB = 1024 * 1024


def iota(shape, dim):
    return lax.broadcasted_iota(jnp.int32, shape, dim)


def pair_column(values):
    top, toks = values.shape
    shape = (toks, top, toks)
    picked = jnp.where(iota(shape, 0) == iota(shape, 2), values[None], 0.0)
    return jnp.sum(picked, axis=2, keepdims=True)


def slot_rows(ids):
    top, toks = ids.shape
    pairs = top * toks
    down = pair_column(ids.astype(jnp.float32)).reshape(pairs, 1)
    ip, iq = iota((pairs, pairs), 0), iota((pairs, pairs), 1)
    across = jnp.sum(jnp.where(ip == iq, down, 0.0), axis=0, keepdims=True)
    same = down == across
    slot_down = jnp.sum(jnp.where(same & (iq < ip), 1.0, 0.0), axis=1, keepdims=True)
    slot_across = jnp.sum(jnp.where(same & (ip < iq), 1.0, 0.0), axis=0, keepdims=True)

    def row(number, slot):
        number, slot = number.astype(jnp.int32), slot.astype(jnp.int32)
        return number // LOCAL * TILE + number % LOCAL * CAPACITY + slot

    return row(down, slot_down), row(across, slot_across)


def dense_row(shape, dim, owners):
    row = iota(shape, dim)
    slot = row % TILE
    return jnp.where(slot < SLOTS, slot * owners + row // TILE, -1)


def onehot(found):
    return jnp.where(found, 1.0, 0.0).astype(jnp.bfloat16)


def padded(values):
    owners = values.shape[0]
    blank = jnp.zeros((owners, TILE - SLOTS, LANES), values.dtype)
    return jnp.concatenate([values, blank], axis=1).reshape(owners * TILE, LANES)


def start_kernel(
    ids_hbm, tok_hbm, w_in_hbm, w_down_hbm, sent_ref, keep_ref, core_ref, chip_ref, ids_ref, tok_ref, sems
):
    owners, groups = sent_ref.shape[:2]
    first = [
        pltpu.make_async_copy(ids_hbm, ids_ref, sems.at[0]),
        pltpu.make_async_copy(tok_hbm, tok_ref, sems.at[1]),
    ]
    for copy in first:
        copy.start()
    place = lax.rem(lax.axis_index("tensor"), QUAD)
    moves = []
    for r, out in ((2, chip_ref.at[0]), (3, chip_ref.at[1]), (1, core_ref), (0, keep_ref)):
        for j in range(groups):
            owner = QUAD * j + jnp.bitwise_xor(place, r)
            src = pl.ds(pl.multiple_of(owner * LANES, LANES), LANES)
            dst = pl.ds(j * LANES, LANES)
            for e in range(LOCAL):
                moves.append((w_in_hbm.at[e, :, :, src], out.at[pl.ds(2 * e, 2), :, dst]))
            moves.append((w_down_hbm.at[:, :, src], out.at[pl.ds(2 * LOCAL, LOCAL), :, dst]))
    rest = [pltpu.make_async_copy(a, b, sems.at[2 + i]) for i, (a, b) in enumerate(moves)]
    for copy in rest:
        copy.start()
    for copy in first:
        copy.wait()

    toks = tok_ref.shape[0]
    _, across = slot_rows(ids_ref[...])
    pairs = across.shape[1]
    token_of = onehot(iota((pairs, toks), 0) // (pairs // toks) == iota((pairs, toks), 1))
    values = jnp.dot(token_of, tok_ref[...], preferred_element_type=jnp.float32)
    placing = onehot(iota((owners * TILE, pairs), 0) == across)
    values = jnp.dot(placing, values.astype(jnp.bfloat16), preferred_element_type=jnp.float32)
    values = values.reshape(owners, TILE, LANES)[:, :SLOTS].astype(jnp.bfloat16)
    for m in range(groups):
        sent_ref[:, m] = values
    for copy in rest:
        copy.wait()


def table_kernel(ids_ref, gates_ref, dense_ref, spread_ref, picking_ref, shares_ref):
    rows, held = dense_ref.shape
    owners = held // TILE
    dense_ref[...] = onehot(iota((rows, held), 0) == dense_row((1, held), 1, owners))
    spread_ref[...] = onehot(iota((held, rows), 1) == dense_row((held, 1), 0, owners))
    down, _ = slot_rows(ids_ref[...])
    picking_ref[...] = onehot(down == iota(picking_ref.shape, 1))
    gates = gates_ref[...]
    shares = pair_column(gates / jnp.sum(gates, axis=0, keepdims=True))
    shares_ref[...] = jnp.broadcast_to(shares, shares_ref.shape)


def preact(w_ref, x):
    _, hid, depth = w_ref.shape
    rows = x.shape[0]
    both = lax.dot_general(
        w_ref[: 2 * LOCAL].reshape(2 * LOCAL * hid, depth),
        x,
        (((1,), (1,)), ((), ())),
        preferred_element_type=jnp.float32,
    )
    first = iota((2 * hid, rows), 1) < rows // LOCAL
    return jnp.where(first, both[: 2 * hid], both[2 * hid :])


def up_kernel(x_ref, dense_ref, w1_ref, w3_ref, dense_x_ref, send_ref):
    groups = x_ref.shape[1]
    x = jnp.concatenate(
        [padded(x_ref[:, m].astype(jnp.float32)).astype(jnp.bfloat16) for m in range(groups)],
        axis=1,
    )
    x = jnp.dot(dense_ref[...], x, preferred_element_type=jnp.float32).astype(jnp.bfloat16)
    dense_x_ref[...] = x
    send_ref[0] = preact(w1_ref, x).astype(jnp.bfloat16)
    send_ref[1] = preact(w3_ref, x).astype(jnp.bfloat16)


def own_kernel(x_ref, w0_ref, w2_ref, own_ref):
    x = x_ref[...]
    own_ref[0] = preact(w0_ref, x)
    own_ref[1] = preact(w2_ref.at[0], x)


def add_kernel(own_ref, got_ref, sum_ref, send_ref):
    total = own_ref[...] + got_ref[...].astype(jnp.float32)
    sum_ref[...] = total
    send_ref[...] = total.astype(jnp.bfloat16)


def act_kernel(own_ref, got_ref, out_ref):
    hid = out_ref.shape[1]
    for r in range(2):
        pre = own_ref[r] + got_ref[1 - r].astype(jnp.float32)
        gate, up = pre[:hid], pre[hid:]
        out_ref[r] = (gate / (1.0 + jnp.exp(-gate)) * up).astype(jnp.bfloat16)


def down_kernel(own_ref, got_ref, spread_ref, w0_ref, w1_ref, w2_ref, w3_ref, out_ref):
    owners, groups = out_ref.shape[:2]
    hid, rows = own_ref.shape[1:]
    first = iota((hid, rows), 1) < rows // LOCAL
    values, weights = [], []
    for r, w_ref in enumerate((w0_ref, w1_ref, w2_ref.at[0], w3_ref)):
        hidden = (got_ref if r % 2 else own_ref)[r // 2].astype(jnp.float32)
        values += [jnp.where(first, hidden, 0.0), jnp.where(first, 0.0, hidden)]
        weights.append(w_ref[2 * LOCAL :].reshape(LOCAL * hid, groups * LANES))
    values = jnp.concatenate(values, axis=0).astype(jnp.bfloat16)
    weights = jnp.concatenate(weights, axis=0)
    values = lax.dot_general(
        spread_ref[...], values, (((1,), (1,)), ((), ())), preferred_element_type=jnp.float32
    ).astype(jnp.bfloat16)
    out = jnp.dot(values, weights, preferred_element_type=jnp.float32)
    for m in range(groups):
        part = out[:, m * LANES : (m + 1) * LANES]
        out_ref[:, m] = part.reshape(owners, TILE, LANES)[:, :SLOTS].astype(jnp.bfloat16)


def combine_kernel(picking_ref, shares_ref, x_ref, out_ref):
    groups = x_ref.shape[1]
    values = x_ref[:, 0].astype(jnp.float32)
    for m in range(1, groups):
        values = values + x_ref[:, m].astype(jnp.float32)
    values = padded(values).astype(jnp.bfloat16)
    picked = jnp.dot(picking_ref[...], values, preferred_element_type=jnp.float32)
    mixed = jnp.sum(picked.reshape(shares_ref.shape) * shares_ref[...], axis=1)
    out_ref[...] = mixed.astype(jnp.bfloat16)


def call(kernel, shapes, args):
    return pl.pallas_call(
        kernel,
        out_shape=shapes,
        in_specs=[VMEM] * len(args),
        out_specs=jax.tree.map(lambda _: VMEM, shapes),
        compiler_params=pltpu.CompilerParams(vmem_limit_bytes=48 * MIB),
    )(*args)


def start(ids, tokens, w_in, w_down, sent, part):
    pair = jax.ShapeDtypeStruct((2, *part.shape), part.dtype)
    copies = 2 + 3 * QUAD * (w_in.shape[3] // (QUAD * LANES))
    return pl.pallas_call(
        start_kernel,
        out_shape=[sent, part, part, pair],
        in_specs=[ANY] * 4,
        out_specs=[VMEM, ANY, ANY, ANY],
        scratch_shapes=[
            pltpu.VMEM(ids.shape, ids.dtype),
            pltpu.VMEM(tokens.shape, tokens.dtype),
            pltpu.SemaphoreType.DMA((copies,)),
        ],
        compiler_params=pltpu.CompilerParams(vmem_limit_bytes=60 * MIB),
    )(ids, tokens, w_in, w_down)


def shards(tokens, expert_ids, gate_scores, w_in, w_down):
    n_expert, n_tensor = lax.axis_size("expert"), lax.axis_size("tensor")
    groups = n_tensor // QUAD
    toks = tokens.shape[0]
    _, _, hid, _ = w_in.shape
    rows = n_expert * SLOTS
    ids, gates = expert_ids.T, gate_scores.T
    peers = [
        [e * n_tensor + QUAD * m + q for e in range(n_expert) for m in range(groups)]
        for q in range(QUAD)
    ]
    held = (n_expert, groups, SLOTS, LANES)

    def bf16(*shape):
        return jax.ShapeDtypeStruct(shape, jnp.bfloat16)

    def f32(*shape):
        return jax.ShapeDtypeStruct(shape, jnp.float32)

    def exchange(value, r):
        return lax.ppermute(value, "tensor", [(i, i ^ r) for i in range(n_tensor)])

    def deal(value):
        value = value.reshape(n_expert * groups, SLOTS, LANES)
        value = lax.all_to_all(
            value, ("expert", "tensor"), 0, 0, tiled=True, axis_index_groups=peers
        )
        return value.reshape(held)

    part = bf16(3 * LOCAL, hid, groups * LANES)
    sent, keep, core, chip = start(ids, tokens, w_in, w_down, bf16(*held), part)
    chip, core = exchange(chip, 2), exchange(core, 1)
    weights = (keep, core, chip, exchange(chip[1], 1))

    ids, gates, core = lax.optimization_barrier((ids, gates, core))
    top, slot_table = ids.shape[0], n_expert * TILE
    dense, spread, picking, shares = call(
        table_kernel,
        [
            bf16(rows, slot_table),
            bf16(slot_table, rows),
            bf16(top * toks, slot_table),
            f32(toks, top, LANES),
        ],
        (ids, gates),
    )
    pair = (2, 2 * hid, rows)
    x, send = call(
        up_kernel,
        [bf16(rows, groups * LANES), bf16(*pair)],
        (deal(sent), dense, weights[1], weights[3]),
    )
    got = exchange(send, 1)
    own = call(own_kernel, f32(*pair), (x, weights[0], weights[2]))
    own, send = call(add_kernel, [f32(*pair), bf16(*pair)], (own, got))
    hidden = call(act_kernel, bf16(2, hid, rows), (own, exchange(send, 2)))
    out = call(down_kernel, bf16(*held), (hidden, exchange(hidden, 1), spread, *weights))
    return call(combine_kernel, bf16(toks, LANES), (picking, shares, deal(out)))


def solution(mesh):
    in_specs = (
        P("expert", "tensor"),
        P("expert", None),
        P("expert", None),
        P("expert", None, "tensor", None),
        P("expert", "tensor", None),
    )
    out_specs = P("expert", "tensor")
    return jax.shard_map(shards, mesh=mesh, in_specs=in_specs, out_specs=out_specs, check_vma=False)
```

time: 117 us -> 143 us (1.22)
  Pallas kernels: 4.26 us -> 41.4 us
  blocking collectives: 39.1 us -> 31.2 us
  waiting for transfers between devices: 26.6 us -> 25 us
    pallas_call x0 -> x1, Pallas kernels: none -> 38.1 us  [start(): pl.pallas_call(start_kernel, out_shape=[sent, part, part, pair], in_specs...]
    ppermute x6, waiting for transfers between devices: 26.6 us -> 7.76 us  [exchange(): return lax.ppermute(value, 'tensor', [(i, i ^ r) for i in range(n_tensor)])]
    all_to_all x1, waiting for transfers between devices: 0.01 us -> 17.3 us  [deal(): lax.all_to_all(value, ('expert', 'tensor'), 0, 0, tiled=True, axis_index_...]
    all_to_all x1, blocking collectives: 39.1 us -> 31.2 us  [deal(): lax.all_to_all(value, ('expert', 'tensor'), 0, 0, tiled=True, axis_index_...]
  transfers between devices with their start and end apart: 7 -> 7, of which waited for: 5 -> 4; matrix products, arithmetic and copies ran while one was open for 0% -> 0% of each run, Pallas kernels for 0% -> 1%
where the time goes in v7:
time: 143 us
  starting transfers between devices  44.9 us (31%)
  Pallas kernels  41.4 us (29%)
  blocking collectives  31.2 us (22%)
  waiting for transfers between devices  25 us (17%)
    pallas_call x1, Pallas kernels, start(): pl.pallas_call(start_kernel, out_shape=[sent, part, part, pair], in_specs...  38.1 us
    all_to_all x1, blocking collectives, deal(): lax.all_to_all(value, ('expert', 'tensor'), 0, 0, tiled=True, axis_index_...  31.2 us
    all_to_all x1, starting transfers between devices, deal(): lax.all_to_all(value, ('expert', 'tensor'), 0, 0, tiled=True, axis_index_...  29.3 us
    all_to_all x1, waiting for transfers between devices, deal(): lax.all_to_all(value, ('expert', 'tensor'), 0, 0, tiled=True, axis_index_...  17.3 us
    ppermute x6, starting transfers between devices, exchange(): return lax.ppermute(value, 'tensor', [(i, i ^ r) for i in range(n_tensor)])  15.5 us
    ppermute x6, waiting for transfers between devices, exchange(): return lax.ppermute(value, 'tensor', [(i, i ^ r) for i in range(n_tensor)])  7.76 us
    pallas_call x7, Pallas kernels, call(): pl.pallas_call(kernel, out_shape=shapes, in_specs=[VMEM] * len(args), out...  3.26 us
  transfers between devices with their start and end apart: 7, of which 4 were waited for; matrix products, arithmetic and copies ran while one was open for 0% of the time, Pallas kernels for 1%

profile of v7, /device:TPU:4, one launch (start us, length us, event | category | flops | bytes accessed | tf_op | source)
XLA Modules:
  0.0 142.7 jit_solution(3307186052328869032)
XLA Ops:
  0.0 38.1 %shard_map.55 = (bf16[64,4,6,128]{3,2,1,0:T(8,128)(2,1)}, bf16[6,48,512]{2,1,0:T(8,128)(2,1)}, bf16[6,48,512]{2,1,0:T(8,128)(2,1)}, bf16[2,6,48,512]{3,2,1,0:T(8,128)(2,1)}) custom-call(s32[8,16]{1,0:T(8,128)} %bitcast.11, bf16[16,128]{1,0:T(8,128)(2,1)} %tok_hbm.1, bf16[2,2,48,2048]{3,2,1,0:T(8,128)(2,1)} %w_in_hbm.1, bf16[2,48,2048]{2,1,0:T(8,128)(2,1)} %w_down_hbm.1), custom_call_target="tpu_custom_call" | custom-call | tf_op jit(solution)/shard_map/pallas_call | solution.py:204
  38.1 5.2 %collective-permute-start.1 = (bf16[2,6,48,512]{3,2,1,0:T(8,128)(2,1)}, bf16[2,6,48,512]{3,2,1,0:T(8,128)(2,1)S(1)}, u32[]{:S(2)}, u32[]{:S(2)}) collective-permute-start(bf16[2,6,48,512]{3,2,1,0:T(8,128)(2,1)} %get-tuple-element.26), channel_id=1, source_target_pairs={{0,2},{1,3},{2,0},{3,1},{4,6},{5,7},{6,4},{7,5},{8,10},{9,11},{10,... | collective-permute-start | bytes 1769480 | tf_op jit(solution)/shard_map/ppermute | solution.py:238
  43.3 0.0 copy-start.3
  43.3 29.3 %all-to-all-start = ((bf16[256,6,128]{2,1,0:T(8,128)(2,1)}), bf16[256,6,128]{2,1,0:T(8,128)(2,1)S(1)}, u32[]{:S(2)}, u32[]{:S(2)}) async-start(bf16[256,6,128]{2,1,0:T(8,128)(2,1)} %bitcast.14), calls=%async_computation | async-start | bytes 1048576 | tf_op jit(solution)/shard_map/all_to_all | solution.py:242
  72.6 0.0 copy-done.3
  72.6 1.9 %collective-permute-start = (bf16[6,48,512]{2,1,0:T(8,128)(2,1)S(1)}, bf16[6,48,512]{2,1,0:T(8,128)(2,1)S(1)}, u32[]{:S(2)}, u32[]{:S(2)}) collective-permute-start(bf16[6,48,512]{2,1,0:T(8,128)(2,1)S(1)} %copy-done.3), channel_id=1, source_target_pairs={{0,1},{1,0},{2,3},{3,2},{4,5},{5,4},{6,7},{7,6},{8,9},{9,8},{10,11... | collective-permute-start | bytes 884744 | tf_op jit(solution)/shard_map/ppermute | solution.py:238
  74.6 0.0 collective-permute-done.1.w2_ref
  74.6 0.0 copy-start.1
  74.6 0.0 copy-start.2
  74.6 2.4 %collective-permute-start.2 = (bf16[6,48,512]{2,1,0:T(8,128)(2,1)S(1)}, bf16[6,48,512]{2,1,0:T(8,128)(2,1)S(1)}, u32[]{:S(2)}, u32[]{:S(2)}) collective-permute-start(bf16[6,48,512]{2,1,0:T(8,128)(2,1)S(1)} %slice_bitcast_fusion), channel_id=1, source_target_pairs={{0,1},{1,0},{2,3},{3,2},{4,5},{5,4},{6,7},{7,6},{8,9},{9,8},{10,11... | collective-permute-start | bytes 884744 | tf_op jit(solution)/shard_map/ppermute | solution.py:238
  77.0 0.0 collective-permute-done.w1_ref
  77.1 0.0 copy-done.1
  77.1 0.0 copy-done.2
  77.1 0.4 shard_map.56
  77.5 17.3 %all-to-all-done = bf16[256,6,128]{2,1,0:T(8,128)(2,1)S(1)} async-done(((bf16[256,6,128]{2,1,0:T(8,128)(2,1)}), bf16[256,6,128]{2,1,0:T(8,128)(2,1)S(1)}, u32[]{:S(2)}, u32[]{:S(2)}) %all-to-all-start) | async-done | bytes 393248 | tf_op jit(solution)/shard_map/all_to_all | solution.py:242
  94.8 0.0 collective-permute-done.2.w3_ref
  94.8 0.0 copy-start
  94.8 0.7 shard_map.57
  95.5 1.9 %collective-permute-start.3 = (bf16[2,96,384]{2,1,0:T(8,128)(2,1)S(1)}, bf16[2,96,384]{2,1,0:T(8,128)(2,1)S(1)}, u32[]{:S(2)}, u32[]{:S(2)}) collective-permute-start(bf16[2,96,384]{2,1,0:T(8,128)(2,1)S(1)} %get-tuple-element.29), channel_id=1, source_target_pairs={{0,1},{1,0},{2,3},{3,2},{4,5},{5,4},{6,7},{7,6},{8,9},{9,8},{10,11... | collective-permute-start | bytes 442376 | tf_op jit(solution)/shard_map/ppermute | solution.py:238
  97.5 0.0 copy-done
  97.5 0.4 shard_map.58.own_ref
  97.9 0.9 collective-permute-done.3.got_ref
  98.8 2.2 %collective-permute-start.4 = (bf16[2,96,384]{2,1,0:T(8,128)(2,1)S(1)}, bf16[2,96,384]{2,1,0:T(8,128)(2,1)S(1)}, u32[]{:S(2)}, u32[]{:S(2)}) collective-permute-start(bf16[2,96,384]{2,1,0:T(8,128)(2,1)S(1)} %get-tuple-element.31), channel_id=1, source_target_pairs={{0,2},{1,3},{2,0},{3,1},{4,6},{5,7},{6,4},{7,5},{8,10},{9,11},{10,... | collective-permute-start | bytes 442376 | tf_op jit(solution)/shard_map/ppermute | solution.py:238
  101.0 5.6 %collective-permute-done.4.got_ref = bf16[2,96,384]{2,1,0:T(8,128)(2,1)S(1)} collective-permute-done((bf16[2,96,384]{2,1,0:T(8,128)(2,1)S(1)}, bf16[2,96,384]{2,1,0:T(8,128)(2,1)S(1)}, u32[]{:S(2)}, u32[]{:S(2)}) %collective-permute-start.4) | collective-permute-done | bytes 147488 | tf_op jit(solution)/shard_map/ppermute | solution.py:238
  106.6 0.1 shard_map.60.own_ref
  106.7 1.9 %collective-permute-start.5 = (bf16[2,48,384]{2,1,0:T(8,128)(2,1)S(1)}, bf16[2,48,384]{2,1,0:T(8,128)(2,1)S(1)}, u32[]{:S(2)}, u32[]{:S(2)}) collective-permute-start(bf16[2,48,384]{2,1,0:T(8,128)(2,1)S(1)} %shard_map.60.own_ref), channel_id=1, source_target_pairs={{0,1},{1,0},{2,3},{3,2},{4,5},{5,4},{6,7},{7,6},{8,9},{9,8},{10,11... | collective-permute-start | bytes 221192 | tf_op jit(solution)/shard_map/ppermute | solution.py:238
  108.6 1.2 collective-permute-done.5.got_ref
  109.9 0.7 shard_map.61
  110.6 31.2 %all_to_all.10 = bf16[256,6,128]{2,1,0:T(8,128)(2,1)S(1)} all-to-all(bf16[256,6,128]{2,1,0:T(8,128)(2,1)S(1)} %bitcast.9), channel_id=1, replica_groups={{0,4,8,12,16,20,24,28,32,36,40,44,48,52,56,60,64,68,72,76,80,84,88,92,9..., dimensions={0} | all-to-all | bytes 786432 | tf_op jit(solution)/shard_map/all_to_all | solution.py:242
  141.8 0.8 shard_map.62
  (2 shorter events, 0.1 us)
Async XLA Ops:
  38.1 36.5 %collective-permute-start.1 = (bf16[2,6,48,512]{3,2,1,0:T(8,128)(2,1)}, bf16[2,6,48,512]{3,2,1,0:T(8,128)(2,1)S(1)}, u32[]{:S(2)}, u32[]{:S(2)}) collective-permute-start(bf16[2,6,48,512]{3,2,1,0:T(8,128)(2,1)} %get-tuple-element.26), channel_id=1, source_target_pairs={{0,2},{1,3},{2,0},{3,1},{4,6},{5,7},{6,4},{7,5},{8,10},{9,11},{10,... | collective-permute-start | bytes 1769480 | tf_op jit(solution)/shard_map/ppermute | solution.py:238
  43.3 29.3 %copy-start.3 = (bf16[6,48,512]{2,1,0:T(8,128)(2,1)S(1)}, bf16[6,48,512]{2,1,0:T(8,128)(2,1)}, u32[]{:S(2)}) copy-start(bf16[6,48,512]{2,1,0:T(8,128)(2,1)} %get-tuple-element.19) | copy-start | bytes 884740
  43.3 51.5 %all-to-all-start = ((bf16[256,6,128]{2,1,0:T(8,128)(2,1)}), bf16[256,6,128]{2,1,0:T(8,128)(2,1)S(1)}, u32[]{:S(2)}, u32[]{:S(2)}) async-start(bf16[256,6,128]{2,1,0:T(8,128)(2,1)} %bitcast.14), calls=%async_computation | async-start | bytes 1048576 | tf_op jit(solution)/shard_map/all_to_all | solution.py:242
  72.6 4.4 %collective-permute-start = (bf16[6,48,512]{2,1,0:T(8,128)(2,1)S(1)}, bf16[6,48,512]{2,1,0:T(8,128)(2,1)S(1)}, u32[]{:S(2)}, u32[]{:S(2)}) collective-permute-start(bf16[6,48,512]{2,1,0:T(8,128)(2,1)S(1)} %copy-done.3), channel_id=1, source_target_pairs={{0,1},{1,0},{2,3},{3,2},{4,5},{5,4},{6,7},{7,6},{8,9},{9,8},{10,11... | collective-permute-start | bytes 884744 | tf_op jit(solution)/shard_map/ppermute | solution.py:238
  74.6 2.5 %copy-start.1 = (s32[16,8]{0,1:T(8,128)S(1)}, s32[16,8]{0,1:T(8,128)}, u32[]{:S(2)}) copy-start(s32[16,8]{0,1:T(8,128)} %param.6) | copy-start | bytes 1540
  74.6 2.5 %copy-start.2 = (f32[16,8]{0,1:T(8,128)S(1)}, f32[16,8]{0,1:T(8,128)}, u32[]{:S(2)}) copy-start(f32[16,8]{0,1:T(8,128)} %param.7) | copy-start | bytes 1540
  74.6 20.2 %collective-permute-start.2 = (bf16[6,48,512]{2,1,0:T(8,128)(2,1)S(1)}, bf16[6,48,512]{2,1,0:T(8,128)(2,1)S(1)}, u32[]{:S(2)}, u32[]{:S(2)}) collective-permute-start(bf16[6,48,512]{2,1,0:T(8,128)(2,1)S(1)} %slice_bitcast_fusion), channel_id=1, source_target_pairs={{0,1},{1,0},{2,3},{3,2},{4,5},{5,4},{6,7},{7,6},{8,9},{9,8},{10,11... | collective-permute-start | bytes 884744 | tf_op jit(solution)/shard_map/ppermute | solution.py:238
  94.8 2.7 %copy-start = (bf16[6,48,512]{2,1,0:T(8,128)(2,1)S(1)}, bf16[6,48,512]{2,1,0:T(8,128)(2,1)}, u32[]{:S(2)}) copy-start(bf16[6,48,512]{2,1,0:T(8,128)(2,1)} %get-tuple-element.28.w0_ref) | copy-start | bytes 884740
  95.5 3.3 %collective-permute-start.3 = (bf16[2,96,384]{2,1,0:T(8,128)(2,1)S(1)}, bf16[2,96,384]{2,1,0:T(8,128)(2,1)S(1)}, u32[]{:S(2)}, u32[]{:S(2)}) collective-permute-start(bf16[2,96,384]{2,1,0:T(8,128)(2,1)S(1)} %get-tuple-element.29), channel_id=1, source_target_pairs={{0,1},{1,0},{2,3},{3,2},{4,5},{5,4},{6,7},{7,6},{8,9},{9,8},{10,11... | collective-permute-start | bytes 442376 | tf_op jit(solution)/shard_map/ppermute | solution.py:238
  98.8 7.8 %collective-permute-start.4 = (bf16[2,96,384]{2,1,0:T(8,128)(2,1)S(1)}, bf16[2,96,384]{2,1,0:T(8,128)(2,1)S(1)}, u32[]{:S(2)}, u32[]{:S(2)}) collective-permute-start(bf16[2,96,384]{2,1,0:T(8,128)(2,1)S(1)} %get-tuple-element.31), channel_id=1, source_target_pairs={{0,2},{1,3},{2,0},{3,1},{4,6},{5,7},{6,4},{7,5},{8,10},{9,11},{10,... | collective-permute-start | bytes 442376 | tf_op jit(solution)/shard_map/ppermute | solution.py:238
  106.7 3.2 %collective-permute-start.5 = (bf16[2,48,384]{2,1,0:T(8,128)(2,1)S(1)}, bf16[2,48,384]{2,1,0:T(8,128)(2,1)S(1)}, u32[]{:S(2)}, u32[]{:S(2)}) collective-permute-start(bf16[2,48,384]{2,1,0:T(8,128)(2,1)S(1)} %shard_map.60.own_ref), channel_id=1, source_target_pairs={{0,1},{1,0},{2,3},{3,2},{4,5},{5,4},{6,7},{7,6},{8,9},{9,8},{10,11... | collective-permute-start | bytes 221192 | tf_op jit(solution)/shard_map/ppermute | solution.py:238

commit v8 on v7

--- a/solution.py
+++ b/solution.py
@@ -60,32 +60,31 @@
     return jnp.concatenate([values, blank], axis=1).reshape(owners * TILE, LANES)
 
 
+def pack(w_in_ref, w_down_ref, out_ref, distance):
+    place = lax.rem(lax.axis_index("tensor"), QUAD)
+    for j in range(out_ref.shape[2] // LANES):
+        owner = QUAD * j + jnp.bitwise_xor(place, distance)
+        src = pl.ds(pl.multiple_of(owner * LANES, LANES), LANES)
+        dst = pl.ds(j * LANES, LANES)
+        for e in range(LOCAL):
+            for g in range(2):
+                out_ref[2 * e + g, :, dst] = w_in_ref[e, g, :, src]
+            out_ref[2 * LOCAL + e, :, dst] = w_down_ref[e, :, src]
+
+
 def start_kernel(
-    ids_hbm, tok_hbm, w_in_hbm, w_down_hbm, sent_ref, keep_ref, core_ref, chip_ref, ids_ref, tok_ref, sems
+    ids_hbm, tok_hbm, w_in_hbm, w_down_hbm, sent_ref, chip_ref, ids_ref, tok_ref, w_in_ref, w_down_ref, sems
 ):
-    owners, groups = sent_ref.shape[:2]
-    first = [
-        pltpu.make_async_copy(ids_hbm, ids_ref, sems.at[0]),
-        pltpu.make_async_copy(tok_hbm, tok_ref, sems.at[1]),
-    ]
-    for copy in first:
+    moves = [(ids_hbm, ids_ref), (tok_hbm, tok_ref)]
+    moves += [(w_in_hbm.at[e], w_in_ref.at[e]) for e in range(LOCAL)]
+    moves += [(w_down_hbm, w_down_ref)]
+    copies = [pltpu.make_async_copy(a, b, sems.at[i]) for i, (a, b) in enumerate(moves)]
+    for copy in copies:
         copy.start()
-    place = lax.rem(lax.axis_index("tensor"), QUAD)
-    moves = []
-    for r, out in ((2, chip_ref.at[0]), (3, chip_ref.at[1]), (1, core_ref), (0, keep_ref)):
-        for j in range(groups):
-            owner = QUAD * j + jnp.bitwise_xor(place, r)
-            src = pl.ds(pl.multiple_of(owner * LANES, LANES), LANES)
-            dst = pl.ds(j * LANES, LANES)
-            for e in range(LOCAL):
-                moves.append((w_in_hbm.at[e, :, :, src], out.at[pl.ds(2 * e, 2), :, dst]))
-            moves.append((w_down_hbm.at[:, :, src], out.at[pl.ds(2 * LOCAL, LOCAL), :, dst]))
-    rest = [pltpu.make_async_copy(a, b, sems.at[2 + i]) for i, (a, b) in enumerate(moves)]
-    for copy in rest:
-        copy.start()
-    for copy in first:
+    for copy in copies[:2]:
         copy.wait()
 
+    groups, owners = sent_ref.shape[:2]
     toks = tok_ref.shape[0]
     _, across = slot_rows(ids_ref[...])
     pairs = across.shape[1]
@@ -95,9 +94,17 @@
     values = jnp.dot(placing, values.astype(jnp.bfloat16), preferred_element_type=jnp.float32)
     values = values.reshape(owners, TILE, LANES)[:, :SLOTS].astype(jnp.bfloat16)
     for m in range(groups):
-        sent_ref[:, m] = values
-    for copy in rest:
+        sent_ref[m] = values
+
+    for copy in copies[2:]:
         copy.wait()
+    pack(w_in_ref, w_down_ref, chip_ref.at[0], 2)
+    pack(w_in_ref, w_down_ref, chip_ref.at[1], 3)
+
+
+def pack_kernel(w_in_ref, w_down_ref, keep_ref, core_ref):
+    pack(w_in_ref, w_down_ref, keep_ref, 0)
+    pack(w_in_ref, w_down_ref, core_ref, 1)
 
 
 def table_kernel(ids_ref, gates_ref, dense_ref, spread_ref, picking_ref, shares_ref):
@@ -126,9 +133,9 @@
 
 
 def up_kernel(x_ref, dense_ref, w1_ref, w3_ref, dense_x_ref, send_ref):
-    groups = x_ref.shape[1]
+    groups = x_ref.shape[0]
     x = jnp.concatenate(
-        [padded(x_ref[:, m].astype(jnp.float32)).astype(jnp.bfloat16) for m in range(groups)],
+        [padded(x_ref[m].astype(jnp.float32)).astype(jnp.bfloat16) for m in range(groups)],
         axis=1,
     )
     x = jnp.dot(dense_ref[...], x, preferred_element_type=jnp.float32).astype(jnp.bfloat16)
@@ -158,7 +165,7 @@
 
 
 def down_kernel(own_ref, got_ref, spread_ref, w0_ref, w1_ref, w2_ref, w3_ref, out_ref):
-    owners, groups = out_ref.shape[:2]
+    groups, owners = out_ref.shape[:2]
     hid, rows = own_ref.shape[1:]
     first = iota((hid, rows), 1) < rows // LOCAL
     values, weights = [], []
@@ -174,14 +181,14 @@
     out = jnp.dot(values, weights, preferred_element_type=jnp.float32)
     for m in range(groups):
         part = out[:, m * LANES : (m + 1) * LANES]
-        out_ref[:, m] = part.reshape(owners, TILE, LANES)[:, :SLOTS].astype(jnp.bfloat16)
+        out_ref[m] = part.reshape(owners, TILE, LANES)[:, :SLOTS].astype(jnp.bfloat16)
 
 
 def combine_kernel(picking_ref, shares_ref, x_ref, out_ref):
-    groups = x_ref.shape[1]
-    values = x_ref[:, 0].astype(jnp.float32)
+    groups = x_ref.shape[0]
+    values = x_ref[0].astype(jnp.float32)
     for m in range(1, groups):
-        values = values + x_ref[:, m].astype(jnp.float32)
+        values = values + x_ref[m].astype(jnp.float32)
     values = padded(values).astype(jnp.bfloat16)
     picked = jnp.dot(picking_ref[...], values, preferred_element_type=jnp.float32)
     mixed = jnp.sum(picked.reshape(shares_ref.shape) * shares_ref[...], axis=1)
@@ -198,21 +205,16 @@
     )(*args)
 
 
-def start(ids, tokens, w_in, w_down, sent, part):
-    pair = jax.ShapeDtypeStruct((2, *part.shape), part.dtype)
-    copies = 2 + 3 * QUAD * (w_in.shape[3] // (QUAD * LANES))
+def start(args, shapes):
     return pl.pallas_call(
         start_kernel,
-        out_shape=[sent, part, part, pair],
-        in_specs=[ANY] * 4,
-        out_specs=[VMEM, ANY, ANY, ANY],
-        scratch_shapes=[
-            pltpu.VMEM(ids.shape, ids.dtype),
-            pltpu.VMEM(tokens.shape, tokens.dtype),
-            pltpu.SemaphoreType.DMA((copies,)),
-        ],
+        out_shape=shapes,
+        in_specs=[ANY] * len(args),
+        out_specs=[VMEM] * len(shapes),
+        scratch_shapes=[pltpu.VMEM(a.shape, a.dtype) for a in args]
+        + [pltpu.SemaphoreType.DMA((3 + LOCAL,))],
         compiler_params=pltpu.CompilerParams(vmem_limit_bytes=60 * MIB),
-    )(ids, tokens, w_in, w_down)
+    )(*args)
 
 
 def shards(tokens, expert_ids, gate_scores, w_in, w_down):
@@ -223,10 +225,10 @@
     rows = n_expert * SLOTS
     ids, gates = expert_ids.T, gate_scores.T
     peers = [
-        [e * n_tensor + QUAD * m + q for e in range(n_expert) for m in range(groups)]
+        [e * n_tensor + QUAD * m + q for m in range(groups) for e in range(n_expert)]
         for q in range(QUAD)
     ]
-    held = (n_expert, groups, SLOTS, LANES)
+    held = (groups, n_expert, SLOTS, LANES)
 
     def bf16(*shape):
         return jax.ShapeDtypeStruct(shape, jnp.bfloat16)
@@ -245,8 +247,10 @@
         return value.reshape(held)
 
     part = bf16(3 * LOCAL, hid, groups * LANES)
-    sent, keep, core, chip = start(ids, tokens, w_in, w_down, bf16(*held), part)
-    chip, core = exchange(chip, 2), exchange(core, 1)
+    sent, chip = start((ids, tokens, w_in, w_down), [bf16(*held), bf16(2, *part.shape)])
+    chip, w_in, w_down = lax.optimization_barrier((exchange(chip, 2), w_in, w_down))
+    keep, core = call(pack_kernel, [part, part], (w_in, w_down))
+    core = exchange(core, 1)
     weights = (keep, core, chip, exchange(chip[1], 1))
 
     ids, gates, core = lax.optimization_barrier((ids, gates, core))

time: 143 us -> 109 us (0.76)
  the two profiles are of different devices: /device:TPU:4 before, /device:TPU:2 now
where the time goes in v8:
time: 109 us; the launch traced here: 108 us
  starting transfers between devices  44.5 us (41%)
  blocking collectives  31.8 us (29%)
  waiting for transfers between devices  25.7 us (24%)
  Pallas kernels  5.79 us (5%)
    all_to_all x1, blocking collectives, deal(): lax.all_to_all(value, ('expert', 'tensor'), 0, 0, tiled=True, axis_index_...  31.8 us
    all_to_all x1, starting transfers between devices, deal(): lax.all_to_all(value, ('expert', 'tensor'), 0, 0, tiled=True, axis_index_...  28.9 us
    all_to_all x1, waiting for transfers between devices, deal(): lax.all_to_all(value, ('expert', 'tensor'), 0, 0, tiled=True, axis_index_...  17.9 us
    ppermute x6, starting transfers between devices, exchange(): return lax.ppermute(value, 'tensor', [(i, i ^ r) for i in range(n_tensor)])  15.6 us
    ppermute x6, waiting for transfers between devices, exchange(): return lax.ppermute(value, 'tensor', [(i, i ^ r) for i in range(n_tensor)])  7.81 us
    pallas_call x8, Pallas kernels, call(): pl.pallas_call(kernel, out_shape=shapes, in_specs=[VMEM] * len(args), out...  3.44 us
    pallas_call x1, Pallas kernels, start(): pl.pallas_call(start_kernel, out_shape=shapes, in_specs=[ANY] * len(args)...  2.35 us
  transfers between devices with their start and end apart: 7, of which 4 were waited for; matrix products, arithmetic and copies ran while one was open for 0% of the time, Pallas kernels for 1%

profile of v8, /device:TPU:2, one launch (start us, length us, event | category | flops | bytes accessed | tf_op | source)
XLA Modules:
  0.0 108.1 jit_solution(11621037688478700112)
XLA Ops:
  0.0 0.0 copy-start.1
  0.0 2.3 %shard_map.55 = (bf16[4,64,6,128]{3,2,1,0:T(8,128)(2,1)}, bf16[2,6,48,512]{3,2,1,0:T(8,128)(2,1)}) custom-call(s32[8,16]{1,0:T(8,128)} %bitcast.11, bf16[16,128]{1,0:T(8,128)(2,1)} %tok_hbm.1, bf16[2,2,48,2048]{3,2,1,0:T(8,128)(2,1)} %w_in_ref, bf16[2,48,2048]{2,1,0:T(8,128)(2,1)} %w_down_ref), custom_call_target="tpu_custom_call" | custom-call | tf_op jit(solution)/shard_map/pallas_call | solution.py:209
  2.4 0.0 copy-start
  2.4 5.3 %collective-permute-start = (bf16[2,6,48,512]{3,2,1,0:T(8,128)(2,1)}, bf16[2,6,48,512]{3,2,1,0:T(8,128)(2,1)S(1)}, u32[]{:S(2)}, u32[]{:S(2)}) collective-permute-start(bf16[2,6,48,512]{3,2,1,0:T(8,128)(2,1)} %get-tuple-element.22), channel_id=1, source_target_pairs={{0,2},{1,3},{2,0},{3,1},{4,6},{5,7},{6,4},{7,5},{8,10},{9,11},{10,... | collective-permute-start | bytes 1769480 | tf_op jit(solution)/shard_map/ppermute | solution.py:240
  7.7 28.9 %all-to-all-start = ((bf16[256,6,128]{2,1,0:T(8,128)(2,1)}), bf16[256,6,128]{2,1,0:T(8,128)(2,1)S(1)}, u32[]{:S(2)}, u32[]{:S(2)}) async-start(bf16[256,6,128]{2,1,0:T(8,128)(2,1)} %bitcast.14), calls=%async_computation | async-start | bytes 1048576 | tf_op jit(solution)/shard_map/all_to_all | solution.py:244
  36.6 0.0 collective-permute-done.w2_ref
  36.6 0.0 copy-done.1
  36.6 0.0 copy-done
  36.6 0.2 shard_map.56
  36.8 1.9 %collective-permute-start.1 = (bf16[6,48,512]{2,1,0:T(8,128)(2,1)S(1)}, bf16[6,48,512]{2,1,0:T(8,128)(2,1)S(1)}, u32[]{:S(2)}, u32[]{:S(2)}) collective-permute-start(bf16[6,48,512]{2,1,0:T(8,128)(2,1)S(1)} %get-tuple-element.25), channel_id=1, source_target_pairs={{0,1},{1,0},{2,3},{3,2},{4,5},{5,4},{6,7},{7,6},{8,9},{9,8},{10,11... | collective-permute-start | bytes 884744 | tf_op jit(solution)/shard_map/ppermute | solution.py:240
  38.7 0.0 copy-start.2
  38.7 0.0 copy-start.3
  38.8 2.4 %collective-permute-start.2 = (bf16[6,48,512]{2,1,0:T(8,128)(2,1)S(1)}, bf16[6,48,512]{2,1,0:T(8,128)(2,1)S(1)}, u32[]{:S(2)}, u32[]{:S(2)}) collective-permute-start(bf16[6,48,512]{2,1,0:T(8,128)(2,1)S(1)} %slice_bitcast_fusion), channel_id=1, source_target_pairs={{0,1},{1,0},{2,3},{3,2},{4,5},{5,4},{6,7},{7,6},{8,9},{9,8},{10,11... | collective-permute-start | bytes 884744 | tf_op jit(solution)/shard_map/ppermute | solution.py:240
  41.2 0.0 collective-permute-done.1.w1_ref
  41.2 0.0 copy-done.2
  41.2 0.0 copy-done.3
  41.2 0.4 shard_map.57
  41.7 17.9 %all-to-all-done = bf16[256,6,128]{2,1,0:T(8,128)(2,1)S(1)} async-done(((bf16[256,6,128]{2,1,0:T(8,128)(2,1)}), bf16[256,6,128]{2,1,0:T(8,128)(2,1)S(1)}, u32[]{:S(2)}, u32[]{:S(2)}) %all-to-all-start) | async-done | bytes 393248 | tf_op jit(solution)/shard_map/all_to_all | solution.py:244
  59.6 0.0 collective-permute-done.2.w3_ref
  59.6 0.7 shard_map.58
  60.3 1.9 %collective-permute-start.3 = (bf16[2,96,384]{2,1,0:T(8,128)(2,1)S(1)}, bf16[2,96,384]{2,1,0:T(8,128)(2,1)S(1)}, u32[]{:S(2)}, u32[]{:S(2)}) collective-permute-start(bf16[2,96,384]{2,1,0:T(8,128)(2,1)S(1)} %get-tuple-element.35), channel_id=1, source_target_pairs={{0,1},{1,0},{2,3},{3,2},{4,5},{5,4},{6,7},{7,6},{8,9},{9,8},{10,11... | collective-permute-start | bytes 442376 | tf_op jit(solution)/shard_map/ppermute | solution.py:240
  62.3 0.4 shard_map.59.own_ref
  62.7 0.9 collective-permute-done.3.got_ref
  63.7 2.1 %collective-permute-start.4 = (bf16[2,96,384]{2,1,0:T(8,128)(2,1)S(1)}, bf16[2,96,384]{2,1,0:T(8,128)(2,1)S(1)}, u32[]{:S(2)}, u32[]{:S(2)}) collective-permute-start(bf16[2,96,384]{2,1,0:T(8,128)(2,1)S(1)} %get-tuple-element.37), channel_id=1, source_target_pairs={{0,2},{1,3},{2,0},{3,1},{4,6},{5,7},{6,4},{7,5},{8,10},{9,11},{10,... | collective-permute-start | bytes 442376 | tf_op jit(solution)/shard_map/ppermute | solution.py:240
  65.8 5.6 %collective-permute-done.4.got_ref = bf16[2,96,384]{2,1,0:T(8,128)(2,1)S(1)} collective-permute-done((bf16[2,96,384]{2,1,0:T(8,128)(2,1)S(1)}, bf16[2,96,384]{2,1,0:T(8,128)(2,1)S(1)}, u32[]{:S(2)}, u32[]{:S(2)}) %collective-permute-start.4) | collective-permute-done | bytes 147488 | tf_op jit(solution)/shard_map/ppermute | solution.py:240
  71.4 0.1 shard_map.61.own_ref
  71.5 1.9 %collective-permute-start.5 = (bf16[2,48,384]{2,1,0:T(8,128)(2,1)S(1)}, bf16[2,48,384]{2,1,0:T(8,128)(2,1)S(1)}, u32[]{:S(2)}, u32[]{:S(2)}) collective-permute-start(bf16[2,48,384]{2,1,0:T(8,128)(2,1)S(1)} %shard_map.61.own_ref), channel_id=1, source_target_pairs={{0,1},{1,0},{2,3},{3,2},{4,5},{5,4},{6,7},{7,6},{8,9},{9,8},{10,11... | collective-permute-start | bytes 221192 | tf_op jit(solution)/shard_map/ppermute | solution.py:240
  73.5 1.2 %collective-permute-done.5.got_ref = bf16[2,48,384]{2,1,0:T(8,128)(2,1)S(1)} collective-permute-done((bf16[2,48,384]{2,1,0:T(8,128)(2,1)S(1)}, bf16[2,48,384]{2,1,0:T(8,128)(2,1)S(1)}, u32[]{:S(2)}, u32[]{:S(2)}) %collective-permute-start.5) | collective-permute-done | bytes 73760 | tf_op jit(solution)/shard_map/ppermute | solution.py:240
  74.7 0.7 shard_map.62
  75.4 31.8 %all_to_all.10 = bf16[256,6,128]{2,1,0:T(8,128)(2,1)S(1)} all-to-all(bf16[256,6,128]{2,1,0:T(8,128)(2,1)S(1)} %bitcast.9), channel_id=1, replica_groups={{0,16,32,48,64,80,96,112,128,144,160,176,192,208,224,240,256,272,288,30..., dimensions={0} | all-to-all | bytes 786432 | tf_op jit(solution)/shard_map/all_to_all | solution.py:244
  107.2 0.8 shard_map.63
  (2 shorter events, 0.1 us)
Async XLA Ops:
  0.0 36.6 %copy-start.1 = (bf16[2,48,2048]{2,1,0:T(8,128)(2,1)S(1)}, bf16[2,48,2048]{2,1,0:T(8,128)(2,1)}, u32[]{:S(2)}) copy-start(bf16[2,48,2048]{2,1,0:T(8,128)(2,1)} %w_down_ref) | copy-start | bytes 1179652
  2.4 34.3 %copy-start = (bf16[2,2,48,2048]{3,2,1,0:T(8,128)(2,1)S(1)}, bf16[2,2,48,2048]{3,2,1,0:T(8,128)(2,1)}, u32[]{:S(2)}) copy-start(bf16[2,2,48,2048]{3,2,1,0:T(8,128)(2,1)} %w_in_ref) | copy-start | bytes 2359300
  2.4 34.2 %collective-permute-start = (bf16[2,6,48,512]{3,2,1,0:T(8,128)(2,1)}, bf16[2,6,48,512]{3,2,1,0:T(8,128)(2,1)S(1)}, u32[]{:S(2)}, u32[]{:S(2)}) collective-permute-start(bf16[2,6,48,512]{3,2,1,0:T(8,128)(2,1)} %get-tuple-element.22), channel_id=1, source_target_pairs={{0,2},{1,3},{2,0},{3,1},{4,6},{5,7},{6,4},{7,5},{8,10},{9,11},{10,... | collective-permute-start | bytes 1769480 | tf_op jit(solution)/shard_map/ppermute | solution.py:240
  7.7 51.9 %all-to-all-start = ((bf16[256,6,128]{2,1,0:T(8,128)(2,1)}), bf16[256,6,128]{2,1,0:T(8,128)(2,1)S(1)}, u32[]{:S(2)}, u32[]{:S(2)}) async-start(bf16[256,6,128]{2,1,0:T(8,128)(2,1)} %bitcast.14), calls=%async_computation | async-start | bytes 1048576 | tf_op jit(solution)/shard_map/all_to_all | solution.py:244
  36.8 4.4 %collective-permute-start.1 = (bf16[6,48,512]{2,1,0:T(8,128)(2,1)S(1)}, bf16[6,48,512]{2,1,0:T(8,128)(2,1)S(1)}, u32[]{:S(2)}, u32[]{:S(2)}) collective-permute-start(bf16[6,48,512]{2,1,0:T(8,128)(2,1)S(1)} %get-tuple-element.25), channel_id=1, source_target_pairs={{0,1},{1,0},{2,3},{3,2},{4,5},{5,4},{6,7},{7,6},{8,9},{9,8},{10,11... | collective-permute-start | bytes 884744 | tf_op jit(solution)/shard_map/ppermute | solution.py:240
  38.7 2.5 %copy-start.2 = (s32[16,8]{0,1:T(8,128)S(1)}, s32[16,8]{0,1:T(8,128)}, u32[]{:S(2)}) copy-start(s32[16,8]{0,1:T(8,128)} %param.6) | copy-start | bytes 1540
  38.7 2.5 %copy-start.3 = (f32[16,8]{0,1:T(8,128)S(1)}, f32[16,8]{0,1:T(8,128)}, u32[]{:S(2)}) copy-start(f32[16,8]{0,1:T(8,128)} %param.7) | copy-start | bytes 1540
  38.8 20.8 %collective-permute-start.2 = (bf16[6,48,512]{2,1,0:T(8,128)(2,1)S(1)}, bf16[6,48,512]{2,1,0:T(8,128)(2,1)S(1)}, u32[]{:S(2)}, u32[]{:S(2)}) collective-permute-start(bf16[6,48,512]{2,1,0:T(8,128)(2,1)S(1)} %slice_bitcast_fusion), channel_id=1, source_target_pairs={{0,1},{1,0},{2,3},{3,2},{4,5},{5,4},{6,7},{7,6},{8,9},{9,8},{10,11... | collective-permute-start | bytes 884744 | tf_op jit(solution)/shard_map/ppermute | solution.py:240
  60.3 3.3 %collective-permute-start.3 = (bf16[2,96,384]{2,1,0:T(8,128)(2,1)S(1)}, bf16[2,96,384]{2,1,0:T(8,128)(2,1)S(1)}, u32[]{:S(2)}, u32[]{:S(2)}) collective-permute-start(bf16[2,96,384]{2,1,0:T(8,128)(2,1)S(1)} %get-tuple-element.35), channel_id=1, source_target_pairs={{0,1},{1,0},{2,3},{3,2},{4,5},{5,4},{6,7},{7,6},{8,9},{9,8},{10,11... | collective-permute-start | bytes 442376 | tf_op jit(solution)/shard_map/ppermute | solution.py:240
  63.7 7.8 %collective-permute-start.4 = (bf16[2,96,384]{2,1,0:T(8,128)(2,1)S(1)}, bf16[2,96,384]{2,1,0:T(8,128)(2,1)S(1)}, u32[]{:S(2)}, u32[]{:S(2)}) collective-permute-start(bf16[2,96,384]{2,1,0:T(8,128)(2,1)S(1)} %get-tuple-element.37), channel_id=1, source_target_pairs={{0,2},{1,3},{2,0},{3,1},{4,6},{5,7},{6,4},{7,5},{8,10},{9,11},{10,... | collective-permute-start | bytes 442376 | tf_op jit(solution)/shard_map/ppermute | solution.py:240
  71.5 3.2 %collective-permute-start.5 = (bf16[2,48,384]{2,1,0:T(8,128)(2,1)S(1)}, bf16[2,48,384]{2,1,0:T(8,128)(2,1)S(1)}, u32[]{:S(2)}, u32[]{:S(2)}) collective-permute-start(bf16[2,48,384]{2,1,0:T(8,128)(2,1)S(1)} %shard_map.61.own_ref), channel_id=1, source_target_pairs={{0,1},{1,0},{2,3},{3,2},{4,5},{5,4},{6,7},{7,6},{8,9},{9,8},{10,11... | collective-permute-start | bytes 221192 | tf_op jit(solution)/shard_map/ppermute | solution.py:240

commit v9 on v8

--- a/solution.py
+++ b/solution.py
@@ -84,7 +84,7 @@
     for copy in copies[:2]:
         copy.wait()
 
-    groups, owners = sent_ref.shape[:2]
+    owners, groups = sent_ref.shape[:2]
     toks = tok_ref.shape[0]
     _, across = slot_rows(ids_ref[...])
     pairs = across.shape[1]
@@ -94,7 +94,7 @@
     values = jnp.dot(placing, values.astype(jnp.bfloat16), preferred_element_type=jnp.float32)
     values = values.reshape(owners, TILE, LANES)[:, :SLOTS].astype(jnp.bfloat16)
     for m in range(groups):
-        sent_ref[m] = values
+        sent_ref[:, m] = values
 
     for copy in copies[2:]:
         copy.wait()
@@ -133,9 +133,9 @@
 
 
 def up_kernel(x_ref, dense_ref, w1_ref, w3_ref, dense_x_ref, send_ref):
-    groups = x_ref.shape[0]
+    groups = x_ref.shape[1]
     x = jnp.concatenate(
-        [padded(x_ref[m].astype(jnp.float32)).astype(jnp.bfloat16) for m in range(groups)],
+        [padded(x_ref[:, m].astype(jnp.float32)).astype(jnp.bfloat16) for m in range(groups)],
         axis=1,
     )
     x = jnp.dot(dense_ref[...], x, preferred_element_type=jnp.float32).astype(jnp.bfloat16)
@@ -165,7 +165,7 @@
 
 
 def down_kernel(own_ref, got_ref, spread_ref, w0_ref, w1_ref, w2_ref, w3_ref, out_ref):
-    groups, owners = out_ref.shape[:2]
+    owners, groups = out_ref.shape[:2]
     hid, rows = own_ref.shape[1:]
     first = iota((hid, rows), 1) < rows // LOCAL
     values, weights = [], []
@@ -181,14 +181,14 @@
     out = jnp.dot(values, weights, preferred_element_type=jnp.float32)
     for m in range(groups):
         part = out[:, m * LANES : (m + 1) * LANES]
-        out_ref[m] = part.reshape(owners, TILE, LANES)[:, :SLOTS].astype(jnp.bfloat16)
+        out_ref[:, m] = part.reshape(owners, TILE, LANES)[:, :SLOTS].astype(jnp.bfloat16)
 
 
 def combine_kernel(picking_ref, shares_ref, x_ref, out_ref):
-    groups = x_ref.shape[0]
-    values = x_ref[0].astype(jnp.float32)
+    groups = x_ref.shape[1]
+    values = x_ref[:, 0].astype(jnp.float32)
     for m in range(1, groups):
-        values = values + x_ref[m].astype(jnp.float32)
+        values = values + x_ref[:, m].astype(jnp.float32)
     values = padded(values).astype(jnp.bfloat16)
     picked = jnp.dot(picking_ref[...], values, preferred_element_type=jnp.float32)
     mixed = jnp.sum(picked.reshape(shares_ref.shape) * shares_ref[...], axis=1)
@@ -225,10 +225,10 @@
     rows = n_expert * SLOTS
     ids, gates = expert_ids.T, gate_scores.T
     peers = [
-        [e * n_tensor + QUAD * m + q for m in range(groups) for e in range(n_expert)]
+        [e * n_tensor + QUAD * m + q for e in range(n_expert) for m in range(groups)]
         for q in range(QUAD)
     ]
-    held = (groups, n_expert, SLOTS, LANES)
+    held = (n_expert, groups, SLOTS, LANES)
 
     def bf16(*shape):
         return jax.ShapeDtypeStruct(shape, jnp.bfloat16)

time: 109 us -> 107 us (0.982)
  the two profiles are of different devices: /device:TPU:2 before, /device:TPU:4 now
where the time goes in v9:
time: 107 us
  starting transfers between devices  44.9 us (42%)
  blocking collectives  31.2 us (29%)
  waiting for transfers between devices  24.8 us (23%)
  Pallas kernels  5.78 us (5%)
    all_to_all x1, blocking collectives, deal(): lax.all_to_all(value, ('expert', 'tensor'), 0, 0, tiled=True, axis_index_...  31.2 us
    all_to_all x1, starting transfers between devices, deal(): lax.all_to_all(value, ('expert', 'tensor'), 0, 0, tiled=True, axis_index_...  29.2 us
    all_to_all x1, waiting for transfers between devices, deal(): lax.all_to_all(value, ('expert', 'tensor'), 0, 0, tiled=True, axis_index_...  17.1 us
    ppermute x6, starting transfers between devices, exchange(): return lax.ppermute(value, 'tensor', [(i, i ^ r) for i in range(n_tensor)])  15.7 us
    ppermute x6, waiting for transfers between devices, exchange(): return lax.ppermute(value, 'tensor', [(i, i ^ r) for i in range(n_tensor)])  7.77 us
    pallas_call x8, Pallas kernels, call(): pl.pallas_call(kernel, out_shape=shapes, in_specs=[VMEM] * len(args), out...  3.43 us
    pallas_call x1, Pallas kernels, start(): pl.pallas_call(start_kernel, out_shape=shapes, in_specs=[ANY] * len(args)...  2.35 us
  transfers between devices with their start and end apart: 7, of which 4 were waited for; matrix products, arithmetic and copies ran while one was open for 0% of the time, Pallas kernels for 1%

profile of v9, /device:TPU:4, one launch (start us, length us, event | category | flops | bytes accessed | tf_op | source)
XLA Modules:
  0.0 106.9 jit_solution(12252325432861954451)
XLA Ops:
  0.0 0.0 copy-start.1
  0.0 2.3 %shard_map.55 = (bf16[64,4,6,128]{3,2,1,0:T(8,128)(2,1)}, bf16[2,6,48,512]{3,2,1,0:T(8,128)(2,1)}) custom-call(s32[8,16]{1,0:T(8,128)} %bitcast.11, bf16[16,128]{1,0:T(8,128)(2,1)} %tok_hbm.1, bf16[2,2,48,2048]{3,2,1,0:T(8,128)(2,1)} %w_in_ref, bf16[2,48,2048]{2,1,0:T(8,128)(2,1)} %w_down_ref), custom_call_target="tpu_custom_call" | custom-call | tf_op jit(solution)/shard_map/pallas_call | solution.py:209
  2.4 0.0 copy-start
  2.4 5.3 %collective-permute-start = (bf16[2,6,48,512]{3,2,1,0:T(8,128)(2,1)}, bf16[2,6,48,512]{3,2,1,0:T(8,128)(2,1)S(1)}, u32[]{:S(2)}, u32[]{:S(2)}) collective-permute-start(bf16[2,6,48,512]{3,2,1,0:T(8,128)(2,1)} %get-tuple-element.22), channel_id=1, source_target_pairs={{0,2},{1,3},{2,0},{3,1},{4,6},{5,7},{6,4},{7,5},{8,10},{9,11},{10,... | collective-permute-start | bytes 1769480 | tf_op jit(solution)/shard_map/ppermute | solution.py:240
  7.7 29.2 %all-to-all-start = ((bf16[256,6,128]{2,1,0:T(8,128)(2,1)}), bf16[256,6,128]{2,1,0:T(8,128)(2,1)S(1)}, u32[]{:S(2)}, u32[]{:S(2)}) async-start(bf16[256,6,128]{2,1,0:T(8,128)(2,1)} %bitcast.14), calls=%async_computation | async-start | bytes 1048576 | tf_op jit(solution)/shard_map/all_to_all | solution.py:244
  36.9 0.0 collective-permute-done.w2_ref
  36.9 0.0 copy-done.1
  36.9 0.0 copy-done
  36.9 0.2 shard_map.56
  37.1 1.9 %collective-permute-start.1 = (bf16[6,48,512]{2,1,0:T(8,128)(2,1)S(1)}, bf16[6,48,512]{2,1,0:T(8,128)(2,1)S(1)}, u32[]{:S(2)}, u32[]{:S(2)}) collective-permute-start(bf16[6,48,512]{2,1,0:T(8,128)(2,1)S(1)} %get-tuple-element.25), channel_id=1, source_target_pairs={{0,1},{1,0},{2,3},{3,2},{4,5},{5,4},{6,7},{7,6},{8,9},{9,8},{10,11... | collective-permute-start | bytes 884744 | tf_op jit(solution)/shard_map/ppermute | solution.py:240
  39.0 0.0 copy-start.2
  39.0 0.0 copy-start.3
  39.1 2.4 %collective-permute-start.2 = (bf16[6,48,512]{2,1,0:T(8,128)(2,1)S(1)}, bf16[6,48,512]{2,1,0:T(8,128)(2,1)S(1)}, u32[]{:S(2)}, u32[]{:S(2)}) collective-permute-start(bf16[6,48,512]{2,1,0:T(8,128)(2,1)S(1)} %slice_bitcast_fusion), channel_id=1, source_target_pairs={{0,1},{1,0},{2,3},{3,2},{4,5},{5,4},{6,7},{7,6},{8,9},{9,8},{10,11... | collective-permute-start | bytes 884744 | tf_op jit(solution)/shard_map/ppermute | solution.py:240
  41.5 0.0 collective-permute-done.1.w1_ref
  41.5 0.0 copy-done.2
  41.5 0.0 copy-done.3
  41.5 0.4 shard_map.57
  42.0 17.1 %all-to-all-done = bf16[256,6,128]{2,1,0:T(8,128)(2,1)S(1)} async-done(((bf16[256,6,128]{2,1,0:T(8,128)(2,1)}), bf16[256,6,128]{2,1,0:T(8,128)(2,1)S(1)}, u32[]{:S(2)}, u32[]{:S(2)}) %all-to-all-start) | async-done | bytes 393248 | tf_op jit(solution)/shard_map/all_to_all | solution.py:244
  59.0 0.0 collective-permute-done.2.w3_ref
  59.0 0.7 shard_map.58
  59.8 1.9 %collective-permute-start.3 = (bf16[2,96,384]{2,1,0:T(8,128)(2,1)S(1)}, bf16[2,96,384]{2,1,0:T(8,128)(2,1)S(1)}, u32[]{:S(2)}, u32[]{:S(2)}) collective-permute-start(bf16[2,96,384]{2,1,0:T(8,128)(2,1)S(1)} %get-tuple-element.35), channel_id=1, source_target_pairs={{0,1},{1,0},{2,3},{3,2},{4,5},{5,4},{6,7},{7,6},{8,9},{9,8},{10,11... | collective-permute-start | bytes 442376 | tf_op jit(solution)/shard_map/ppermute | solution.py:240
  61.7 0.4 shard_map.59.own_ref
  62.1 0.9 collective-permute-done.3.got_ref
  63.1 2.2 %collective-permute-start.4 = (bf16[2,96,384]{2,1,0:T(8,128)(2,1)S(1)}, bf16[2,96,384]{2,1,0:T(8,128)(2,1)S(1)}, u32[]{:S(2)}, u32[]{:S(2)}) collective-permute-start(bf16[2,96,384]{2,1,0:T(8,128)(2,1)S(1)} %get-tuple-element.37), channel_id=1, source_target_pairs={{0,2},{1,3},{2,0},{3,1},{4,6},{5,7},{6,4},{7,5},{8,10},{9,11},{10,... | collective-permute-start | bytes 442376 | tf_op jit(solution)/shard_map/ppermute | solution.py:240
  65.3 5.6 %collective-permute-done.4.got_ref = bf16[2,96,384]{2,1,0:T(8,128)(2,1)S(1)} collective-permute-done((bf16[2,96,384]{2,1,0:T(8,128)(2,1)S(1)}, bf16[2,96,384]{2,1,0:T(8,128)(2,1)S(1)}, u32[]{:S(2)}, u32[]{:S(2)}) %collective-permute-start.4) | collective-permute-done | bytes 147488 | tf_op jit(solution)/shard_map/ppermute | solution.py:240
  70.9 0.1 shard_map.61.own_ref
  71.0 1.9 %collective-permute-start.5 = (bf16[2,48,384]{2,1,0:T(8,128)(2,1)S(1)}, bf16[2,48,384]{2,1,0:T(8,128)(2,1)S(1)}, u32[]{:S(2)}, u32[]{:S(2)}) collective-permute-start(bf16[2,48,384]{2,1,0:T(8,128)(2,1)S(1)} %shard_map.61.own_ref), channel_id=1, source_target_pairs={{0,1},{1,0},{2,3},{3,2},{4,5},{5,4},{6,7},{7,6},{8,9},{9,8},{10,11... | collective-permute-start | bytes 221192 | tf_op jit(solution)/shard_map/ppermute | solution.py:240
  72.9 1.2 %collective-permute-done.5.got_ref = bf16[2,48,384]{2,1,0:T(8,128)(2,1)S(1)} collective-permute-done((bf16[2,48,384]{2,1,0:T(8,128)(2,1)S(1)}, bf16[2,48,384]{2,1,0:T(8,128)(2,1)S(1)}, u32[]{:S(2)}, u32[]{:S(2)}) %collective-permute-start.5) | collective-permute-done | bytes 73760 | tf_op jit(solution)/shard_map/ppermute | solution.py:240
  74.1 0.7 shard_map.62
  74.9 31.2 %all_to_all.10 = bf16[256,6,128]{2,1,0:T(8,128)(2,1)S(1)} all-to-all(bf16[256,6,128]{2,1,0:T(8,128)(2,1)S(1)} %bitcast.9), channel_id=1, replica_groups={{0,4,8,12,16,20,24,28,32,36,40,44,48,52,56,60,64,68,72,76,80,84,88,92,9..., dimensions={0} | all-to-all | bytes 786432 | tf_op jit(solution)/shard_map/all_to_all | solution.py:244
  106.1 0.8 shard_map.63
  (2 shorter events, 0.1 us)
Async XLA Ops:
  0.0 36.9 %copy-start.1 = (bf16[2,48,2048]{2,1,0:T(8,128)(2,1)S(1)}, bf16[2,48,2048]{2,1,0:T(8,128)(2,1)}, u32[]{:S(2)}) copy-start(bf16[2,48,2048]{2,1,0:T(8,128)(2,1)} %w_down_ref) | copy-start | bytes 1179652
  2.4 34.6 %copy-start = (bf16[2,2,48,2048]{3,2,1,0:T(8,128)(2,1)S(1)}, bf16[2,2,48,2048]{3,2,1,0:T(8,128)(2,1)}, u32[]{:S(2)}) copy-start(bf16[2,2,48,2048]{3,2,1,0:T(8,128)(2,1)} %w_in_ref) | copy-start | bytes 2359300
  2.4 34.5 %collective-permute-start = (bf16[2,6,48,512]{3,2,1,0:T(8,128)(2,1)}, bf16[2,6,48,512]{3,2,1,0:T(8,128)(2,1)S(1)}, u32[]{:S(2)}, u32[]{:S(2)}) collective-permute-start(bf16[2,6,48,512]{3,2,1,0:T(8,128)(2,1)} %get-tuple-element.22), channel_id=1, source_target_pairs={{0,2},{1,3},{2,0},{3,1},{4,6},{5,7},{6,4},{7,5},{8,10},{9,11},{10,... | collective-permute-start | bytes 1769480 | tf_op jit(solution)/shard_map/ppermute | solution.py:240
  7.7 51.3 %all-to-all-start = ((bf16[256,6,128]{2,1,0:T(8,128)(2,1)}), bf16[256,6,128]{2,1,0:T(8,128)(2,1)S(1)}, u32[]{:S(2)}, u32[]{:S(2)}) async-start(bf16[256,6,128]{2,1,0:T(8,128)(2,1)} %bitcast.14), calls=%async_computation | async-start | bytes 1048576 | tf_op jit(solution)/shard_map/all_to_all | solution.py:244
  37.1 4.4 %collective-permute-start.1 = (bf16[6,48,512]{2,1,0:T(8,128)(2,1)S(1)}, bf16[6,48,512]{2,1,0:T(8,128)(2,1)S(1)}, u32[]{:S(2)}, u32[]{:S(2)}) collective-permute-start(bf16[6,48,512]{2,1,0:T(8,128)(2,1)S(1)} %get-tuple-element.25), channel_id=1, source_target_pairs={{0,1},{1,0},{2,3},{3,2},{4,5},{5,4},{6,7},{7,6},{8,9},{9,8},{10,11... | collective-permute-start | bytes 884744 | tf_op jit(solution)/shard_map/ppermute | solution.py:240
  39.0 2.5 %copy-start.2 = (s32[16,8]{0,1:T(8,128)S(1)}, s32[16,8]{0,1:T(8,128)}, u32[]{:S(2)}) copy-start(s32[16,8]{0,1:T(8,128)} %param.6) | copy-start | bytes 1540
  39.0 2.5 %copy-start.3 = (f32[16,8]{0,1:T(8,128)S(1)}, f32[16,8]{0,1:T(8,128)}, u32[]{:S(2)}) copy-start(f32[16,8]{0,1:T(8,128)} %param.7) | copy-start | bytes 1540
  39.1 20.0 %collective-permute-start.2 = (bf16[6,48,512]{2,1,0:T(8,128)(2,1)S(1)}, bf16[6,48,512]{2,1,0:T(8,128)(2,1)S(1)}, u32[]{:S(2)}, u32[]{:S(2)}) collective-permute-start(bf16[6,48,512]{2,1,0:T(8,128)(2,1)S(1)} %slice_bitcast_fusion), channel_id=1, source_target_pairs={{0,1},{1,0},{2,3},{3,2},{4,5},{5,4},{6,7},{7,6},{8,9},{9,8},{10,11... | collective-permute-start | bytes 884744 | tf_op jit(solution)/shard_map/ppermute | solution.py:240
  59.8 3.3 %collective-permute-start.3 = (bf16[2,96,384]{2,1,0:T(8,128)(2,1)S(1)}, bf16[2,96,384]{2,1,0:T(8,128)(2,1)S(1)}, u32[]{:S(2)}, u32[]{:S(2)}) collective-permute-start(bf16[2,96,384]{2,1,0:T(8,128)(2,1)S(1)} %get-tuple-element.35), channel_id=1, source_target_pairs={{0,1},{1,0},{2,3},{3,2},{4,5},{5,4},{6,7},{7,6},{8,9},{9,8},{10,11... | collective-permute-start | bytes 442376 | tf_op jit(solution)/shard_map/ppermute | solution.py:240
  63.1 7.8 %collective-permute-start.4 = (bf16[2,96,384]{2,1,0:T(8,128)(2,1)S(1)}, bf16[2,96,384]{2,1,0:T(8,128)(2,1)S(1)}, u32[]{:S(2)}, u32[]{:S(2)}) collective-permute-start(bf16[2,96,384]{2,1,0:T(8,128)(2,1)S(1)} %get-tuple-element.37), channel_id=1, source_target_pairs={{0,2},{1,3},{2,0},{3,1},{4,6},{5,7},{6,4},{7,5},{8,10},{9,11},{10,... | collective-permute-start | bytes 442376 | tf_op jit(solution)/shard_map/ppermute | solution.py:240
  71.0 3.2 %collective-permute-start.5 = (bf16[2,48,384]{2,1,0:T(8,128)(2,1)S(1)}, bf16[2,48,384]{2,1,0:T(8,128)(2,1)S(1)}, u32[]{:S(2)}, u32[]{:S(2)}) collective-permute-start(bf16[2,48,384]{2,1,0:T(8,128)(2,1)S(1)} %shard_map.61.own_ref), channel_id=1, source_target_pairs={{0,1},{1,0},{2,3},{3,2},{4,5},{5,4},{6,7},{7,6},{8,9},{9,8},{10,11... | collective-permute-start | bytes 221192 | tf_op jit(solution)/shard_map/ppermute | solution.py:240

commit v10 on v9

--- a/solution.py
+++ b/solution.py
@@ -60,30 +60,15 @@
     return jnp.concatenate([values, blank], axis=1).reshape(owners * TILE, LANES)
 
 
-def pack(w_in_ref, w_down_ref, out_ref, distance):
-    place = lax.rem(lax.axis_index("tensor"), QUAD)
-    for j in range(out_ref.shape[2] // LANES):
-        owner = QUAD * j + jnp.bitwise_xor(place, distance)
-        src = pl.ds(pl.multiple_of(owner * LANES, LANES), LANES)
-        dst = pl.ds(j * LANES, LANES)
-        for e in range(LOCAL):
-            for g in range(2):
-                out_ref[2 * e + g, :, dst] = w_in_ref[e, g, :, src]
-            out_ref[2 * LOCAL + e, :, dst] = w_down_ref[e, :, src]
-
-
-def start_kernel(
-    ids_hbm, tok_hbm, w_in_hbm, w_down_hbm, sent_ref, chip_ref, ids_ref, tok_ref, w_in_ref, w_down_ref, sems
-):
-    moves = [(ids_hbm, ids_ref), (tok_hbm, tok_ref)]
-    moves += [(w_in_hbm.at[e], w_in_ref.at[e]) for e in range(LOCAL)]
-    moves += [(w_down_hbm, w_down_ref)]
-    copies = [pltpu.make_async_copy(a, b, sems.at[i]) for i, (a, b) in enumerate(moves)]
+def start_kernel(ids_hbm, tok_hbm, sent_ref, ids_ref, tok_ref, sems):
+    copies = [
+        pltpu.make_async_copy(ids_hbm, ids_ref, sems.at[0]),
+        pltpu.make_async_copy(tok_hbm, tok_ref, sems.at[1]),
+    ]
     for copy in copies:
         copy.start()
-    for copy in copies[:2]:
+    for copy in copies:
         copy.wait()
-
     owners, groups = sent_ref.shape[:2]
     toks = tok_ref.shape[0]
     _, across = slot_rows(ids_ref[...])
@@ -96,15 +81,21 @@
     for m in range(groups):
         sent_ref[:, m] = values
 
-    for copy in copies[2:]:
-        copy.wait()
-    pack(w_in_ref, w_down_ref, chip_ref.at[0], 2)
-    pack(w_in_ref, w_down_ref, chip_ref.at[1], 3)
-
-
-def pack_kernel(w_in_ref, w_down_ref, keep_ref, core_ref):
-    pack(w_in_ref, w_down_ref, keep_ref, 0)
-    pack(w_in_ref, w_down_ref, core_ref, 1)
+
+def pack_kernel(w_in_ref, w_down_ref, keep_ref, core_ref, up2_ref, up3_ref, down2_ref, down3_ref):
+    place = lax.rem(lax.axis_index("tensor"), QUAD)
+    both = 2 * LOCAL
+    ups = (keep_ref, core_ref, up2_ref, up3_ref)
+    downs = (keep_ref.at[both:], core_ref.at[both:], down2_ref, down3_ref)
+    for r in range(QUAD):
+        for j in range(keep_ref.shape[2] // LANES):
+            owner = QUAD * j + jnp.bitwise_xor(place, r)
+            src = pl.ds(pl.multiple_of(owner * LANES, LANES), LANES)
+            dst = pl.ds(j * LANES, LANES)
+            for e in range(LOCAL):
+                for g in range(2):
+                    ups[r][2 * e + g, :, dst] = w_in_ref[e, g, :, src]
+                downs[r][e, :, dst] = w_down_ref[e, :, src]
 
 
 def table_kernel(ids_ref, gates_ref, dense_ref, spread_ref, picking_ref, shares_ref):
@@ -147,7 +138,7 @@
 def own_kernel(x_ref, w0_ref, w2_ref, own_ref):
     x = x_ref[...]
     own_ref[0] = preact(w0_ref, x)
-    own_ref[1] = preact(w2_ref.at[0], x)
+    own_ref[1] = preact(w2_ref, x)
 
 
 def add_kernel(own_ref, got_ref, sum_ref, send_ref):
@@ -169,10 +160,11 @@
     hid, rows = own_ref.shape[1:]
     first = iota((hid, rows), 1) < rows // LOCAL
     values, weights = [], []
-    for r, w_ref in enumerate((w0_ref, w1_ref, w2_ref.at[0], w3_ref)):
+    both = 2 * LOCAL
+    for r, w_ref in enumerate((w0_ref.at[both:], w1_ref.at[both:], w2_ref, w3_ref)):
         hidden = (got_ref if r % 2 else own_ref)[r // 2].astype(jnp.float32)
         values += [jnp.where(first, hidden, 0.0), jnp.where(first, 0.0, hidden)]
-        weights.append(w_ref[2 * LOCAL :].reshape(LOCAL * hid, groups * LANES))
+        weights.append(w_ref[...].reshape(LOCAL * hid, groups * LANES))
     values = jnp.concatenate(values, axis=0).astype(jnp.bfloat16)
     weights = jnp.concatenate(weights, axis=0)
     values = lax.dot_general(
@@ -205,14 +197,14 @@
     )(*args)
 
 
-def start(args, shapes):
+def start(args, shape):
     return pl.pallas_call(
         start_kernel,
-        out_shape=shapes,
+        out_shape=shape,
         in_specs=[ANY] * len(args),
-        out_specs=[VMEM] * len(shapes),
+        out_specs=VMEM,
         scratch_shapes=[pltpu.VMEM(a.shape, a.dtype) for a in args]
-        + [pltpu.SemaphoreType.DMA((3 + LOCAL,))],
+        + [pltpu.SemaphoreType.DMA((len(args),))],
         compiler_params=pltpu.CompilerParams(vmem_limit_bytes=60 * MIB),
     )(*args)
 
@@ -246,12 +238,14 @@
         )
         return value.reshape(held)
 
-    part = bf16(3 * LOCAL, hid, groups * LANES)
-    sent, chip = start((ids, tokens, w_in, w_down), [bf16(*held), bf16(2, *part.shape)])
-    chip, w_in, w_down = lax.optimization_barrier((exchange(chip, 2), w_in, w_down))
-    keep, core = call(pack_kernel, [part, part], (w_in, w_down))
-    core = exchange(core, 1)
-    weights = (keep, core, chip, exchange(chip[1], 1))
+    sent = start((ids, tokens), bf16(*held))
+    part, wide, deep = [bf16(n * LOCAL, hid, groups * LANES) for n in (3, 2, 1)]
+    keep, core, up2, up3, down2, down3 = call(
+        pack_kernel, [part, part, wide, wide, deep, deep], (w_in, w_down)
+    )
+    up2, up3, core = exchange(up2, 2), exchange(up3, 3), exchange(core, 1)
+    up2, up3, down2, down3 = lax.optimization_barrier((up2, up3, down2, down3))
+    down2, down3 = exchange(down2, 2), exchange(down3, 3)
 
     ids, gates, core = lax.optimization_barrier((ids, gates, core))
     top, slot_table = ids.shape[0], n_expert * TILE
@@ -269,13 +263,13 @@
     x, send = call(
         up_kernel,
         [bf16(rows, groups * LANES), bf16(*pair)],
-        (deal(sent), dense, weights[1], weights[3]),
+        (deal(sent), dense, core, up3),
     )
     got = exchange(send, 1)
-    own = call(own_kernel, f32(*pair), (x, weights[0], weights[2]))
+    own = call(own_kernel, f32(*pair), (x, keep, up2))
     own, send = call(add_kernel, [f32(*pair), bf16(*pair)], (own, got))
     hidden = call(act_kernel, bf16(2, hid, rows), (own, exchange(send, 2)))
-    out = call(down_kernel, bf16(*held), (hidden, exchange(hidden, 1), spread, *weights))
+    out = call(down_kernel, bf16(*held), (hidden, exchange(hidden, 1), spread, keep, core, down2, down3))
     return call(combine_kernel, bf16(toks, LANES), (picking, shares, deal(out)))
 
 

time: 107 us -> 114 us (1.065)
  blocking collectives: 31.2 us -> 38.8 us
  waiting for transfers between devices: 24.8 us -> 17.7 us
  starting transfers between devices: 44.9 us -> 51.2 us
    all_to_all x1, waiting for transfers between devices: 17.1 us -> 0.01 us  [deal(): lax.all_to_all(value, ('expert', 'tensor'), 0, 0, tiled=True, axis_index_...]
    ppermute x6 -> x8, waiting for transfers between devices: 7.77 us -> 17.7 us  [exchange(): return lax.ppermute(value, 'tensor', [(i, i ^ r) for i in range(n_tensor)])]
    all_to_all x1, blocking collectives: 31.2 us -> 38.8 us  [deal(): lax.all_to_all(value, ('expert', 'tensor'), 0, 0, tiled=True, axis_index_...]
    ppermute x6 -> x8, starting transfers between devices: 15.7 us -> 21 us  [exchange(): return lax.ppermute(value, 'tensor', [(i, i ^ r) for i in range(n_tensor)])]
  transfers between devices with their start and end apart: 7 -> 9, of which waited for: 4 -> 5; matrix products, arithmetic and copies ran while one was open for 0% -> 0% of each run, Pallas kernels for 1% -> 1%
where the time goes in v10:
time: 114 us; the launch traced here: 113 us
  starting transfers between devices  51.2 us (45%)
  blocking collectives  38.8 us (34%)
  waiting for transfers between devices  17.7 us (16%)
  Pallas kernels  5.5 us (5%)
    all_to_all x1, blocking collectives, deal(): lax.all_to_all(value, ('expert', 'tensor'), 0, 0, tiled=True, axis_index_...  38.8 us
    all_to_all x1, starting transfers between devices, deal(): lax.all_to_all(value, ('expert', 'tensor'), 0, 0, tiled=True, axis_index_...  30.2 us
    ppermute x8, starting transfers between devices, exchange(): return lax.ppermute(value, 'tensor', [(i, i ^ r) for i in range(n_tensor)])  21 us
    ppermute x8, waiting for transfers between devices, exchange(): return lax.ppermute(value, 'tensor', [(i, i ^ r) for i in range(n_tensor)])  17.7 us
    pallas_call x8, Pallas kernels, call(): pl.pallas_call(kernel, out_shape=shapes, in_specs=[VMEM] * len(args), out...  3.59 us
  transfers between devices with their start and end apart: 9, of which 5 were waited for; matrix products, arithmetic and copies ran while one was open for 0% of the time, Pallas kernels for 1%

profile of v10, /device:TPU:4, one launch (start us, length us, event | category | flops | bytes accessed | tf_op | source)
XLA Modules:
  0.0 113.5 jit_solution(11046752429222101981)
XLA Ops:
  0.0 0.0 copy-start
  0.0 1.9 %shard_map.57 = bf16[64,4,6,128]{3,2,1,0:T(8,128)(2,1)} custom-call(s32[8,16]{1,0:T(8,128)} %bitcast.9, bf16[16,128]{1,0:T(8,128)(2,1)} %tok_hbm.1), custom_call_target="tpu_custom_call" | custom-call | tf_op jit(solution)/shard_map/pallas_call | solution.py:201
  1.9 0.0 copy-start.1
  1.9 30.2 %all-to-all-start = ((bf16[256,6,128]{2,1,0:T(8,128)(2,1)}), bf16[256,6,128]{2,1,0:T(8,128)(2,1)S(1)}, u32[]{:S(2)}, u32[]{:S(2)}) async-start(bf16[256,6,128]{2,1,0:T(8,128)(2,1)} %bitcast.12), calls=%async_computation | async-start | bytes 1048576 | tf_op jit(solution)/shard_map/all_to_all | solution.py:236
  32.2 0.0 copy-done
  32.2 0.0 copy-done.1
  32.2 0.3 shard_map.55
  32.5 1.9 %collective-permute-start = (bf16[6,48,512]{2,1,0:T(8,128)(2,1)S(1)}, bf16[6,48,512]{2,1,0:T(8,128)(2,1)S(1)}, u32[]{:S(2)}, u32[]{:S(2)}) collective-permute-start(bf16[6,48,512]{2,1,0:T(8,128)(2,1)S(1)} %get-tuple-element.26), channel_id=1, source_target_pairs={{0,1},{1,0},{2,3},{3,2},{4,5},{5,4},{6,7},{7,6},{8,9},{9,8},{10,11... | collective-permute-start | bytes 884744 | tf_op jit(solution)/shard_map/ppermute | solution.py:232
  34.4 0.0 copy-start.3
  34.4 0.0 copy-start.2
  34.5 4.3 %collective-permute-start.1 = (bf16[4,48,512]{2,1,0:T(8,128)(2,1)S(1)}, bf16[4,48,512]{2,1,0:T(8,128)(2,1)S(1)}, u32[]{:S(2)}, u32[]{:S(2)}) collective-permute-start(bf16[4,48,512]{2,1,0:T(8,128)(2,1)S(1)} %get-tuple-element.33), channel_id=1, source_target_pairs={{0,2},{1,3},{2,0},{3,1},{4,6},{5,7},{6,4},{7,5},{8,10},{9,11},{10,... | collective-permute-start | bytes 589832 | tf_op jit(solution)/shard_map/ppermute | solution.py:232
  38.8 2.0 %collective-permute-start.2 = (bf16[4,48,512]{2,1,0:T(8,128)(2,1)S(1)}, bf16[4,48,512]{2,1,0:T(8,128)(2,1)S(1)}, u32[]{:S(2)}, u32[]{:S(2)}) collective-permute-start(bf16[4,48,512]{2,1,0:T(8,128)(2,1)S(1)} %get-tuple-element.34), channel_id=1, source_target_pairs={{0,3},{1,2},{2,1},{3,0},{4,7},{5,6},{6,5},{7,4},{8,11},{9,10},{10,... | collective-permute-start | bytes 589832 | tf_op jit(solution)/shard_map/ppermute | solution.py:232
  40.8 10.9 %collective-permute-done.1.w2_ref = bf16[4,48,512]{2,1,0:T(8,128)(2,1)S(1)} collective-permute-done((bf16[4,48,512]{2,1,0:T(8,128)(2,1)S(1)}, bf16[4,48,512]{2,1,0:T(8,128)(2,1)S(1)}, u32[]{:S(2)}, u32[]{:S(2)}) %collective-permute-start.1) | collective-permute-done | bytes 196640 | tf_op jit(solution)/shard_map/ppermute | solution.py:232
  51.7 4.3 %collective-permute-done.2.w3_ref = bf16[4,48,512]{2,1,0:T(8,128)(2,1)S(1)} collective-permute-done((bf16[4,48,512]{2,1,0:T(8,128)(2,1)S(1)}, bf16[4,48,512]{2,1,0:T(8,128)(2,1)S(1)}, u32[]{:S(2)}, u32[]{:S(2)}) %collective-permute-start.2) | collective-permute-done | bytes 196640 | tf_op jit(solution)/shard_map/ppermute | solution.py:232
  55.9 0.0 collective-permute-done.w1_ref
  55.9 0.0 copy-done.3
  55.9 0.0 copy-done.2
  56.0 0.4 shard_map.56
  56.4 0.0 all-to-all-done
  56.4 0.7 shard_map.58
  57.1 2.0 %collective-permute-start.3 = (bf16[2,96,384]{2,1,0:T(8,128)(2,1)S(1)}, bf16[2,96,384]{2,1,0:T(8,128)(2,1)S(1)}, u32[]{:S(2)}, u32[]{:S(2)}) collective-permute-start(bf16[2,96,384]{2,1,0:T(8,128)(2,1)S(1)} %get-tuple-element.41), channel_id=1, source_target_pairs={{0,1},{1,0},{2,3},{3,2},{4,5},{5,4},{6,7},{7,6},{8,9},{9,8},{10,11... | collective-permute-start | bytes 442376 | tf_op jit(solution)/shard_map/ppermute | solution.py:232
  59.2 0.4 shard_map.59.own_ref
  59.6 0.8 collective-permute-done.3.got_ref
  60.5 3.0 %collective-permute-start.4 = (bf16[2,96,384]{2,1,0:T(8,128)(2,1)S(1)}, bf16[2,96,384]{2,1,0:T(8,128)(2,1)S(1)}, u32[]{:S(2)}, u32[]{:S(2)}) collective-permute-start(bf16[2,96,384]{2,1,0:T(8,128)(2,1)S(1)} %get-tuple-element.43), channel_id=1, source_target_pairs={{0,2},{1,3},{2,0},{3,1},{4,6},{5,7},{6,4},{7,5},{8,10},{9,11},{10,... | collective-permute-start | bytes 442376 | tf_op jit(solution)/shard_map/ppermute | solution.py:232
  63.5 2.8 %collective-permute-start.6 = (bf16[2,48,512]{2,1,0:T(8,128)(2,1)S(1)}, bf16[2,48,512]{2,1,0:T(8,128)(2,1)S(1)}, u32[]{:S(2)}, u32[]{:S(2)}) collective-permute-start(bf16[2,48,512]{2,1,0:T(8,128)(2,1)S(1)} %get-tuple-element.45), channel_id=1, source_target_pairs={{0,2},{1,3},{2,0},{3,1},{4,6},{5,7},{6,4},{7,5},{8,10},{9,11},{10,... | collective-permute-start | bytes 294920 | tf_op jit(solution)/shard_map/ppermute | solution.py:232
  66.3 2.2 %collective-permute-start.7 = (bf16[2,48,512]{2,1,0:T(8,128)(2,1)S(1)}, bf16[2,48,512]{2,1,0:T(8,128)(2,1)S(1)}, u32[]{:S(2)}, u32[]{:S(2)}) collective-permute-start(bf16[2,48,512]{2,1,0:T(8,128)(2,1)S(1)} %get-tuple-element.46), channel_id=1, source_target_pairs={{0,3},{1,2},{2,1},{3,0},{4,7},{5,6},{6,5},{7,4},{8,11},{9,10},{10,... | collective-permute-start | bytes 294920 | tf_op jit(solution)/shard_map/ppermute | solution.py:232
  68.5 0.1 collective-permute-done.4.got_ref
  68.6 0.1 shard_map.61.own_ref
  68.7 2.7 %collective-permute-start.5 = (bf16[2,48,384]{2,1,0:T(8,128)(2,1)S(1)}, bf16[2,48,384]{2,1,0:T(8,128)(2,1)S(1)}, u32[]{:S(2)}, u32[]{:S(2)}) collective-permute-start(bf16[2,48,384]{2,1,0:T(8,128)(2,1)S(1)} %shard_map.61.own_ref), channel_id=1, source_target_pairs={{0,1},{1,0},{2,3},{3,2},{4,5},{5,4},{6,7},{7,6},{8,9},{9,8},{10,11... | collective-permute-start | bytes 221192 | tf_op jit(solution)/shard_map/ppermute | solution.py:232
  71.4 0.0 collective-permute-done.6.w2_ref
  71.5 1.6 %collective-permute-done.7.w3_ref = bf16[2,48,512]{2,1,0:T(8,128)(2,1)S(1)} collective-permute-done((bf16[2,48,512]{2,1,0:T(8,128)(2,1)S(1)}, bf16[2,48,512]{2,1,0:T(8,128)(2,1)S(1)}, u32[]{:S(2)}, u32[]{:S(2)}) %collective-permute-start.7) | collective-permute-done | bytes 98336 | tf_op jit(solution)/shard_map/ppermute | solution.py:232
  73.1 0.0 collective-permute-done.5.got_ref
  73.1 0.7 shard_map.62
  73.8 38.8 %all_to_all.10 = bf16[256,6,128]{2,1,0:T(8,128)(2,1)S(1)} all-to-all(bf16[256,6,128]{2,1,0:T(8,128)(2,1)S(1)} %bitcast.6), channel_id=1, replica_groups={{0,4,8,12,16,20,24,28,32,36,40,44,48,52,56,60,64,68,72,76,80,84,88,92,9..., dimensions={0} | all-to-all | bytes 786432 | tf_op jit(solution)/shard_map/all_to_all | solution.py:236
  112.6 0.8 shard_map.63
  (1 shorter events, 0.0 us)
Async XLA Ops:
  0.0 32.2 %copy-start = (bf16[2,2,48,2048]{3,2,1,0:T(8,128)(2,1)S(1)}, bf16[2,2,48,2048]{3,2,1,0:T(8,128)(2,1)}, u32[]{:S(2)}) copy-start(bf16[2,2,48,2048]{3,2,1,0:T(8,128)(2,1)} %w_in_ref.1) | copy-start | bytes 2359300
  1.9 30.2 %copy-start.1 = (bf16[2,48,2048]{2,1,0:T(8,128)(2,1)S(1)}, bf16[2,48,2048]{2,1,0:T(8,128)(2,1)}, u32[]{:S(2)}) copy-start(bf16[2,48,2048]{2,1,0:T(8,128)(2,1)} %w_down_ref.1) | copy-start | bytes 1179652
  1.9 54.5 %all-to-all-start = ((bf16[256,6,128]{2,1,0:T(8,128)(2,1)}), bf16[256,6,128]{2,1,0:T(8,128)(2,1)S(1)}, u32[]{:S(2)}, u32[]{:S(2)}) async-start(bf16[256,6,128]{2,1,0:T(8,128)(2,1)} %bitcast.12), calls=%async_computation | async-start | bytes 1048576 | tf_op jit(solution)/shard_map/all_to_all | solution.py:236
  32.5 23.4 %collective-permute-start = (bf16[6,48,512]{2,1,0:T(8,128)(2,1)S(1)}, bf16[6,48,512]{2,1,0:T(8,128)(2,1)S(1)}, u32[]{:S(2)}, u32[]{:S(2)}) collective-permute-start(bf16[6,48,512]{2,1,0:T(8,128)(2,1)S(1)} %get-tuple-element.26), channel_id=1, source_target_pairs={{0,1},{1,0},{2,3},{3,2},{4,5},{5,4},{6,7},{7,6},{8,9},{9,8},{10,11... | collective-permute-start | bytes 884744 | tf_op jit(solution)/shard_map/ppermute | solution.py:232
  34.4 21.5 %copy-start.3 = (f32[16,8]{0,1:T(8,128)S(1)}, f32[16,8]{0,1:T(8,128)}, u32[]{:S(2)}) copy-start(f32[16,8]{0,1:T(8,128)} %param.7) | copy-start | bytes 1540
  34.4 21.5 %copy-start.2 = (s32[16,8]{0,1:T(8,128)S(1)}, s32[16,8]{0,1:T(8,128)}, u32[]{:S(2)}) copy-start(s32[16,8]{0,1:T(8,128)} %param.6) | copy-start | bytes 1540
  34.5 17.2 %collective-permute-start.1 = (bf16[4,48,512]{2,1,0:T(8,128)(2,1)S(1)}, bf16[4,48,512]{2,1,0:T(8,128)(2,1)S(1)}, u32[]{:S(2)}, u32[]{:S(2)}) collective-permute-start(bf16[4,48,512]{2,1,0:T(8,128)(2,1)S(1)} %get-tuple-element.33), channel_id=1, source_target_pairs={{0,2},{1,3},{2,0},{3,1},{4,6},{5,7},{6,4},{7,5},{8,10},{9,11},{10,... | collective-permute-start | bytes 589832 | tf_op jit(solution)/shard_map/ppermute | solution.py:232
  38.8 17.2 %collective-permute-start.2 = (bf16[4,48,512]{2,1,0:T(8,128)(2,1)S(1)}, bf16[4,48,512]{2,1,0:T(8,128)(2,1)S(1)}, u32[]{:S(2)}, u32[]{:S(2)}) collective-permute-start(bf16[4,48,512]{2,1,0:T(8,128)(2,1)S(1)} %get-tuple-element.34), channel_id=1, source_target_pairs={{0,3},{1,2},{2,1},{3,0},{4,7},{5,6},{6,5},{7,4},{8,11},{9,10},{10,... | collective-permute-start | bytes 589832 | tf_op jit(solution)/shard_map/ppermute | solution.py:232
  57.1 3.3 %collective-permute-start.3 = (bf16[2,96,384]{2,1,0:T(8,128)(2,1)S(1)}, bf16[2,96,384]{2,1,0:T(8,128)(2,1)S(1)}, u32[]{:S(2)}, u32[]{:S(2)}) collective-permute-start(bf16[2,96,384]{2,1,0:T(8,128)(2,1)S(1)} %get-tuple-element.41), channel_id=1, source_target_pairs={{0,1},{1,0},{2,3},{3,2},{4,5},{5,4},{6,7},{7,6},{8,9},{9,8},{10,11... | collective-permute-start | bytes 442376 | tf_op jit(solution)/shard_map/ppermute | solution.py:232
  60.5 8.2 %collective-permute-start.4 = (bf16[2,96,384]{2,1,0:T(8,128)(2,1)S(1)}, bf16[2,96,384]{2,1,0:T(8,128)(2,1)S(1)}, u32[]{:S(2)}, u32[]{:S(2)}) collective-permute-start(bf16[2,96,384]{2,1,0:T(8,128)(2,1)S(1)} %get-tuple-element.43), channel_id=1, source_target_pairs={{0,2},{1,3},{2,0},{3,1},{4,6},{5,7},{6,4},{7,5},{8,10},{9,11},{10,... | collective-permute-start | bytes 442376 | tf_op jit(solution)/shard_map/ppermute | solution.py:232
  63.5 8.0 %collective-permute-start.6 = (bf16[2,48,512]{2,1,0:T(8,128)(2,1)S(1)}, bf16[2,48,512]{2,1,0:T(8,128)(2,1)S(1)}, u32[]{:S(2)}, u32[]{:S(2)}) collective-permute-start(bf16[2,48,512]{2,1,0:T(8,128)(2,1)S(1)} %get-tuple-element.45), channel_id=1, source_target_pairs={{0,2},{1,3},{2,0},{3,1},{4,6},{5,7},{6,4},{7,5},{8,10},{9,11},{10,... | collective-permute-start | bytes 294920 | tf_op jit(solution)/shard_map/ppermute | solution.py:232
  66.3 6.8 %collective-permute-start.7 = (bf16[2,48,512]{2,1,0:T(8,128)(2,1)S(1)}, bf16[2,48,512]{2,1,0:T(8,128)(2,1)S(1)}, u32[]{:S(2)}, u32[]{:S(2)}) collective-permute-start(bf16[2,48,512]{2,1,0:T(8,128)(2,1)S(1)} %get-tuple-element.46), channel_id=1, source_target_pairs={{0,3},{1,2},{2,1},{3,0},{4,7},{5,6},{6,5},{7,4},{8,11},{9,10},{10,... | collective-permute-start | bytes 294920 | tf_op jit(solution)/shard_map/ppermute | solution.py:232
  68.7 4.4 %collective-permute-start.5 = (bf16[2,48,384]{2,1,0:T(8,128)(2,1)S(1)}, bf16[2,48,384]{2,1,0:T(8,128)(2,1)S(1)}, u32[]{:S(2)}, u32[]{:S(2)}) collective-permute-start(bf16[2,48,384]{2,1,0:T(8,128)(2,1)S(1)} %shard_map.61.own_ref), channel_id=1, source_target_pairs={{0,1},{1,0},{2,3},{3,2},{4,5},{5,4},{6,7},{7,6},{8,9},{9,8},{10,11... | collective-permute-start | bytes 221192 | tf_op jit(solution)/shard_map/ppermute | solution.py:232

commit v11 on v9

--- a/solution.py
+++ b/solution.py
@@ -1,3 +1,5 @@
+import functools
+
 import jax
 import jax.numpy as jnp
 from jax import lax
@@ -150,27 +152,34 @@
     own_ref[1] = preact(w2_ref.at[0], x)
 
 
-def add_kernel(own_ref, got_ref, sum_ref, send_ref):
+def add_kernel(own_ref, got_ref, sum_ref, send0_ref, send2_ref):
     total = own_ref[...] + got_ref[...].astype(jnp.float32)
     sum_ref[...] = total
-    send_ref[...] = total.astype(jnp.bfloat16)
-
-
-def act_kernel(own_ref, got_ref, out_ref):
-    hid = out_ref.shape[1]
-    for r in range(2):
-        pre = own_ref[r] + got_ref[1 - r].astype(jnp.float32)
-        gate, up = pre[:hid], pre[hid:]
-        out_ref[r] = (gate / (1.0 + jnp.exp(-gate)) * up).astype(jnp.bfloat16)
-
-
-def down_kernel(own_ref, got_ref, spread_ref, w0_ref, w1_ref, w2_ref, w3_ref, out_ref):
+    send0_ref[...] = total[0].astype(jnp.bfloat16)
+    send2_ref[...] = total[1].astype(jnp.bfloat16)
+
+
+def act_kernel(block, own_ref, got_ref, out_ref):
+    hid = out_ref.shape[0]
+    pre = own_ref[block] + got_ref[...].astype(jnp.float32)
+    gate, up = pre[:hid], pre[hid:]
+    out_ref[...] = (gate / (1.0 + jnp.exp(-gate)) * up).astype(jnp.bfloat16)
+
+
+def down_kernel(
+    h0_ref, h1_ref, h2_ref, h3_ref, spread_ref, w0_ref, w1_ref, w2_ref, w3_ref, out_ref
+):
     owners, groups = out_ref.shape[:2]
-    hid, rows = own_ref.shape[1:]
+    hid, rows = h0_ref.shape
     first = iota((hid, rows), 1) < rows // LOCAL
     values, weights = [], []
-    for r, w_ref in enumerate((w0_ref, w1_ref, w2_ref.at[0], w3_ref)):
-        hidden = (got_ref if r % 2 else own_ref)[r // 2].astype(jnp.float32)
+    for h_ref, w_ref in (
+        (h0_ref, w0_ref),
+        (h1_ref, w1_ref),
+        (h2_ref, w2_ref.at[0]),
+        (h3_ref, w3_ref),
+    ):
+        hidden = h_ref[...].astype(jnp.float32)
         values += [jnp.where(first, hidden, 0.0), jnp.where(first, 0.0, hidden)]
         weights.append(w_ref[2 * LOCAL :].reshape(LOCAL * hid, groups * LANES))
     values = jnp.concatenate(values, axis=0).astype(jnp.bfloat16)
@@ -273,9 +282,15 @@
     )
     got = exchange(send, 1)
     own = call(own_kernel, f32(*pair), (x, weights[0], weights[2]))
-    own, send = call(add_kernel, [f32(*pair), bf16(*pair)], (own, got))
-    hidden = call(act_kernel, bf16(2, hid, rows), (own, exchange(send, 2)))
-    out = call(down_kernel, bf16(*held), (hidden, exchange(hidden, 1), spread, *weights))
+    half = bf16(2 * hid, rows)
+    own, send0, send2 = call(add_kernel, [f32(*pair), half, half], (own, got))
+    got0, got2 = exchange(send2, 2), exchange(send0, 2)
+    hidden0 = call(functools.partial(act_kernel, 0), bf16(hid, rows), (own, got0))
+    hidden1 = exchange(hidden0, 1)
+    hidden2 = call(functools.partial(act_kernel, 1), bf16(hid, rows), (own, got2))
+    hidden3 = exchange(hidden2, 1)
+    hidden = (hidden0, hidden1, hidden2, hidden3)
+    out = call(down_kernel, bf16(*held), (*hidden, spread, *weights))
     return call(combine_kernel, bf16(toks, LANES), (picking, shares, deal(out)))
 
 

time: 107 us -> 108 us (level)
  starting transfers between devices: 44.9 us -> 50.7 us
  waiting for transfers between devices: 24.8 us -> 19.5 us
    ppermute x6 -> x8, starting transfers between devices: 15.7 us -> 21.5 us  [exchange(): return lax.ppermute(value, 'tensor', [(i, i ^ r) for i in range(n_tensor)])]
    ppermute x6 -> x8, waiting for transfers between devices: 7.77 us -> 2.44 us  [exchange(): return lax.ppermute(value, 'tensor', [(i, i ^ r) for i in range(n_tensor)])]
    pallas_call x8 -> x9, Pallas kernels: 3.43 us -> 3.45 us  [call(): pl.pallas_call(kernel, out_shape=shapes, in_specs=[VMEM] * len(args), out...]
  transfers between devices with their start and end apart: 7 -> 9, of which waited for: 4 -> 5; matrix products, arithmetic and copies ran while one was open for 0% -> 0% of each run, Pallas kernels for 1% -> 1%
where the time goes in v11:
time: 108 us
  starting transfers between devices  50.7 us (47%)
  blocking collectives  31.4 us (29%)
  waiting for transfers between devices  19.5 us (18%)
  Pallas kernels  5.81 us (5%)
    all_to_all x1, blocking collectives, deal(): lax.all_to_all(value, ('expert', 'tensor'), 0, 0, tiled=True, axis_index_...  31.4 us
    all_to_all x1, starting transfers between devices, deal(): lax.all_to_all(value, ('expert', 'tensor'), 0, 0, tiled=True, axis_index_...  29.2 us
    ppermute x8, starting transfers between devices, exchange(): return lax.ppermute(value, 'tensor', [(i, i ^ r) for i in range(n_tensor)])  21.5 us
    all_to_all x1, waiting for transfers between devices, deal(): lax.all_to_all(value, ('expert', 'tensor'), 0, 0, tiled=True, axis_index_...  17.1 us
    pallas_call x9, Pallas kernels, call(): pl.pallas_call(kernel, out_shape=shapes, in_specs=[VMEM] * len(args), out...  3.45 us
    ppermute x8, waiting for transfers between devices, exchange(): return lax.ppermute(value, 'tensor', [(i, i ^ r) for i in range(n_tensor)])  2.44 us
    pallas_call x1, Pallas kernels, start(): pl.pallas_call(start_kernel, out_shape=shapes, in_specs=[ANY] * len(args)...  2.36 us
  transfers between devices with their start and end apart: 9, of which 5 were waited for; matrix products, arithmetic and copies ran while one was open for 0% of the time, Pallas kernels for 1%

profile of v11, /device:TPU:4, one launch (start us, length us, event | category | flops | bytes accessed | tf_op | source)
XLA Modules:
  0.0 107.7 jit_solution(2836935788060117805)
XLA Ops:
  0.0 0.0 copy-start.1
  0.0 2.4 %shard_map.55 = (bf16[64,4,6,128]{3,2,1,0:T(8,128)(2,1)}, bf16[2,6,48,512]{3,2,1,0:T(8,128)(2,1)}) custom-call(s32[8,16]{1,0:T(8,128)} %bitcast.11, bf16[16,128]{1,0:T(8,128)(2,1)} %tok_hbm.1, bf16[2,2,48,2048]{3,2,1,0:T(8,128)(2,1)} %w_in_ref, bf16[2,48,2048]{2,1,0:T(8,128)(2,1)} %w_down_ref), custom_call_target="tpu_custom_call" | custom-call | tf_op jit(solution)/shard_map/pallas_call | solution.py:218
  2.4 0.0 copy-start
  2.4 5.3 %collective-permute-start = (bf16[2,6,48,512]{3,2,1,0:T(8,128)(2,1)}, bf16[2,6,48,512]{3,2,1,0:T(8,128)(2,1)S(1)}, u32[]{:S(2)}, u32[]{:S(2)}) collective-permute-start(bf16[2,6,48,512]{3,2,1,0:T(8,128)(2,1)} %get-tuple-element.23), channel_id=1, source_target_pairs={{0,2},{1,3},{2,0},{3,1},{4,6},{5,7},{6,4},{7,5},{8,10},{9,11},{10,... | collective-permute-start | bytes 1769480 | tf_op jit(solution)/shard_map/ppermute | solution.py:249
  7.7 29.2 %all-to-all-start = ((bf16[256,6,128]{2,1,0:T(8,128)(2,1)}), bf16[256,6,128]{2,1,0:T(8,128)(2,1)S(1)}, u32[]{:S(2)}, u32[]{:S(2)}) async-start(bf16[256,6,128]{2,1,0:T(8,128)(2,1)} %bitcast.14), calls=%async_computation | async-start | bytes 1048576 | tf_op jit(solution)/shard_map/all_to_all | solution.py:253
  36.9 0.0 collective-permute-done.w2_ref
  36.9 0.0 copy-done.1
  36.9 0.0 copy-done
  36.9 0.2 shard_map.56
  37.1 1.9 %collective-permute-start.1 = (bf16[6,48,512]{2,1,0:T(8,128)(2,1)S(1)}, bf16[6,48,512]{2,1,0:T(8,128)(2,1)S(1)}, u32[]{:S(2)}, u32[]{:S(2)}) collective-permute-start(bf16[6,48,512]{2,1,0:T(8,128)(2,1)S(1)} %get-tuple-element.26), channel_id=1, source_target_pairs={{0,1},{1,0},{2,3},{3,2},{4,5},{5,4},{6,7},{7,6},{8,9},{9,8},{10,11... | collective-permute-start | bytes 884744 | tf_op jit(solution)/shard_map/ppermute | solution.py:249
  39.0 0.0 copy-start.2
  39.0 0.0 copy-start.3
  39.1 2.4 %collective-permute-start.2 = (bf16[6,48,512]{2,1,0:T(8,128)(2,1)S(1)}, bf16[6,48,512]{2,1,0:T(8,128)(2,1)S(1)}, u32[]{:S(2)}, u32[]{:S(2)}) collective-permute-start(bf16[6,48,512]{2,1,0:T(8,128)(2,1)S(1)} %slice_bitcast_fusion), channel_id=1, source_target_pairs={{0,1},{1,0},{2,3},{3,2},{4,5},{5,4},{6,7},{7,6},{8,9},{9,8},{10,11... | collective-permute-start | bytes 884744 | tf_op jit(solution)/shard_map/ppermute | solution.py:249
  41.5 0.0 collective-permute-done.1.w1_ref
  41.5 0.0 copy-done.2
  41.5 0.0 copy-done.3
  41.5 0.4 shard_map.57
  42.0 17.1 %all-to-all-done = bf16[256,6,128]{2,1,0:T(8,128)(2,1)S(1)} async-done(((bf16[256,6,128]{2,1,0:T(8,128)(2,1)}), bf16[256,6,128]{2,1,0:T(8,128)(2,1)S(1)}, u32[]{:S(2)}, u32[]{:S(2)}) %all-to-all-start) | async-done | bytes 393248 | tf_op jit(solution)/shard_map/all_to_all | solution.py:253
  59.1 0.0 collective-permute-done.2.w3_ref
  59.1 0.7 shard_map.58
  59.8 1.9 %collective-permute-start.3 = (bf16[2,96,384]{2,1,0:T(8,128)(2,1)S(1)}, bf16[2,96,384]{2,1,0:T(8,128)(2,1)S(1)}, u32[]{:S(2)}, u32[]{:S(2)}) collective-permute-start(bf16[2,96,384]{2,1,0:T(8,128)(2,1)S(1)} %get-tuple-element.36), channel_id=1, source_target_pairs={{0,1},{1,0},{2,3},{3,2},{4,5},{5,4},{6,7},{7,6},{8,9},{9,8},{10,11... | collective-permute-start | bytes 442376 | tf_op jit(solution)/shard_map/ppermute | solution.py:249
  61.7 0.4 shard_map.59.own_ref
  62.1 0.9 collective-permute-done.3.got_ref
  63.1 2.2 %collective-permute-start.4 = (bf16[96,384]{1,0:T(8,128)(2,1)S(1)}, bf16[96,384]{1,0:T(8,128)(2,1)S(1)}, u32[]{:S(2)}, u32[]{:S(2)}) collective-permute-start(bf16[96,384]{1,0:T(8,128)(2,1)S(1)} %get-tuple-element.38), channel_id=1, source_target_pairs={{0,2},{1,3},{2,0},{3,1},{4,6},{5,7},{6,4},{7,5},{8,10},{9,11},{10,... | collective-permute-start | bytes 221192 | tf_op jit(solution)/shard_map/ppermute | solution.py:249
  65.3 3.7 %collective-permute-start.6 = (bf16[96,384]{1,0:T(8,128)(2,1)S(1)}, bf16[96,384]{1,0:T(8,128)(2,1)S(1)}, u32[]{:S(2)}, u32[]{:S(2)}) collective-permute-start(bf16[96,384]{1,0:T(8,128)(2,1)S(1)} %get-tuple-element.39), channel_id=1, source_target_pairs={{0,2},{1,3},{2,0},{3,1},{4,6},{5,7},{6,4},{7,5},{8,10},{9,11},{10,... | collective-permute-start | bytes 221192 | tf_op jit(solution)/shard_map/ppermute | solution.py:249
  69.0 0.4 collective-permute-done.4.got_ref
  69.4 1.9 %collective-permute-start.5 = (bf16[48,384]{1,0:T(8,128)(2,1)S(1)}, bf16[48,384]{1,0:T(8,128)(2,1)S(1)}, u32[]{:S(2)}, u32[]{:S(2)}) collective-permute-start(bf16[48,384]{1,0:T(8,128)(2,1)S(1)} %shard_map.61.h0_ref), channel_id=1, source_target_pairs={{0,1},{1,0},{2,3},{3,2},{4,5},{5,4},{6,7},{7,6},{8,9},{9,8},{10,11... | collective-permute-start | bytes 110600 | tf_op jit(solution)/shard_map/ppermute | solution.py:249
  71.3 0.2 collective-permute-done.6.got_ref
  71.6 2.2 %collective-permute-start.7 = (bf16[48,384]{1,0:T(8,128)(2,1)S(1)}, bf16[48,384]{1,0:T(8,128)(2,1)S(1)}, u32[]{:S(2)}, u32[]{:S(2)}) collective-permute-start(bf16[48,384]{1,0:T(8,128)(2,1)S(1)} %shard_map.62.h2_ref), channel_id=1, source_target_pairs={{0,1},{1,0},{2,3},{3,2},{4,5},{5,4},{6,7},{7,6},{8,9},{9,8},{10,11... | collective-permute-start | bytes 110600 | tf_op jit(solution)/shard_map/ppermute | solution.py:249
  73.8 0.0 collective-permute-done.5.h1_ref
  73.8 0.9 collective-permute-done.7.h3_ref
  74.7 0.7 shard_map.63
  75.5 31.4 %all_to_all.10 = bf16[256,6,128]{2,1,0:T(8,128)(2,1)S(1)} all-to-all(bf16[256,6,128]{2,1,0:T(8,128)(2,1)S(1)} %bitcast.9), channel_id=1, replica_groups={{0,4,8,12,16,20,24,28,32,36,40,44,48,52,56,60,64,68,72,76,80,84,88,92,9..., dimensions={0} | all-to-all | bytes 786432 | tf_op jit(solution)/shard_map/all_to_all | solution.py:253
  106.8 0.8 shard_map.64
  (4 shorter events, 0.1 us)
Async XLA Ops:
  0.0 36.9 %copy-start.1 = (bf16[2,48,2048]{2,1,0:T(8,128)(2,1)S(1)}, bf16[2,48,2048]{2,1,0:T(8,128)(2,1)}, u32[]{:S(2)}) copy-start(bf16[2,48,2048]{2,1,0:T(8,128)(2,1)} %w_down_ref) | copy-start | bytes 1179652
  2.4 34.6 %copy-start = (bf16[2,2,48,2048]{3,2,1,0:T(8,128)(2,1)S(1)}, bf16[2,2,48,2048]{3,2,1,0:T(8,128)(2,1)}, u32[]{:S(2)}) copy-start(bf16[2,2,48,2048]{3,2,1,0:T(8,128)(2,1)} %w_in_ref) | copy-start | bytes 2359300
  2.4 34.5 %collective-permute-start = (bf16[2,6,48,512]{3,2,1,0:T(8,128)(2,1)}, bf16[2,6,48,512]{3,2,1,0:T(8,128)(2,1)S(1)}, u32[]{:S(2)}, u32[]{:S(2)}) collective-permute-start(bf16[2,6,48,512]{3,2,1,0:T(8,128)(2,1)} %get-tuple-element.23), channel_id=1, source_target_pairs={{0,2},{1,3},{2,0},{3,1},{4,6},{5,7},{6,4},{7,5},{8,10},{9,11},{10,... | collective-permute-start | bytes 1769480 | tf_op jit(solution)/shard_map/ppermute | solution.py:249
  7.7 51.3 %all-to-all-start = ((bf16[256,6,128]{2,1,0:T(8,128)(2,1)}), bf16[256,6,128]{2,1,0:T(8,128)(2,1)S(1)}, u32[]{:S(2)}, u32[]{:S(2)}) async-start(bf16[256,6,128]{2,1,0:T(8,128)(2,1)} %bitcast.14), calls=%async_computation | async-start | bytes 1048576 | tf_op jit(solution)/shard_map/all_to_all | solution.py:253
  37.1 4.4 %collective-permute-start.1 = (bf16[6,48,512]{2,1,0:T(8,128)(2,1)S(1)}, bf16[6,48,512]{2,1,0:T(8,128)(2,1)S(1)}, u32[]{:S(2)}, u32[]{:S(2)}) collective-permute-start(bf16[6,48,512]{2,1,0:T(8,128)(2,1)S(1)} %get-tuple-element.26), channel_id=1, source_target_pairs={{0,1},{1,0},{2,3},{3,2},{4,5},{5,4},{6,7},{7,6},{8,9},{9,8},{10,11... | collective-permute-start | bytes 884744 | tf_op jit(solution)/shard_map/ppermute | solution.py:249
  39.0 2.5 %copy-start.2 = (s32[16,8]{0,1:T(8,128)S(1)}, s32[16,8]{0,1:T(8,128)}, u32[]{:S(2)}) copy-start(s32[16,8]{0,1:T(8,128)} %param.6) | copy-start | bytes 1540
  39.0 2.5 %copy-start.3 = (f32[16,8]{0,1:T(8,128)S(1)}, f32[16,8]{0,1:T(8,128)}, u32[]{:S(2)}) copy-start(f32[16,8]{0,1:T(8,128)} %param.7) | copy-start | bytes 1540
  39.1 20.0 %collective-permute-start.2 = (bf16[6,48,512]{2,1,0:T(8,128)(2,1)S(1)}, bf16[6,48,512]{2,1,0:T(8,128)(2,1)S(1)}, u32[]{:S(2)}, u32[]{:S(2)}) collective-permute-start(bf16[6,48,512]{2,1,0:T(8,128)(2,1)S(1)} %slice_bitcast_fusion), channel_id=1, source_target_pairs={{0,1},{1,0},{2,3},{3,2},{4,5},{5,4},{6,7},{7,6},{8,9},{9,8},{10,11... | collective-permute-start | bytes 884744 | tf_op jit(solution)/shard_map/ppermute | solution.py:249
  59.8 3.3 %collective-permute-start.3 = (bf16[2,96,384]{2,1,0:T(8,128)(2,1)S(1)}, bf16[2,96,384]{2,1,0:T(8,128)(2,1)S(1)}, u32[]{:S(2)}, u32[]{:S(2)}) collective-permute-start(bf16[2,96,384]{2,1,0:T(8,128)(2,1)S(1)} %get-tuple-element.36), channel_id=1, source_target_pairs={{0,1},{1,0},{2,3},{3,2},{4,5},{5,4},{6,7},{7,6},{8,9},{9,8},{10,11... | collective-permute-start | bytes 442376 | tf_op jit(solution)/shard_map/ppermute | solution.py:249
  63.1 6.2 %collective-permute-start.4 = (bf16[96,384]{1,0:T(8,128)(2,1)S(1)}, bf16[96,384]{1,0:T(8,128)(2,1)S(1)}, u32[]{:S(2)}, u32[]{:S(2)}) collective-permute-start(bf16[96,384]{1,0:T(8,128)(2,1)S(1)} %get-tuple-element.38), channel_id=1, source_target_pairs={{0,2},{1,3},{2,0},{3,1},{4,6},{5,7},{6,4},{7,5},{8,10},{9,11},{10,... | collective-permute-start | bytes 221192 | tf_op jit(solution)/shard_map/ppermute | solution.py:249
  65.3 6.2 %collective-permute-start.6 = (bf16[96,384]{1,0:T(8,128)(2,1)S(1)}, bf16[96,384]{1,0:T(8,128)(2,1)S(1)}, u32[]{:S(2)}, u32[]{:S(2)}) collective-permute-start(bf16[96,384]{1,0:T(8,128)(2,1)S(1)} %get-tuple-element.39), channel_id=1, source_target_pairs={{0,2},{1,3},{2,0},{3,1},{4,6},{5,7},{6,4},{7,5},{8,10},{9,11},{10,... | collective-permute-start | bytes 221192 | tf_op jit(solution)/shard_map/ppermute | solution.py:249
  69.4 4.4 %collective-permute-start.5 = (bf16[48,384]{1,0:T(8,128)(2,1)S(1)}, bf16[48,384]{1,0:T(8,128)(2,1)S(1)}, u32[]{:S(2)}, u32[]{:S(2)}) collective-permute-start(bf16[48,384]{1,0:T(8,128)(2,1)S(1)} %shard_map.61.h0_ref), channel_id=1, source_target_pairs={{0,1},{1,0},{2,3},{3,2},{4,5},{5,4},{6,7},{7,6},{8,9},{9,8},{10,11... | collective-permute-start | bytes 110600 | tf_op jit(solution)/shard_map/ppermute | solution.py:249
  71.6 3.1 %collective-permute-start.7 = (bf16[48,384]{1,0:T(8,128)(2,1)S(1)}, bf16[48,384]{1,0:T(8,128)(2,1)S(1)}, u32[]{:S(2)}, u32[]{:S(2)}) collective-permute-start(bf16[48,384]{1,0:T(8,128)(2,1)S(1)} %shard_map.62.h2_ref), channel_id=1, source_target_pairs={{0,1},{1,0},{2,3},{3,2},{4,5},{5,4},{6,7},{7,6},{8,9},{9,8},{10,11... | collective-permute-start | bytes 110600 | tf_op jit(solution)/shard_map/ppermute | solution.py:249

commit v12 on v9

--- a/solution.py
+++ b/solution.py
@@ -10,6 +10,7 @@
 QUAD = 4
 LOCAL = 2
 SLOTS = LOCAL * CAPACITY
+STRIDE = 5
 TILE = 8
 VMEM = pl.BlockSpec(memory_space=pltpu.VMEM)
 ANY = pl.BlockSpec(memory_space=pl.ANY)
@@ -27,7 +28,7 @@
     return jnp.sum(picked, axis=2, keepdims=True)
 
 
-def slot_rows(ids):
+def slot_rows(ids, owners):
     top, toks = ids.shape
     pairs = top * toks
     down = pair_column(ids.astype(jnp.float32)).reshape(pairs, 1)
@@ -39,7 +40,8 @@
 
     def row(number, slot):
         number, slot = number.astype(jnp.int32), slot.astype(jnp.int32)
-        return number // LOCAL * TILE + number % LOCAL * CAPACITY + slot
+        place = number // LOCAL * STRIDE % owners
+        return place * TILE + number % LOCAL * CAPACITY + slot
 
     return row(down, slot_down), row(across, slot_across)
 
@@ -86,7 +88,7 @@
 
     owners, groups = sent_ref.shape[:2]
     toks = tok_ref.shape[0]
-    _, across = slot_rows(ids_ref[...])
+    _, across = slot_rows(ids_ref[...], owners)
     pairs = across.shape[1]
     token_of = onehot(iota((pairs, toks), 0) // (pairs // toks) == iota((pairs, toks), 1))
     values = jnp.dot(token_of, tok_ref[...], preferred_element_type=jnp.float32)
@@ -112,7 +114,7 @@
     owners = held // TILE
     dense_ref[...] = onehot(iota((rows, held), 0) == dense_row((1, held), 1, owners))
     spread_ref[...] = onehot(iota((held, rows), 1) == dense_row((held, 1), 0, owners))
-    down, _ = slot_rows(ids_ref[...])
+    down, _ = slot_rows(ids_ref[...], owners)
     picking_ref[...] = onehot(down == iota(picking_ref.shape, 1))
     gates = gates_ref[...]
     shares = pair_column(gates / jnp.sum(gates, axis=0, keepdims=True))
@@ -224,8 +226,9 @@
     _, _, hid, _ = w_in.shape
     rows = n_expert * SLOTS
     ids, gates = expert_ids.T, gate_scores.T
+    order = sorted(range(n_expert), key=lambda e: e * STRIDE % n_expert)
     peers = [
-        [e * n_tensor + QUAD * m + q for e in range(n_expert) for m in range(groups)]
+        [e * n_tensor + QUAD * m + q for e in order for m in range(groups)]
         for q in range(QUAD)
     ]
     held = (n_expert, groups, SLOTS, LANES)

time: 107 us -> 108 us (level)
  the two profiles are of different devices: /device:TPU:4 before, /device:TPU:1 now
where the time goes in v12:
time: 108 us
  starting transfers between devices  51 us (47%)
  blocking collectives  29.8 us (28%)
  waiting for transfers between devices  20.8 us (19%)
  Pallas kernels  5.8 us (5%)
    all_to_all x1, starting transfers between devices, deal(): lax.all_to_all(value, ('expert', 'tensor'), 0, 0, tiled=True, axis_index_...  29.8 us
    all_to_all x1, blocking collectives, deal(): lax.all_to_all(value, ('expert', 'tensor'), 0, 0, tiled=True, axis_index_...  29.8 us
    ppermute x6, starting transfers between devices, exchange(): return lax.ppermute(value, 'tensor', [(i, i ^ r) for i in range(n_tensor)])  21.2 us
    all_to_all x1, waiting for transfers between devices, deal(): lax.all_to_all(value, ('expert', 'tensor'), 0, 0, tiled=True, axis_index_...  14.3 us
    ppermute x6, waiting for transfers between devices, exchange(): return lax.ppermute(value, 'tensor', [(i, i ^ r) for i in range(n_tensor)])  6.51 us
    pallas_call x8, Pallas kernels, call(): pl.pallas_call(kernel, out_shape=shapes, in_specs=[VMEM] * len(args), out...  3.45 us
    pallas_call x1, Pallas kernels, start(): pl.pallas_call(start_kernel, out_shape=shapes, in_specs=[ANY] * len(args)...  2.35 us
  transfers between devices with their start and end apart: 7, of which 4 were waited for; matrix products, arithmetic and copies ran while one was open for 0% of the time, Pallas kernels for 1%

profile of v12, /device:TPU:1, one launch (start us, length us, event | category | flops | bytes accessed | tf_op | source)
XLA Modules:
  0.0 107.7 jit_solution(3214911814525103958)
XLA Ops:
  0.0 0.0 copy-start.1
  0.0 2.3 %shard_map.55 = (bf16[64,4,6,128]{3,2,1,0:T(8,128)(2,1)}, bf16[2,6,48,512]{3,2,1,0:T(8,128)(2,1)}) custom-call(s32[8,16]{1,0:T(8,128)} %bitcast.11, bf16[16,128]{1,0:T(8,128)(2,1)} %tok_hbm.1, bf16[2,2,48,2048]{3,2,1,0:T(8,128)(2,1)} %w_in_ref, bf16[2,48,2048]{2,1,0:T(8,128)(2,1)} %w_down_ref), custom_call_target="tpu_custom_call" | custom-call | tf_op jit(solution)/shard_map/pallas_call | solution.py:211
  2.4 0.0 copy-start
  2.4 5.9 %collective-permute-start = (bf16[2,6,48,512]{3,2,1,0:T(8,128)(2,1)}, bf16[2,6,48,512]{3,2,1,0:T(8,128)(2,1)S(1)}, u32[]{:S(2)}, u32[]{:S(2)}) collective-permute-start(bf16[2,6,48,512]{3,2,1,0:T(8,128)(2,1)} %get-tuple-element.22), channel_id=1, source_target_pairs={{0,2},{1,3},{2,0},{3,1},{4,6},{5,7},{6,4},{7,5},{8,10},{9,11},{10,... | collective-permute-start | bytes 1769480 | tf_op jit(solution)/shard_map/ppermute | solution.py:243
  8.2 29.8 %all-to-all-start = ((bf16[256,6,128]{2,1,0:T(8,128)(2,1)}), bf16[256,6,128]{2,1,0:T(8,128)(2,1)S(1)}, u32[]{:S(2)}, u32[]{:S(2)}) async-start(bf16[256,6,128]{2,1,0:T(8,128)(2,1)} %bitcast.14), calls=%async_computation | async-start | bytes 1048576 | tf_op jit(solution)/shard_map/all_to_all | solution.py:247
  38.1 0.0 collective-permute-done.w2_ref
  38.1 0.0 copy-done.1
  38.1 0.0 copy-done
  38.1 0.2 shard_map.56
  38.3 3.1 %collective-permute-start.1 = (bf16[6,48,512]{2,1,0:T(8,128)(2,1)S(1)}, bf16[6,48,512]{2,1,0:T(8,128)(2,1)S(1)}, u32[]{:S(2)}, u32[]{:S(2)}) collective-permute-start(bf16[6,48,512]{2,1,0:T(8,128)(2,1)S(1)} %get-tuple-element.25), channel_id=1, source_target_pairs={{0,1},{1,0},{2,3},{3,2},{4,5},{5,4},{6,7},{7,6},{8,9},{9,8},{10,11... | collective-permute-start | bytes 884744 | tf_op jit(solution)/shard_map/ppermute | solution.py:243
  41.5 0.0 copy-start.2
  41.5 0.0 copy-start.3
  41.5 1.9 %collective-permute-start.2 = (bf16[6,48,512]{2,1,0:T(8,128)(2,1)S(1)}, bf16[6,48,512]{2,1,0:T(8,128)(2,1)S(1)}, u32[]{:S(2)}, u32[]{:S(2)}) collective-permute-start(bf16[6,48,512]{2,1,0:T(8,128)(2,1)S(1)} %slice_bitcast_fusion), channel_id=1, source_target_pairs={{0,1},{1,0},{2,3},{3,2},{4,5},{5,4},{6,7},{7,6},{8,9},{9,8},{10,11... | collective-permute-start | bytes 884744 | tf_op jit(solution)/shard_map/ppermute | solution.py:243
  43.4 0.0 collective-permute-done.1.w1_ref
  43.5 0.0 copy-done.2
  43.5 0.0 copy-done.3
  43.5 0.5 shard_map.57
  43.9 14.3 %all-to-all-done = bf16[256,6,128]{2,1,0:T(8,128)(2,1)S(1)} async-done(((bf16[256,6,128]{2,1,0:T(8,128)(2,1)}), bf16[256,6,128]{2,1,0:T(8,128)(2,1)S(1)}, u32[]{:S(2)}, u32[]{:S(2)}) %all-to-all-start) | async-done | bytes 393248 | tf_op jit(solution)/shard_map/all_to_all | solution.py:247
  58.2 0.0 collective-permute-done.2.w3_ref
  58.2 0.7 shard_map.58
  59.0 5.2 %collective-permute-start.3 = (bf16[2,96,384]{2,1,0:T(8,128)(2,1)S(1)}, bf16[2,96,384]{2,1,0:T(8,128)(2,1)S(1)}, u32[]{:S(2)}, u32[]{:S(2)}) collective-permute-start(bf16[2,96,384]{2,1,0:T(8,128)(2,1)S(1)} %get-tuple-element.35), channel_id=1, source_target_pairs={{0,1},{1,0},{2,3},{3,2},{4,5},{5,4},{6,7},{7,6},{8,9},{9,8},{10,11... | collective-permute-start | bytes 442376 | tf_op jit(solution)/shard_map/ppermute | solution.py:243
  64.2 0.4 shard_map.59.own_ref
  64.6 0.6 collective-permute-done.3.got_ref
  65.2 1.9 %collective-permute-start.4 = (bf16[2,96,384]{2,1,0:T(8,128)(2,1)S(1)}, bf16[2,96,384]{2,1,0:T(8,128)(2,1)S(1)}, u32[]{:S(2)}, u32[]{:S(2)}) collective-permute-start(bf16[2,96,384]{2,1,0:T(8,128)(2,1)S(1)} %get-tuple-element.37), channel_id=1, source_target_pairs={{0,2},{1,3},{2,0},{3,1},{4,6},{5,7},{6,4},{7,5},{8,10},{9,11},{10,... | collective-permute-start | bytes 442376 | tf_op jit(solution)/shard_map/ppermute | solution.py:243
  67.2 5.0 %collective-permute-done.4.got_ref = bf16[2,96,384]{2,1,0:T(8,128)(2,1)S(1)} collective-permute-done((bf16[2,96,384]{2,1,0:T(8,128)(2,1)S(1)}, bf16[2,96,384]{2,1,0:T(8,128)(2,1)S(1)}, u32[]{:S(2)}, u32[]{:S(2)}) %collective-permute-start.4) | collective-permute-done | bytes 147488 | tf_op jit(solution)/shard_map/ppermute | solution.py:243
  72.2 0.1 shard_map.61.own_ref
  72.3 3.1 %collective-permute-start.5 = (bf16[2,48,384]{2,1,0:T(8,128)(2,1)S(1)}, bf16[2,48,384]{2,1,0:T(8,128)(2,1)S(1)}, u32[]{:S(2)}, u32[]{:S(2)}) collective-permute-start(bf16[2,48,384]{2,1,0:T(8,128)(2,1)S(1)} %shard_map.61.own_ref), channel_id=1, source_target_pairs={{0,1},{1,0},{2,3},{3,2},{4,5},{5,4},{6,7},{7,6},{8,9},{9,8},{10,11... | collective-permute-start | bytes 221192 | tf_op jit(solution)/shard_map/ppermute | solution.py:243
  75.4 0.9 collective-permute-done.5.got_ref
  76.3 0.7 shard_map.62
  77.0 29.8 %all_to_all.10 = bf16[256,6,128]{2,1,0:T(8,128)(2,1)S(1)} all-to-all(bf16[256,6,128]{2,1,0:T(8,128)(2,1)S(1)} %bitcast.9), channel_id=1, replica_groups={{0,4,8,12,208,212,216,220,416,420,424,428,624,628,632,636,832,836,840,8..., dimensions={0} | all-to-all | bytes 786432 | tf_op jit(solution)/shard_map/all_to_all | solution.py:247
  106.8 0.8 shard_map.63
  (2 shorter events, 0.1 us)
Async XLA Ops:
  0.0 38.1 %copy-start.1 = (bf16[2,48,2048]{2,1,0:T(8,128)(2,1)S(1)}, bf16[2,48,2048]{2,1,0:T(8,128)(2,1)}, u32[]{:S(2)}) copy-start(bf16[2,48,2048]{2,1,0:T(8,128)(2,1)} %w_down_ref) | copy-start | bytes 1179652
  2.4 35.8 %copy-start = (bf16[2,2,48,2048]{3,2,1,0:T(8,128)(2,1)S(1)}, bf16[2,2,48,2048]{3,2,1,0:T(8,128)(2,1)}, u32[]{:S(2)}) copy-start(bf16[2,2,48,2048]{3,2,1,0:T(8,128)(2,1)} %w_in_ref) | copy-start | bytes 2359300
  2.4 35.7 %collective-permute-start = (bf16[2,6,48,512]{3,2,1,0:T(8,128)(2,1)}, bf16[2,6,48,512]{3,2,1,0:T(8,128)(2,1)S(1)}, u32[]{:S(2)}, u32[]{:S(2)}) collective-permute-start(bf16[2,6,48,512]{3,2,1,0:T(8,128)(2,1)} %get-tuple-element.22), channel_id=1, source_target_pairs={{0,2},{1,3},{2,0},{3,1},{4,6},{5,7},{6,4},{7,5},{8,10},{9,11},{10,... | collective-permute-start | bytes 1769480 | tf_op jit(solution)/shard_map/ppermute | solution.py:243
  8.2 50.0 %all-to-all-start = ((bf16[256,6,128]{2,1,0:T(8,128)(2,1)}), bf16[256,6,128]{2,1,0:T(8,128)(2,1)S(1)}, u32[]{:S(2)}, u32[]{:S(2)}) async-start(bf16[256,6,128]{2,1,0:T(8,128)(2,1)} %bitcast.14), calls=%async_computation | async-start | bytes 1048576 | tf_op jit(solution)/shard_map/all_to_all | solution.py:247
  38.3 5.1 %collective-permute-start.1 = (bf16[6,48,512]{2,1,0:T(8,128)(2,1)S(1)}, bf16[6,48,512]{2,1,0:T(8,128)(2,1)S(1)}, u32[]{:S(2)}, u32[]{:S(2)}) collective-permute-start(bf16[6,48,512]{2,1,0:T(8,128)(2,1)S(1)} %get-tuple-element.25), channel_id=1, source_target_pairs={{0,1},{1,0},{2,3},{3,2},{4,5},{5,4},{6,7},{7,6},{8,9},{9,8},{10,11... | collective-permute-start | bytes 884744 | tf_op jit(solution)/shard_map/ppermute | solution.py:243
  41.5 2.0 %copy-start.2 = (s32[16,8]{0,1:T(8,128)S(1)}, s32[16,8]{0,1:T(8,128)}, u32[]{:S(2)}) copy-start(s32[16,8]{0,1:T(8,128)} %param.6) | copy-start | bytes 1540
  41.5 2.0 %copy-start.3 = (f32[16,8]{0,1:T(8,128)S(1)}, f32[16,8]{0,1:T(8,128)}, u32[]{:S(2)}) copy-start(f32[16,8]{0,1:T(8,128)} %param.7) | copy-start | bytes 1540
  41.5 16.7 %collective-permute-start.2 = (bf16[6,48,512]{2,1,0:T(8,128)(2,1)S(1)}, bf16[6,48,512]{2,1,0:T(8,128)(2,1)S(1)}, u32[]{:S(2)}, u32[]{:S(2)}) collective-permute-start(bf16[6,48,512]{2,1,0:T(8,128)(2,1)S(1)} %slice_bitcast_fusion), channel_id=1, source_target_pairs={{0,1},{1,0},{2,3},{3,2},{4,5},{5,4},{6,7},{7,6},{8,9},{9,8},{10,11... | collective-permute-start | bytes 884744 | tf_op jit(solution)/shard_map/ppermute | solution.py:243
  59.0 6.2 %collective-permute-start.3 = (bf16[2,96,384]{2,1,0:T(8,128)(2,1)S(1)}, bf16[2,96,384]{2,1,0:T(8,128)(2,1)S(1)}, u32[]{:S(2)}, u32[]{:S(2)}) collective-permute-start(bf16[2,96,384]{2,1,0:T(8,128)(2,1)S(1)} %get-tuple-element.35), channel_id=1, source_target_pairs={{0,1},{1,0},{2,3},{3,2},{4,5},{5,4},{6,7},{7,6},{8,9},{9,8},{10,11... | collective-permute-start | bytes 442376 | tf_op jit(solution)/shard_map/ppermute | solution.py:243
  65.2 7.0 %collective-permute-start.4 = (bf16[2,96,384]{2,1,0:T(8,128)(2,1)S(1)}, bf16[2,96,384]{2,1,0:T(8,128)(2,1)S(1)}, u32[]{:S(2)}, u32[]{:S(2)}) collective-permute-start(bf16[2,96,384]{2,1,0:T(8,128)(2,1)S(1)} %get-tuple-element.37), channel_id=1, source_target_pairs={{0,2},{1,3},{2,0},{3,1},{4,6},{5,7},{6,4},{7,5},{8,10},{9,11},{10,... | collective-permute-start | bytes 442376 | tf_op jit(solution)/shard_map/ppermute | solution.py:243
  72.3 4.0 %collective-permute-start.5 = (bf16[2,48,384]{2,1,0:T(8,128)(2,1)S(1)}, bf16[2,48,384]{2,1,0:T(8,128)(2,1)S(1)}, u32[]{:S(2)}, u32[]{:S(2)}) collective-permute-start(bf16[2,48,384]{2,1,0:T(8,128)(2,1)S(1)} %shard_map.61.own_ref), channel_id=1, source_target_pairs={{0,1},{1,0},{2,3},{3,2},{4,5},{5,4},{6,7},{7,6},{8,9},{9,8},{10,11... | collective-permute-start | bytes 221192 | tf_op jit(solution)/shard_map/ppermute | solution.py:243

commit v13 on v9

--- a/solution.py
+++ b/solution.py
@@ -76,8 +76,8 @@
     ids_hbm, tok_hbm, w_in_hbm, w_down_hbm, sent_ref, chip_ref, ids_ref, tok_ref, w_in_ref, w_down_ref, sems
 ):
     moves = [(ids_hbm, ids_ref), (tok_hbm, tok_ref)]
-    moves += [(w_in_hbm.at[e], w_in_ref.at[e]) for e in range(LOCAL)]
-    moves += [(w_down_hbm, w_down_ref)]
+    moves += [(w_in_hbm.at[e, g], w_in_ref.at[e, g]) for e in range(LOCAL) for g in range(2)]
+    moves += [(w_down_hbm.at[e], w_down_ref.at[e]) for e in range(LOCAL)]
     copies = [pltpu.make_async_copy(a, b, sems.at[i]) for i, (a, b) in enumerate(moves)]
     for copy in copies:
         copy.start()
@@ -212,7 +212,7 @@
         in_specs=[ANY] * len(args),
         out_specs=[VMEM] * len(shapes),
         scratch_shapes=[pltpu.VMEM(a.shape, a.dtype) for a in args]
-        + [pltpu.SemaphoreType.DMA((3 + LOCAL,))],
+        + [pltpu.SemaphoreType.DMA((2 + 3 * LOCAL,))],
         compiler_params=pltpu.CompilerParams(vmem_limit_bytes=60 * MIB),
     )(*args)
 

time: 107 us -> 107 us (level)
  no operation moved by 1% of the time
where the time goes in v13:
time: 107 us
  starting transfers between devices  44.9 us (42%)
  blocking collectives  31.2 us (29%)
  waiting for transfers between devices  24.8 us (23%)
  Pallas kernels  5.91 us (6%)
    all_to_all x1, blocking collectives, deal(): lax.all_to_all(value, ('expert', 'tensor'), 0, 0, tiled=True, axis_index_...  31.2 us
    all_to_all x1, starting transfers between devices, deal(): lax.all_to_all(value, ('expert', 'tensor'), 0, 0, tiled=True, axis_index_...  29.2 us
    all_to_all x1, waiting for transfers between devices, deal(): lax.all_to_all(value, ('expert', 'tensor'), 0, 0, tiled=True, axis_index_...  17.1 us
    ppermute x6, starting transfers between devices, exchange(): return lax.ppermute(value, 'tensor', [(i, i ^ r) for i in range(n_tensor)])  15.7 us
    ppermute x6, waiting for transfers between devices, exchange(): return lax.ppermute(value, 'tensor', [(i, i ^ r) for i in range(n_tensor)])  7.76 us
    pallas_call x8, Pallas kernels, call(): pl.pallas_call(kernel, out_shape=shapes, in_specs=[VMEM] * len(args), out...  3.44 us
    pallas_call x1, Pallas kernels, start(): pl.pallas_call(start_kernel, out_shape=shapes, in_specs=[ANY] * len(args)...  2.47 us
  transfers between devices with their start and end apart: 7, of which 4 were waited for; matrix products, arithmetic and copies ran while one was open for 0% of the time, Pallas kernels for 1%

profile of v13, /device:TPU:4, one launch (start us, length us, event | category | flops | bytes accessed | tf_op | source)
XLA Modules:
  0.0 107.0 jit_solution(10198767178370800388)
XLA Ops:
  0.0 0.0 copy-start.1
  0.0 2.5 %shard_map.55 = (bf16[64,4,6,128]{3,2,1,0:T(8,128)(2,1)}, bf16[2,6,48,512]{3,2,1,0:T(8,128)(2,1)}) custom-call(s32[8,16]{1,0:T(8,128)} %bitcast.11, bf16[16,128]{1,0:T(8,128)(2,1)} %tok_hbm.1, bf16[2,2,48,2048]{3,2,1,0:T(8,128)(2,1)} %w_in_ref, bf16[2,48,2048]{2,1,0:T(8,128)(2,1)} %w_down_ref), custom_call_target="tpu_custom_call" | custom-call | tf_op jit(solution)/shard_map/pallas_call | solution.py:209
  2.5 0.0 copy-start
  2.5 5.3 %collective-permute-start = (bf16[2,6,48,512]{3,2,1,0:T(8,128)(2,1)}, bf16[2,6,48,512]{3,2,1,0:T(8,128)(2,1)S(1)}, u32[]{:S(2)}, u32[]{:S(2)}) collective-permute-start(bf16[2,6,48,512]{3,2,1,0:T(8,128)(2,1)} %get-tuple-element.22), channel_id=1, source_target_pairs={{0,2},{1,3},{2,0},{3,1},{4,6},{5,7},{6,4},{7,5},{8,10},{9,11},{10,... | collective-permute-start | bytes 1769480 | tf_op jit(solution)/shard_map/ppermute | solution.py:240
  7.8 29.2 %all-to-all-start = ((bf16[256,6,128]{2,1,0:T(8,128)(2,1)}), bf16[256,6,128]{2,1,0:T(8,128)(2,1)S(1)}, u32[]{:S(2)}, u32[]{:S(2)}) async-start(bf16[256,6,128]{2,1,0:T(8,128)(2,1)} %bitcast.14), calls=%async_computation | async-start | bytes 1048576 | tf_op jit(solution)/shard_map/all_to_all | solution.py:244
  37.0 0.0 collective-permute-done.w2_ref
  37.0 0.0 copy-done.1
  37.0 0.0 copy-done
  37.0 0.2 shard_map.56
  37.2 1.9 %collective-permute-start.1 = (bf16[6,48,512]{2,1,0:T(8,128)(2,1)S(1)}, bf16[6,48,512]{2,1,0:T(8,128)(2,1)S(1)}, u32[]{:S(2)}, u32[]{:S(2)}) collective-permute-start(bf16[6,48,512]{2,1,0:T(8,128)(2,1)S(1)} %get-tuple-element.25), channel_id=1, source_target_pairs={{0,1},{1,0},{2,3},{3,2},{4,5},{5,4},{6,7},{7,6},{8,9},{9,8},{10,11... | collective-permute-start | bytes 884744 | tf_op jit(solution)/shard_map/ppermute | solution.py:240
  39.1 0.0 copy-start.2
  39.2 0.0 copy-start.3
  39.2 2.4 %collective-permute-start.2 = (bf16[6,48,512]{2,1,0:T(8,128)(2,1)S(1)}, bf16[6,48,512]{2,1,0:T(8,128)(2,1)S(1)}, u32[]{:S(2)}, u32[]{:S(2)}) collective-permute-start(bf16[6,48,512]{2,1,0:T(8,128)(2,1)S(1)} %slice_bitcast_fusion), channel_id=1, source_target_pairs={{0,1},{1,0},{2,3},{3,2},{4,5},{5,4},{6,7},{7,6},{8,9},{9,8},{10,11... | collective-permute-start | bytes 884744 | tf_op jit(solution)/shard_map/ppermute | solution.py:240
  41.6 0.0 collective-permute-done.1.w1_ref
  41.6 0.0 copy-done.2
  41.6 0.0 copy-done.3
  41.6 0.4 shard_map.57
  42.1 17.1 %all-to-all-done = bf16[256,6,128]{2,1,0:T(8,128)(2,1)S(1)} async-done(((bf16[256,6,128]{2,1,0:T(8,128)(2,1)}), bf16[256,6,128]{2,1,0:T(8,128)(2,1)S(1)}, u32[]{:S(2)}, u32[]{:S(2)}) %all-to-all-start) | async-done | bytes 393248 | tf_op jit(solution)/shard_map/all_to_all | solution.py:244
  59.2 0.0 collective-permute-done.2.w3_ref
  59.2 0.7 shard_map.58
  59.9 1.9 %collective-permute-start.3 = (bf16[2,96,384]{2,1,0:T(8,128)(2,1)S(1)}, bf16[2,96,384]{2,1,0:T(8,128)(2,1)S(1)}, u32[]{:S(2)}, u32[]{:S(2)}) collective-permute-start(bf16[2,96,384]{2,1,0:T(8,128)(2,1)S(1)} %get-tuple-element.35), channel_id=1, source_target_pairs={{0,1},{1,0},{2,3},{3,2},{4,5},{5,4},{6,7},{7,6},{8,9},{9,8},{10,11... | collective-permute-start | bytes 442376 | tf_op jit(solution)/shard_map/ppermute | solution.py:240
  61.8 0.4 shard_map.59.own_ref
  62.3 0.9 collective-permute-done.3.got_ref
  63.2 2.2 %collective-permute-start.4 = (bf16[2,96,384]{2,1,0:T(8,128)(2,1)S(1)}, bf16[2,96,384]{2,1,0:T(8,128)(2,1)S(1)}, u32[]{:S(2)}, u32[]{:S(2)}) collective-permute-start(bf16[2,96,384]{2,1,0:T(8,128)(2,1)S(1)} %get-tuple-element.37), channel_id=1, source_target_pairs={{0,2},{1,3},{2,0},{3,1},{4,6},{5,7},{6,4},{7,5},{8,10},{9,11},{10,... | collective-permute-start | bytes 442376 | tf_op jit(solution)/shard_map/ppermute | solution.py:240
  65.4 5.6 %collective-permute-done.4.got_ref = bf16[2,96,384]{2,1,0:T(8,128)(2,1)S(1)} collective-permute-done((bf16[2,96,384]{2,1,0:T(8,128)(2,1)S(1)}, bf16[2,96,384]{2,1,0:T(8,128)(2,1)S(1)}, u32[]{:S(2)}, u32[]{:S(2)}) %collective-permute-start.4) | collective-permute-done | bytes 147488 | tf_op jit(solution)/shard_map/ppermute | solution.py:240
  71.0 0.1 shard_map.61.own_ref
  71.1 1.9 %collective-permute-start.5 = (bf16[2,48,384]{2,1,0:T(8,128)(2,1)S(1)}, bf16[2,48,384]{2,1,0:T(8,128)(2,1)S(1)}, u32[]{:S(2)}, u32[]{:S(2)}) collective-permute-start(bf16[2,48,384]{2,1,0:T(8,128)(2,1)S(1)} %shard_map.61.own_ref), channel_id=1, source_target_pairs={{0,1},{1,0},{2,3},{3,2},{4,5},{5,4},{6,7},{7,6},{8,9},{9,8},{10,11... | collective-permute-start | bytes 221192 | tf_op jit(solution)/shard_map/ppermute | solution.py:240
  73.0 1.2 %collective-permute-done.5.got_ref = bf16[2,48,384]{2,1,0:T(8,128)(2,1)S(1)} collective-permute-done((bf16[2,48,384]{2,1,0:T(8,128)(2,1)S(1)}, bf16[2,48,384]{2,1,0:T(8,128)(2,1)S(1)}, u32[]{:S(2)}, u32[]{:S(2)}) %collective-permute-start.5) | collective-permute-done | bytes 73760 | tf_op jit(solution)/shard_map/ppermute | solution.py:240
  74.3 0.7 shard_map.62
  75.0 31.2 %all_to_all.10 = bf16[256,6,128]{2,1,0:T(8,128)(2,1)S(1)} all-to-all(bf16[256,6,128]{2,1,0:T(8,128)(2,1)S(1)} %bitcast.9), channel_id=1, replica_groups={{0,4,8,12,16,20,24,28,32,36,40,44,48,52,56,60,64,68,72,76,80,84,88,92,9..., dimensions={0} | all-to-all | bytes 786432 | tf_op jit(solution)/shard_map/all_to_all | solution.py:244
  106.2 0.8 shard_map.63
  (2 shorter events, 0.1 us)
Async XLA Ops:
  0.0 37.0 %copy-start.1 = (bf16[2,48,2048]{2,1,0:T(8,128)(2,1)S(1)}, bf16[2,48,2048]{2,1,0:T(8,128)(2,1)}, u32[]{:S(2)}) copy-start(bf16[2,48,2048]{2,1,0:T(8,128)(2,1)} %w_down_ref) | copy-start | bytes 1179652
  2.5 34.6 %copy-start = (bf16[2,2,48,2048]{3,2,1,0:T(8,128)(2,1)S(1)}, bf16[2,2,48,2048]{3,2,1,0:T(8,128)(2,1)}, u32[]{:S(2)}) copy-start(bf16[2,2,48,2048]{3,2,1,0:T(8,128)(2,1)} %w_in_ref) | copy-start | bytes 2359300
  2.5 34.5 %collective-permute-start = (bf16[2,6,48,512]{3,2,1,0:T(8,128)(2,1)}, bf16[2,6,48,512]{3,2,1,0:T(8,128)(2,1)S(1)}, u32[]{:S(2)}, u32[]{:S(2)}) collective-permute-start(bf16[2,6,48,512]{3,2,1,0:T(8,128)(2,1)} %get-tuple-element.22), channel_id=1, source_target_pairs={{0,2},{1,3},{2,0},{3,1},{4,6},{5,7},{6,4},{7,5},{8,10},{9,11},{10,... | collective-permute-start | bytes 1769480 | tf_op jit(solution)/shard_map/ppermute | solution.py:240
  7.8 51.3 %all-to-all-start = ((bf16[256,6,128]{2,1,0:T(8,128)(2,1)}), bf16[256,6,128]{2,1,0:T(8,128)(2,1)S(1)}, u32[]{:S(2)}, u32[]{:S(2)}) async-start(bf16[256,6,128]{2,1,0:T(8,128)(2,1)} %bitcast.14), calls=%async_computation | async-start | bytes 1048576 | tf_op jit(solution)/shard_map/all_to_all | solution.py:244
  37.2 4.4 %collective-permute-start.1 = (bf16[6,48,512]{2,1,0:T(8,128)(2,1)S(1)}, bf16[6,48,512]{2,1,0:T(8,128)(2,1)S(1)}, u32[]{:S(2)}, u32[]{:S(2)}) collective-permute-start(bf16[6,48,512]{2,1,0:T(8,128)(2,1)S(1)} %get-tuple-element.25), channel_id=1, source_target_pairs={{0,1},{1,0},{2,3},{3,2},{4,5},{5,4},{6,7},{7,6},{8,9},{9,8},{10,11... | collective-permute-start | bytes 884744 | tf_op jit(solution)/shard_map/ppermute | solution.py:240
  39.1 2.5 %copy-start.2 = (s32[16,8]{0,1:T(8,128)S(1)}, s32[16,8]{0,1:T(8,128)}, u32[]{:S(2)}) copy-start(s32[16,8]{0,1:T(8,128)} %param.6) | copy-start | bytes 1540
  39.2 2.5 %copy-start.3 = (f32[16,8]{0,1:T(8,128)S(1)}, f32[16,8]{0,1:T(8,128)}, u32[]{:S(2)}) copy-start(f32[16,8]{0,1:T(8,128)} %param.7) | copy-start | bytes 1540
  39.2 20.0 %collective-permute-start.2 = (bf16[6,48,512]{2,1,0:T(8,128)(2,1)S(1)}, bf16[6,48,512]{2,1,0:T(8,128)(2,1)S(1)}, u32[]{:S(2)}, u32[]{:S(2)}) collective-permute-start(bf16[6,48,512]{2,1,0:T(8,128)(2,1)S(1)} %slice_bitcast_fusion), channel_id=1, source_target_pairs={{0,1},{1,0},{2,3},{3,2},{4,5},{5,4},{6,7},{7,6},{8,9},{9,8},{10,11... | collective-permute-start | bytes 884744 | tf_op jit(solution)/shard_map/ppermute | solution.py:240
  59.9 3.3 %collective-permute-start.3 = (bf16[2,96,384]{2,1,0:T(8,128)(2,1)S(1)}, bf16[2,96,384]{2,1,0:T(8,128)(2,1)S(1)}, u32[]{:S(2)}, u32[]{:S(2)}) collective-permute-start(bf16[2,96,384]{2,1,0:T(8,128)(2,1)S(1)} %get-tuple-element.35), channel_id=1, source_target_pairs={{0,1},{1,0},{2,3},{3,2},{4,5},{5,4},{6,7},{7,6},{8,9},{9,8},{10,11... | collective-permute-start | bytes 442376 | tf_op jit(solution)/shard_map/ppermute | solution.py:240
  63.2 7.8 %collective-permute-start.4 = (bf16[2,96,384]{2,1,0:T(8,128)(2,1)S(1)}, bf16[2,96,384]{2,1,0:T(8,128)(2,1)S(1)}, u32[]{:S(2)}, u32[]{:S(2)}) collective-permute-start(bf16[2,96,384]{2,1,0:T(8,128)(2,1)S(1)} %get-tuple-element.37), channel_id=1, source_target_pairs={{0,2},{1,3},{2,0},{3,1},{4,6},{5,7},{6,4},{7,5},{8,10},{9,11},{10,... | collective-permute-start | bytes 442376 | tf_op jit(solution)/shard_map/ppermute | solution.py:240
  71.1 3.2 %collective-permute-start.5 = (bf16[2,48,384]{2,1,0:T(8,128)(2,1)S(1)}, bf16[2,48,384]{2,1,0:T(8,128)(2,1)S(1)}, u32[]{:S(2)}, u32[]{:S(2)}) collective-permute-start(bf16[2,48,384]{2,1,0:T(8,128)(2,1)S(1)} %shard_map.61.own_ref), channel_id=1, source_target_pairs={{0,1},{1,0},{2,3},{3,2},{4,5},{5,4},{6,7},{7,6},{8,9},{9,8},{10,11... | collective-permute-start | bytes 221192 | tf_op jit(solution)/shard_map/ppermute | solution.py:240
